TPU v7x, 32 devices: a whole 2x2x4 slice. The times are simulated.
32 devices in a mesh: row: 4 (over z), col: 8 (over y, x, core).
Axes of the slice: x: 2, y: 2, z: 4, core: 2. Of those that a mesh axis runs over, the one named last changes fastest.
Arguments:
- tokens: bfloat16 [512, 8192], P('row'), may hold values from -6 to 6
- gate_weight: bfloat16 [8192, 16384], P('row', 'col'), may hold values from -0.09375 to 0.09375
- up_weight: bfloat16 [8192, 16384], P('row', 'col'), may hold values from -0.09375 to 0.09375
- down_weight: bfloat16 [16384, 8192], P('col', 'row'), may hold values from -0.0625 to 0.0625
- gate_mask: int32 [64, 128], P('row', 'col'), may hold values from 0 to 1, as said below
- up_mask: int32 [64, 128], P('row', 'col'), may hold values from 0 to 1, as said below
- down_mask: int32 [128, 64], P('col', 'row'), may hold values 0 or 1
Outputs:
- mixed: bfloat16 [512, 8192], P('col', 'row')
Inputs may be any that keep to these rules, and one draw needn't show every extreme that they name: `gate_mask`: each device's block of 16 x 16 tiles keeps between 64 and 192 tiles; in each column of devices some block keeps exactly 192. `up_mask`: as for gate_mask, drawn independently.
All inputs are finite; a program needn't handle non-finite values. No bound on the sum of `down_mask` on one device may be relied on, other than what follows from the above.
Results may differ from a plain program's by a relative error of at most 0.02.
Values may be sent and summed in bfloat16 or wider, within the bound.
No kernel may reach another device: no remote copies, remote signals or barrier semaphores. Data moves between devices by JAX's collectives and lax.ppermute only.
A program may use at most 192 MiB of HBM per device.

v0:
```python
import jax
import jax.numpy as jnp
from jax import lax
from jax.sharding import PartitionSpec as P


def expand(weight, mask):
    rows, cols = weight.shape
    tile_rows, tile_cols = mask.shape
    tile = rows // tile_rows
    shaped = weight.reshape(tile_rows, tile, tile_cols, tile)
    return (shaped * mask.astype(weight.dtype)[:, None, :, None]).reshape(rows, cols)


def pack_tiles(weight, mask):
    rows, cols = weight.shape
    tile_rows, tile_cols = mask.shape
    tile = rows // tile_rows
    count = tile_rows * tile_cols
    slots = 3 * count // 4
    tiles = (
        weight.reshape(tile_rows, tile, tile_cols, tile)
        .transpose(0, 2, 1, 3)
        .reshape(count, tile * tile)
    )
    flags = mask.reshape(count)
    place = jnp.cumsum(flags) - 1
    chosen = (place[None, :] == jnp.arange(slots, dtype=jnp.int32)[:, None]) & (flags[None, :] == 1)
    packed = jnp.dot(chosen.astype(jnp.bfloat16), tiles, preferred_element_type=jnp.float32)
    packed = packed.astype(jnp.bfloat16).reshape(slots, tile, tile)
    where_from = jnp.sum(jnp.where(chosen, jnp.arange(count, dtype=jnp.int32)[None, :], 0), axis=1)
    return (packed, where_from)


def unpack_tiles(packed, where_from, groups, tile_rows, tile_cols):
    slots, tile = (packed.shape[0] // groups, packed.shape[1])
    count = tile_rows * tile_cols
    packed = packed.reshape(groups, slots, tile, tile)
    where_from = where_from.reshape(groups, slots)
    spread = (where_from[:, None, :] == jnp.arange(count, dtype=jnp.int32)[None, :, None]).astype(
        jnp.bfloat16
    )
    dense = jnp.einsum("gcs,gsab->gcab", spread, packed, preferred_element_type=jnp.float32).astype(
        jnp.bfloat16
    )
    dense = dense.reshape(groups, tile_rows, tile_cols, tile, tile).transpose(0, 1, 3, 2, 4)
    return dense.reshape(groups, tile_rows * tile, tile_cols * tile)


def on_device(tokens, gate_weight, up_weight, down_weight, gate_mask, up_mask, down_mask):
    tok_rows = tokens.shape[0]
    panel_rows, panel_cols = gate_weight.shape
    tile_rows, tile_cols = gate_mask.shape
    slots = 3 * tile_rows * tile_cols // 4
    gate_packed, gate_from = pack_tiles(gate_weight, gate_mask)
    up_packed, up_from = pack_tiles(up_weight, up_mask)
    gate_piece = lax.all_gather(gate_packed, "row", axis=0, tiled=True)
    up_piece = lax.all_gather(up_packed, "row", axis=0, tiled=True)
    gate_where = lax.all_gather(gate_from, "row", axis=0, tiled=True)
    up_where = lax.all_gather(up_from, "row", axis=0, tiled=True)
    groups = gate_piece.shape[0] // slots
    columns = tokens
    columns = columns.reshape(tok_rows, groups, panel_rows)

    def partial_value(piece, where_from):
        dense = unpack_tiles(piece, where_from, groups, tile_rows, tile_cols)
        product = jnp.einsum("tgr,grc->gtc", columns, dense, preferred_element_type=jnp.float32)
        rounded = lax.optimization_barrier(product.astype(jnp.bfloat16)).astype(jnp.float32)
        return jnp.sum(rounded, axis=0)

    gate = partial_value(gate_piece, gate_where)
    up = partial_value(up_piece, up_where)
    hidden = (jax.nn.silu(gate) * up).astype(jnp.bfloat16)
    all_hidden = lax.all_gather(hidden, "row", axis=0, tiled=True)
    down_eff = expand(down_weight, down_mask)
    return lax.psum_scatter(
        jnp.dot(all_hidden, down_eff, preferred_element_type=jnp.float32).astype(jnp.bfloat16),
        "col",
        scatter_dimension=0,
        tiled=True,
    )


def solution(mesh):
    return jax.shard_map(
        on_device,
        mesh=mesh,
        in_specs=(
            P("row", None),
            P("row", "col"),
            P("row", "col"),
            P("col", "row"),
            P("row", "col"),
            P("row", "col"),
            P("col", "row"),
        ),
        out_specs=P("col", "row"),
        check_vma=False,
    )
```

profile of v0, /device:TPU:0, one launch (start us, length us, event | category | flops | bytes accessed | tf_op | source)
XLA Modules:
  0.0 1118.4 jit_solution(7846189693477754126)
XLA Ops:
  6.5 0.0 all-gather.4.cloned.1.call-start
  6.5 0.8 reshape.119
  7.3 0.7 broadcast_compare_fusion.1
  8.0 0.3 reduce-window.16
  8.3 0.1 slice.14
  8.4 0.1 slice_reduce_fusion.1
  8.6 0.1 add_bitcast_fusion.1
  8.6 0.1 eq.82
  8.7 9.8 copy.39
  18.5 9.1 copy.26
  27.6 9.1 fusion.11
  36.7 0.0 copy-start.2
  36.7 4.6 copy.41
  41.3 0.0 all-gather.4.cloned.1.call-update
  41.4 0.5 all-gather.6.cloned.1.call-start
  41.9 0.0 copy-done.2
  41.9 0.1 reshape.128
  42.0 0.3 reduce-window.24
  42.3 0.1 slice.16
  42.4 0.1 eq.91
  42.4 10.9 copy.42
  53.4 11.7 %copy.30 = bf16[16,128,16,128]{3,1,2,0:T(8,128)(2,1)} copy(bf16[16,128,16,128]{3,2,1,0:T(8,128)(2,1)} %bitcast.86) | data formatting | bytes 16777216 | tf_op jit(solution)/shard_map/reshape | solution.py:22
  65.1 0.1 slice_reduce_fusion
  65.2 0.1 add_bitcast_fusion
  65.3 9.9 fusion.14
  75.2 0.0 copy-start.5
  75.2 4.7 copy.44
  79.8 0.0 all-gather.6.cloned.1.call-update
  79.9 0.0 all-gather.8.cloned.1.call-start
  79.9 0.0 copy-done.5
  79.9 0.6 dynamic-slice
  81.2 0.1 select_reduce_fusion.1
  81.3 0.2 dynamic-update-slice
  81.6 0.1 select_reduce_fusion
  81.7 0.2 dynamic-update-slice.1
  81.9 18.1 %all-reduce.2 = (s32[768]{0:T(1024)S(1)}, s32[768]{0:T(1024)S(1)}) all-reduce(s32[768]{0:T(1024)S(1)} %dynamic-update-slice.1, s32[768]{0:T(1024)S(1)} %dynamic-update-slice), channel_id=1, replica_groups=mesh['row'=4,'col'=8] {'row'}, use_global_device_ids=true, to_apply=%add.1 | all-reduce | flops 1536 | bytes 12288
  100.0 0.1 eq.83
  100.1 0.1 eq.92
  100.2 369.6 %all-gather.4.cloned.1.call-done = bf16[768,128,128]{2,1,0:T(8,128)(2,1)} async-done(((bf16[192,128,128]{2,1,0:T(8,128)(2,1)}), bf16[768,128,128]{2,1,0:T(8,128)(2,1)}) %all-gather.4.cloned.1.call-update) | async-done | bytes 25165840 | tf_op jit(solution)/shard_map/all_gather | solution.py:57
  469.7 31.1 %convolution_convert_fusion.1 = bf16[4,256,128,128]{3,1,2,0:T(8,128)(2,1)} fusion(bf16[4,192,128,128]{3,2,1,0:T(8,128)(2,1)} %bitcast.81, s32[4,192]{1,0:T(4,128)S(1)} %eq.83), kind=kOutput, calls=%fused_computation.2 | convolution fusion | flops 6459424768 | bytes 58723328 | tf_op jit(solution)/shard_map/gcs,gsab->gcab/dot_general | solution.py:43
  500.9 98.3 %copy.28 = bf16[4,16,128,16,128]{2,1,4,3,0:T(8,128)(2,1)} copy(bf16[4,16,128,16,128]{4,3,1,2,0:T(8,128)(2,1)} %bitcast.78) | data formatting | bytes 67108864 | tf_op jit(solution)/shard_map/transpose | solution.py:46
  599.1 49.6 %reshape.126 = bf16[4,2048,2048]{1,2,0:T(8,128)(2,1)} reshape(bf16[4,16,128,16,128]{2,1,4,3,0:T(8,128)(2,1)} %copy.28) | data formatting | bytes 67108864 | tf_op jit(solution)/shard_map/reshape | solution.py:47
  648.7 0.0 copy-done
  648.7 16.8 %fusion.9 = bf16[4,128,2048]{1,2,0:T(8,128)(2,1)} fusion(bf16[4,2048,2048]{1,2,0:T(8,128)(2,1)} %reshape.126, bf16[16,4,8,2048]{3,2,1,0:T(8,128)(2,1)S(1)} %bitcast.92), kind=kOutput, calls=%fused_computation.19 | convolution fusion | flops 4296015872 | bytes 37748736 | tf_op jit(solution)/shard_map/tgr,grc->gtc/dot_general | solution.py:67
  665.5 229.2 %all-gather.6.cloned.1.call-done = bf16[768,128,128]{2,1,0:T(8,128)(2,1)} async-done(((bf16[192,128,128]{2,1,0:T(8,128)(2,1)}), bf16[768,128,128]{2,1,0:T(8,128)(2,1)}) %all-gather.6.cloned.1.call-update) | async-done | bytes 25165840 | tf_op jit(solution)/shard_map/all_gather | solution.py:58
  894.7 30.5 %convolution_convert_fusion = bf16[4,256,128,128]{3,1,2,0:T(8,128)(2,1)} fusion(bf16[4,192,128,128]{3,2,1,0:T(8,128)(2,1)} %bitcast.82, s32[4,192]{1,0:T(4,128)S(1)} %eq.92), kind=kOutput, calls=%fused_computation.1 | convolution fusion | flops 6459424768 | bytes 58723328 | tf_op jit(solution)/shard_map/gcs,gsab->gcab/dot_general | solution.py:43
  925.3 23.1 %copy.77 = bf16[4,16,16,128,128]{4,2,3,1,0:T(8,128)(2,1)} copy(bf16[4,16,16,128,128]{4,2,1,3,0:T(8,128)(2,1)} %bitcast.79) | data formatting | bytes 67108864 | tf_op jit(solution)/shard_map/reshape | solution.py:46
  948.4 49.3 %reshape.135 = bf16[4,2048,2048]{2,1,0:T(8,128)(2,1)} reshape(bf16[4,16,128,16,128]{4,3,2,1,0:T(8,128)(2,1)} %bitcast.80) | data formatting | bytes 67108864 | tf_op jit(solution)/shard_map/reshape | solution.py:47
  997.6 0.0 copy-start.1
  997.6 16.6 %fusion.10 = bf16[4,128,2048]{1,2,0:T(8,128)(2,1)S(1)} fusion(bf16[4,2048,2048]{2,1,0:T(8,128)(2,1)} %reshape.135, bf16[16,4,8,2048]{3,2,1,0:T(8,128)(2,1)S(1)} %bitcast.93), kind=kOutput, calls=%fused_computation.20 | convolution fusion | flops 4296015872 | bytes 37748736 | tf_op jit(solution)/shard_map/tgr,grc->gtc/dot_general | solution.py:67
  1014.2 0.0 copy-done.1
  1014.2 0.0 copy-start.3
  1014.2 0.7 convert_reduce_fusion
  1014.9 1.1 multiply_convert_fusion
  1016.0 0.0 all-gather.8.cloned.1.call-update
  1016.0 0.0 reduce-scatter.2.cloned.1.call-start
  1016.1 0.0 copy-done.3
  1016.1 44.5 %all-gather.8.cloned.1.call-done = bf16[512,2048]{0,1:T(8,128)(2,1)} async-done(((bf16[128,2048]{0,1:T(8,128)(2,1)}), bf16[512,2048]{0,1:T(8,128)(2,1)}) %all-gather.8.cloned.1.call-update) | async-done | bytes 2097168 | tf_op jit(solution)/shard_map/all_gather | solution.py:74
  1060.6 0.0 copy-start.4
  1060.6 1.1 mul.20
  1061.8 0.4 copy-done.4
  1062.2 9.6 fusion.8
  1071.8 0.0 reduce-scatter.2.cloned.1.call-update
  1071.8 39.6 %reduce-scatter.2.cloned.1.call-done = bf16[64,2048]{1,0:T(8,128)(2,1)} async-done(((bf16[512,2048]{1,0:T(8,128)(2,1)}), bf16[64,2048]{1,0:T(8,128)(2,1)}) %reduce-scatter.2.cloned.1.call-update) | async-done | bytes 262160 | tf_op jit(solution)/shard_map/reduce_scatter | solution.py:76
  (7 shorter events, 0.1 us)
Async XLA Ops:
  6.5 463.2 %all-gather.4.cloned.1.call-start = ((), (), s32[]{:S(2)}) async-start(), calls=%async_computation.1 | async-start | bytes 31457280 | tf_op jit(solution)/shard_map/all_gather | solution.py:57
  36.7 5.2 copy-start.2
  41.4 853.4 %all-gather.6.cloned.1.call-start = ((), (), s32[]{:S(2)}) async-start(), calls=%async_computation.2 | async-start | bytes 31457280 | tf_op jit(solution)/shard_map/all_gather | solution.py:58
  75.2 4.8 copy-start.5
  79.9 980.8 %all-gather.8.cloned.1.call-start = ((), (), s32[]{:S(2)}) async-start(), calls=%async_computation.3 | async-start | bytes 2621440 | tf_op jit(solution)/shard_map/all_gather | solution.py:74
  599.1 49.6 %copy-start = (bf16[128,8192]{1,0:T(8,128)(2,1)S(1)}, bf16[128,8192]{1,0:T(8,128)(2,1)}, u32[]{:S(2)}) copy-start(bf16[128,8192]{1,0:T(8,128)(2,1)} %param.7) | copy-start | bytes 6291460
  997.6 16.6 %copy-start.1 = (bf16[4,128,2048]{1,2,0:T(8,128)(2,1)S(1)}, bf16[4,128,2048]{1,2,0:T(8,128)(2,1)}, u32[]{:S(2)}) copy-start(bf16[4,128,2048]{1,2,0:T(8,128)(2,1)} %fusion.9) | copy-start | bytes 6291460
  1014.2 1.9 copy-start.3
  1016.0 95.4 %reduce-scatter.2.cloned.1.call-start = ((), (), s32[]{:S(2)}) async-start(), calls=%async_computation.4 | async-start | bytes 2359296 | tf_op jit(solution)/shard_map/reduce_scatter | solution.py:76
  1060.6 1.6 copy-start.4
Sparse Core Ops, SparseCore 0:
  41.5 428.2 all-gather.3
  471.3 423.3 all-gather.5
  1016.2 44.4 all-gather.7
  1071.9 39.4 reduce-scatter.1
where the time goes:
time: 1130 us; the launch traced here: 1120 us
  waiting for transfers between devices  683 us (60%)
  local copies, waits for them, and re-layouts  275 us (24%)
  matrix products  124 us (11%)
  blocking collectives  18.1 us (2%)
  between operations  14.4 us (1%)
    all_gather x1, waiting for transfers between devices, on_device(): gate_piece = lax.all_gather(gate_packed, 'row', axis=0, tiled=True)  370 us
    all_gather x1, waiting for transfers between devices, on_device(): up_piece = lax.all_gather(up_packed, 'row', axis=0, tiled=True)  229 us
    reshape x2, local copies, waits for them, and re-layouts, unpack_tiles(): return dense.reshape(groups, tile_rows * tile, tile_cols * tile)  98.9 us
    transpose x1, local copies, waits for them, and re-layouts, unpack_tiles(): dense.reshape(groups, tile_rows, tile_cols, tile, tile)  98.3 us
    dot_general x2, matrix products, unpack_tiles(): jnp.einsum('gcs,gsab->gcab', spread, packed, preferred_element_type=jnp.f...  61.7 us
    all_gather x1, waiting for transfers between devices, on_device(): all_hidden = lax.all_gather(hidden, 'row', axis=0, tiled=True)  44.5 us
    reduce_scatter x1, waiting for transfers between devices, on_device(): lax.psum_scatter(jnp.dot(all_hidden, down_eff, preferred_element_type=jnp...  39.6 us
    dot_general x2, matrix products, partial_value(): jnp.einsum('tgr,grc->gtc', columns, dense, preferred_element_type=jnp.flo...  33.3 us
  transfers between devices with their start and end apart: 4, of which 4 were waited for; matrix products, arithmetic and copies ran while one was open for 21% of the time, Pallas kernels for 0%

commit v1 on v0

v1 whole, which is shorter than its diff:
```python
import functools

import jax
import jax.numpy as jnp
from jax import lax
from jax.experimental import pallas as pl
from jax.experimental.pallas import tpu as pltpu
from jax.sharding import PartitionSpec as P

BLOCK = 256
CHUNKS = 2
VMEM_BYTES = 24 << 20


def swap(value, axis, size, mask):
    return lax.ppermute(value, axis, [(i, i ^ mask) for i in range(size)])


def masked_copy(dst_ref, w_ref, m_ref, first_col, tile):
    rows, cols = w_ref.shape
    for i in range(rows // tile):
        for t in range(cols // tile):
            keep = m_ref[i, first_col + t] != 0
            part = (pl.ds(i * tile, tile), pl.ds(t * tile, tile))
            dst_ref[part] = jnp.where(keep, w_ref[part], jnp.zeros((), w_ref.dtype))


def project_kernel(groups, tile, s_ref, gm_ref, um_ref, *refs):
    n_out = groups * CHUNKS
    x_refs, (gw_ref, uw_ref) = refs[: -n_out - 4], refs[-n_out - 4 : -n_out - 2]
    outs, (x_all, w_all) = refs[-n_out - 2 : -2], refs[-2:]
    j = pl.program_id(0)
    width = w_all.shape[1]

    @pl.when(j == 0)
    def _():
        pos = 0
        for x_ref in x_refs:
            for k in range(x_ref.shape[0]):
                part = x_ref.shape[-1]
                start = pl.multiple_of(s_ref[1 + pos] * part, part)
                for g in range(groups):
                    rows = x_ref.shape[2]
                    x_all[pl.ds(g * rows, rows), pl.ds(start, part)] = x_ref[k, g]
                pos += 1

    for which, (w_ref, m_ref) in enumerate(((gw_ref, gm_ref), (uw_ref, um_ref))):
        masked_copy(w_all, w_ref, m_ref, j * (width // tile), tile)
        product = jnp.dot(x_all[...], w_all[...], preferred_element_type=jnp.float32).astype(jnp.bfloat16)
        rows = product.shape[0] // groups
        half = rows // 2
        piece = half // CHUNKS
        for g in range(groups):
            for k in range(CHUNKS):
                for b in range(2):
                    at = g * rows + b * half + k * piece
                    outs[g * CHUNKS + k][which, b * piece : (b + 1) * piece, :] = product[at : at + piece]


def project(scalars, xs, x_specs, rows, groups, gate_weight, up_weight, gate_mask, up_mask):
    panel, cols = gate_weight.shape
    tile = panel // gate_mask.shape[0]
    width = min(BLOCK, cols)
    out = jax.ShapeDtypeStruct((2, rows // CHUNKS, cols), jnp.bfloat16)
    smem = pl.BlockSpec(memory_space=pltpu.SMEM)
    weight = pl.BlockSpec((panel, width), lambda j, s: (0, j))
    return pl.pallas_call(
        functools.partial(project_kernel, groups, tile),
        grid_spec=pltpu.PrefetchScalarGridSpec(
            num_scalar_prefetch=1,
            grid=(cols // width,),
            in_specs=[smem, smem, *x_specs, weight, weight],
            out_specs=[pl.BlockSpec((2, rows // CHUNKS, width), lambda j, s: (0, 0, j))] * (groups * CHUNKS),
            scratch_shapes=[
                pltpu.VMEM((groups * rows, panel), jnp.bfloat16),
                pltpu.VMEM((panel, width), jnp.bfloat16),
            ],
        ),
        out_shape=[out] * (groups * CHUNKS),
        compiler_params=pltpu.CompilerParams(vmem_limit_bytes=VMEM_BYTES),
        cost_estimate=pl.CostEstimate(
            flops=4 * groups * rows * panel * cols, bytes_accessed=4 * panel * cols, transcendentals=0
        ),
    )(scalars, gate_mask, up_mask, *xs, gate_weight, up_weight)


def down_kernel(n_row, tile, s_ref, m_ref, *refs):
    x_refs, w_ref = refs[:n_row], refs[n_row]
    keep_ref, give_ref, x_all, w_all = refs[n_row + 1 :]
    j = pl.program_id(0)
    rows = x_refs[0].shape[0]

    @pl.when(j == 0)
    def _():
        for d in range(n_row):
            x_all[pl.ds(pl.multiple_of((s_ref[0] ^ d) * rows, rows), rows), :] = x_refs[d][...]

    masked_copy(w_all, w_ref, m_ref, j * (w_ref.shape[1] // tile), tile)
    product = jnp.dot(x_all[...], w_all[...], preferred_element_type=jnp.float32).astype(jnp.bfloat16)
    half = rows // 2
    first = s_ref[1] == 0
    for e in range(n_row):
        low, high = (product[e * rows + b * half : e * rows + (b + 1) * half] for b in range(2))
        keep_ref[e] = jnp.where(first, low, high)
        give_ref[e] = jnp.where(first, high, low)


def project_down(scalars, hidden, down_weight, down_mask):
    n_row = len(hidden)
    rows, panel = hidden[0].shape
    cols = down_weight.shape[1]
    tile = panel // down_mask.shape[0]
    width = min(BLOCK, cols)
    out = jax.ShapeDtypeStruct((n_row, rows // 2, cols), jnp.bfloat16)
    out_spec = pl.BlockSpec((n_row, rows // 2, width), lambda j, s: (0, 0, j))
    return pl.pallas_call(
        functools.partial(down_kernel, n_row, tile),
        grid_spec=pltpu.PrefetchScalarGridSpec(
            num_scalar_prefetch=1,
            grid=(cols // width,),
            in_specs=[pl.BlockSpec(memory_space=pltpu.SMEM)]
            + [pl.BlockSpec((rows, panel), lambda j, s: (0, 0))] * n_row
            + [pl.BlockSpec((panel, width), lambda j, s: (0, j))],
            out_specs=[out_spec] * 2,
            scratch_shapes=[
                pltpu.VMEM((n_row * rows, panel), jnp.bfloat16),
                pltpu.VMEM((panel, width), jnp.bfloat16),
            ],
        ),
        out_shape=[out] * 2,
        compiler_params=pltpu.CompilerParams(vmem_limit_bytes=VMEM_BYTES),
        cost_estimate=pl.CostEstimate(
            flops=2 * n_row * rows * panel * cols, bytes_accessed=2 * panel * cols, transcendentals=0
        ),
    )(scalars, down_mask, *hidden, down_weight)


def add(*terms):
    return functools.reduce(lambda a, b: a + b, (t.astype(jnp.float32) for t in terms))


def on_device(n_row, n_col, tokens, gate_weight, up_weight, down_weight, gate_mask, up_mask, down_mask):
    assert n_col == 2 * n_row and n_row & (n_row - 1) == 0
    rows = tokens.shape[0]
    panel = gate_weight.shape[0]
    row, col = lax.axis_index("row"), lax.axis_index("col")
    weights = (gate_weight, up_weight, gate_mask, up_mask)

    slices = min(n_col, panel // BLOCK)
    part = panel // slices
    mine = []
    for d in range(1, n_row):
        start = (row ^ d) * panel + (col % slices) * part
        mine.append(swap(lax.dynamic_slice(tokens, (0, start), (rows, part)), "row", n_row, d))
    mine = jnp.stack(mine)
    even = jnp.stack([mine] + [swap(mine, "col", n_col, e) for e in range(2, slices, 2)])
    odd = swap(even, "col", n_col, 1)

    zero = jnp.zeros((2,), jnp.int32)
    own_spec = pl.BlockSpec((1, 1, rows, panel), lambda j, s: (0, 0, 0, s[0]))
    own = project(zero.at[0].set(row), [tokens[None, None]], [own_spec], rows, 1, *weights)
    order = jnp.asarray([*range(0, slices, 2), *range(1, slices, 2)], jnp.int32)
    scalars = jnp.concatenate([row[None], (col % slices) ^ order])
    whole = pl.BlockSpec((slices // 2, n_row - 1, rows, part), lambda j, s: (0, 0, 0, 0))
    others = project(scalars, [even, odd], [whole] * 2, rows, n_row - 1, *weights)
    sums = [own] + [others[g * CHUNKS : (g + 1) * CHUNKS] for g in range(n_row - 1)]

    place = jnp.stack([(col // 2) ^ row, col % 2]).astype(jnp.int32)
    result = []
    for k in range(CHUNKS):
        held = {d: sums[d][k] for d in range(n_row)}
        bit = 1
        while bit < n_row:
            for d in [d for d in held if not d & bit]:
                total = add(swap(held.pop(d), "row", n_row, bit), held[d | bit])
                held[d | bit] = total.astype(jnp.bfloat16) if 2 * bit < n_row else total
            bit *= 2
        gate, up = held[n_row - 1]
        hidden = {n_row - 1: (jax.nn.silu(gate) * up).astype(jnp.bfloat16)}
        while bit > 1:
            bit //= 2
            for d in list(hidden):
                hidden[d ^ bit] = swap(hidden[d], "row", n_row, bit)
        keep, give = project_down(place, [hidden[d] for d in range(n_row)], down_weight, down_mask)
        share = add(keep, swap(give, "col", n_col, 1)).astype(jnp.bfloat16)
        came = [swap(share[e], "col", n_col, 2 * e) for e in range(1, n_row)]
        result.append(add(share[0], *came).astype(jnp.bfloat16))
    return jnp.concatenate(result)


def solution(mesh):
    return jax.shard_map(
        functools.partial(on_device, mesh.shape["row"], mesh.shape["col"]),
        mesh=mesh,
        in_specs=(
            P("row", None),
            P("row", "col"),
            P("row", "col"),
            P("col", "row"),
            P("row", "col"),
            P("row", "col"),
            P("col", "row"),
        ),
        out_specs=P("col", "row"),
        check_vma=False,
    )
```

time: 1130 us -> 187 us (0.17); the launches traced: 1120 us -> 187 us
  waiting for transfers between devices: 683 us -> 93.9 us
  local copies, waits for them, and re-layouts: 275 us -> 18.4 us
  matrix products: 124 us -> 0 us
  Pallas kernels: 0 us -> 39.3 us
  starting transfers between devices: 0.59 us -> 31.5 us
  blocking collectives: 18.1 us -> 0 us
  between operations: 14.4 us -> 0.27 us
    all_gather x3 -> x0, waiting for transfers between devices: 643 us -> none  [the longest x1 370 us: on_device(): gate_piece = lax.all_gather(gate_packed, 'row', axis=0, tiled=True)]
    reshape x6 -> x0, local copies, waits for them, and re-layouts: 144 us -> none  [the longest x2 98.9 us: unpack_tiles(): return dense.reshape(groups, tile_rows * tile, tile_cols * tile)]
    dot_general x7 -> x0, matrix products: 124 us -> none  [the longest x2 61.7 us: unpack_tiles(): jnp.einsum('gcs,gsab->gcab', spread, packed, preferred_element_type=jnp.f...]
    transpose x1 -> x0, local copies, waits for them, and re-layouts: 98.3 us -> none  [unpack_tiles(): dense.reshape(groups, tile_rows, tile_cols, tile, tile)]
    ppermute x0 -> x27, waiting for transfers between devices: none -> 93.9 us  [swap(): return lax.ppermute(value, axis, [(i, i ^ mask) for i in range(size)])]
    reduce_scatter x1 -> x0, waiting for transfers between devices: 39.6 us -> none  [on_device(): lax.psum_scatter(jnp.dot(all_hidden, down_eff, preferred_element_type=jnp...]
    pallas_call x0 -> x4, Pallas kernels: none -> 39.3 us  [the longest x2 24.9 us: project(): pl.pallas_call(functools.partial(project_kernel, groups, tile), grid_spec...]
    ppermute x0 -> x27, starting transfers between devices: none -> 31.5 us  [swap(): return lax.ppermute(value, axis, [(i, i ^ mask) for i in range(size)])]
  transfers between devices with their start and end apart: 4 -> 27, of which waited for: 4 -> 15; matrix products, arithmetic and copies ran while one was open for 21% -> 1% of each run, Pallas kernels for 0% -> 21%
where the time goes in v1:
time: 187 us
  waiting for transfers between devices  93.9 us (50%)
  Pallas kernels  39.3 us (21%)
  starting transfers between devices  31.5 us (17%)
  local copies, waits for them, and re-layouts  18.4 us (10%)
  other arithmetic  3.4 us (2%)
    ppermute x27, waiting for transfers between devices, swap(): return lax.ppermute(value, axis, [(i, i ^ mask) for i in range(size)])  93.9 us
    ppermute x27, starting transfers between devices, swap(): return lax.ppermute(value, axis, [(i, i ^ mask) for i in range(size)])  31.5 us
    pallas_call x2, Pallas kernels, project(): pl.pallas_call(functools.partial(project_kernel, groups, tile), grid_spec...  24.9 us
    unnamed x26, local copies, waits for them, and re-layouts  17.5 us
    pallas_call x2, Pallas kernels, project_down(): pl.pallas_call(functools.partial(down_kernel, n_row, tile), grid_spec=plt...  14.4 us
  transfers between devices with their start and end apart: 27, of which 15 were waited for; matrix products, arithmetic and copies ran while one was open for 1% of the time, Pallas kernels for 21%

profile of v1, /device:TPU:0, one launch (start us, length us, event | category | flops | bytes accessed | tf_op | source)
XLA Modules:
  0.0 186.9 jit_solution(4578180229454202447)
XLA Ops:
  0.0 0.9 constant_dynamic-slice_fusion.2
  0.9 5.1 %collective-permute-start.3 = (bf16[128,256]{1,0:T(8,128)(2,1)S(1)}, bf16[128,256]{1,0:T(8,128)(2,1)S(1)}, u32[]{:S(2)}, u32[]{:S(2)}) collective-permute-start(bf16[128,256]{1,0:T(8,128)(2,1)S(1)} %get-tuple-element.42), channel_id=1, source_target_pairs={{0,24},{8,16},{16,8},{24,0},{1,25},{9,17},{17,9},{25,1},{2,26},{10... | collective-permute-start | bytes 196616 | tf_op jit(solution)/shard_map/ppermute | solution.py:16
  6.0 0.6 collective-permute-start.1
  6.7 1.9 %collective-permute-done.3 = bf16[128,256]{1,0:T(8,128)(2,1)S(1)} collective-permute-done((bf16[128,256]{1,0:T(8,128)(2,1)S(1)}, bf16[128,256]{1,0:T(8,128)(2,1)S(1)}, u32[]{:S(2)}, u32[]{:S(2)}) %collective-permute-start.3) | collective-permute-done | bytes 65568 | tf_op jit(solution)/shard_map/ppermute | solution.py:16
  8.6 3.0 %collective-permute-done.2 = bf16[128,256]{1,0:T(8,128)(2,1)S(1)} collective-permute-done((bf16[128,256]{1,0:T(8,128)(2,1)S(1)}, bf16[128,256]{1,0:T(8,128)(2,1)S(1)}, u32[]{:S(2)}, u32[]{:S(2)}) %collective-permute-start.2) | collective-permute-done | bytes 65568 | tf_op jit(solution)/shard_map/ppermute | solution.py:16
  11.7 2.5 %collective-permute-start.6 = (bf16[3,128,256]{2,1,0:T(8,128)(2,1)S(1)}, bf16[3,128,256]{2,1,0:T(8,128)(2,1)S(1)}, u32[]{:S(2)}, u32[]{:S(2)}) collective-permute-start(bf16[3,128,256]{2,1,0:T(8,128)(2,1)S(1)} %get-tuple-element.51), channel_id=1, source_target_pairs={{0,6},{1,7},{2,4},{3,5},{4,2},{5,3},{6,0},{7,1},{8,14},{9,15},{10,... | collective-permute-start | bytes 589832 | tf_op jit(solution)/shard_map/ppermute | solution.py:16
  14.2 0.5 collective-permute-start.5
  14.7 0.5 collective-permute-start.4
  15.2 5.2 %collective-permute-done.6 = bf16[3,128,256]{2,1,0:T(8,128)(2,1)S(1)} collective-permute-done((bf16[3,128,256]{2,1,0:T(8,128)(2,1)S(1)}, bf16[3,128,256]{2,1,0:T(8,128)(2,1)S(1)}, u32[]{:S(2)}, u32[]{:S(2)}) %collective-permute-start.6) | collective-permute-done | bytes 196640 | tf_op jit(solution)/shard_map/ppermute | solution.py:16
  20.5 2.9 %collective-permute-done.5 = bf16[3,128,256]{2,1,0:T(8,128)(2,1)S(1)} collective-permute-done((bf16[3,128,256]{2,1,0:T(8,128)(2,1)S(1)}, bf16[3,128,256]{2,1,0:T(8,128)(2,1)S(1)}, u32[]{:S(2)}, u32[]{:S(2)}) %collective-permute-start.5) | collective-permute-done | bytes 196640 | tf_op jit(solution)/shard_map/ppermute | solution.py:16
  23.3 0.3 collective-permute-done.4
  23.6 0.1 pad_maximum_fusion.refs_0_
  23.7 0.1 collective-permute-start.7
  23.8 3.4 %copy-done = bf16[2048,2048]{1,0:T(8,128)(2,1)S(1)} copy-done((bf16[2048,2048]{1,0:T(8,128)(2,1)S(1)}, bf16[2048,2048]{1,0:T(8,128)(2,1)}, u32[]{:S(2)}) %copy-start) | copy-done | bytes 8388632
  27.2 3.4 %copy-done.2 = bf16[2048,2048]{1,0:T(8,128)(2,1)S(1)} copy-done((bf16[2048,2048]{1,0:T(8,128)(2,1)S(1)}, bf16[2048,2048]{1,0:T(8,128)(2,1)}, u32[]{:S(2)}) %copy-start.2) | copy-done | bytes 8388632
  30.6 1.6 copy-done.4
  32.2 0.7 copy-done.6
  32.9 0.7 copy-done.8
  33.6 11.1 %shard_map.82 = (bf16[2,64,2048]{2,1,0:T(8,128)(2,1)S(1)}, bf16[2,64,2048]{2,1,0:T(8,128)(2,1)S(1)}) custom-call(s32[2]{0:T(128)S(1)} %scatter.4.s_ref, s32[16,16]{1,0:T(8,128)S(1)} %copy-done.6, s32[16,16]{1,0:T(8,128)S(1)} %copy-done.8, bf16[1,1,128,8192]{3,2,1,0:T(8,128)(2,1)S(1)} %bitcast.56, bf16[2048,2048]{1,0:T(8,128)(2,1)S(1)} %copy-done, ...), custom_call_target="tpu_custom_call" | custom-call | flops 2147483648 | bytes 16777216 | tf_op jit(solution)/shard_map/pallas_call | solution.py:67
  44.7 0.1 collective-permute-start.17
  44.8 2.0 %collective-permute-start = (bf16[2,64,2048]{2,1,0:T(8,128)(2,1)S(1)}, bf16[2,64,2048]{2,1,0:T(8,128)(2,1)S(1)}, u32[]{:S(2)}, u32[]{:S(2)}) collective-permute-start(bf16[2,64,2048]{2,1,0:T(8,128)(2,1)S(1)} %get-tuple-element.29), channel_id=1, source_target_pairs={{0,8},{8,0},{16,24},{24,16},{1,9},{9,1},{17,25},{25,17},{2,10},{10... | collective-permute-start | bytes 1572872 | tf_op jit(solution)/shard_map/ppermute | solution.py:16
  46.8 0.1 pad_add_fusion.1.s_ref
  46.9 3.5 %copy-done.1 = bf16[2048,2048]{1,0:T(8,128)(2,1)S(1)} copy-done((bf16[2048,2048]{1,0:T(8,128)(2,1)S(1)}, bf16[2048,2048]{1,0:T(8,128)(2,1)}, u32[]{:S(2)}) %copy-start.1) | copy-done | bytes 8388632
  50.4 4.2 %copy-done.3 = bf16[2048,2048]{1,0:T(8,128)(2,1)S(1)} copy-done((bf16[2048,2048]{1,0:T(8,128)(2,1)S(1)}, bf16[2048,2048]{1,0:T(8,128)(2,1)}, u32[]{:S(2)}) %copy-start.3) | copy-done | bytes 8388632
  54.6 13.7 %shard_map.83 = (bf16[2,64,2048]{2,1,0:T(8,128)(2,1)S(1)}, bf16[2,64,2048]{2,1,0:T(8,128)(2,1)S(1)}, bf16[2,64,2048]{2,1,0:T(8,128)(2,1)S(1)}, bf16[2,64,2048]{2...) custom-call(s32[9]{0:T(128)S(1)} %pad_add_fusion.1.s_ref, ...), custom_call_target="tpu_custom_call" | custom-call | flops 6442450944 | bytes 16777216 | tf_op jit(solution)/shard_map/pallas_call | solution.py:67
  68.4 1.2 add_convert_fusion.2
  69.5 0.2 collective-permute-start.18
  69.8 1.8 collective-permute-start.19
  71.6 0.1 pad_add_fusion.s_ref
  71.7 0.1 add_convert_fusion.5
  71.8 1.1 collective-permute-start.8
  72.9 1.9 %collective-permute-start.9 = (bf16[2,64,2048]{2,1,0:T(8,128)(2,1)S(1)}, bf16[2,64,2048]{2,1,0:T(8,128)(2,1)S(1)}, u32[]{:S(2)}, u32[]{:S(2)}) collective-permute-start(bf16[2,64,2048]{2,1,0:T(8,128)(2,1)S(1)} %get-tuple-element.31), channel_id=1, source_target_pairs={{0,8},{8,0},{16,24},{24,16},{1,9},{9,1},{17,25},{25,17},{2,10},{10... | collective-permute-start | bytes 1572872 | tf_op jit(solution)/shard_map/ppermute | solution.py:16
  74.8 21.3 %collective-permute-done.18 = bf16[2,64,2048]{2,1,0:T(8,128)(2,1)S(1)} collective-permute-done((bf16[2,64,2048]{2,1,0:T(8,128)(2,1)S(1)}, bf16[2,64,2048]{2,1,0:T(8,128)(2,1)S(1)}, u32[]{:S(2)}, u32[]{:S(2)}) %collective-permute-start.18) | collective-permute-done | bytes 524320 | tf_op jit(solution)/shard_map/ppermute | solution.py:16
  96.2 0.2 convert_add_fusion
  96.4 0.1 fusion.1.refs_3_
  96.5 0.5 collective-permute-start.20
  97.1 2.0 %collective-permute-start.22 = (bf16[64,2048]{1,0:T(8,128)(2,1)S(1)}, bf16[64,2048]{1,0:T(8,128)(2,1)S(1)}, u32[]{:S(2)}, u32[]{:S(2)}) collective-permute-start(bf16[64,2048]{1,0:T(8,128)(2,1)S(1)} %fusion.1.refs_3_), channel_id=1, source_target_pairs={{0,8},{8,0},{16,24},{24,16},{1,9},{9,1},{17,25},{25,17},{2,10},{10... | collective-permute-start | bytes 786440 | tf_op jit(solution)/shard_map/ppermute | solution.py:16
  99.1 19.6 %collective-permute-done.8 = bf16[2,64,2048]{2,1,0:T(8,128)(2,1)S(1)} collective-permute-done((bf16[2,64,2048]{2,1,0:T(8,128)(2,1)S(1)}, bf16[2,64,2048]{2,1,0:T(8,128)(2,1)S(1)}, u32[]{:S(2)}, u32[]{:S(2)}) %collective-permute-start.8) | collective-permute-done | bytes 524320 | tf_op jit(solution)/shard_map/ppermute | solution.py:16
  118.7 0.2 convert_add_fusion.1
  118.9 10.2 %collective-permute-done.20.refs_1_ = bf16[64,2048]{1,0:T(8,128)(2,1)S(1)} collective-permute-done((bf16[64,2048]{1,0:T(8,128)(2,1)S(1)}, bf16[64,2048]{1,0:T(8,128)(2,1)S(1)}, u32[]{:S(2)}, u32[]{:S(2)}) %collective-permute-start.20) | collective-permute-done | bytes 262176 | tf_op jit(solution)/shard_map/ppermute | solution.py:16
  129.1 0.1 fusion.3.refs_3_
  129.2 2.2 %collective-permute-start.10 = (bf16[64,2048]{1,0:T(8,128)(2,1)S(1)}, bf16[64,2048]{1,0:T(8,128)(2,1)S(1)}, u32[]{:S(2)}, u32[]{:S(2)}) collective-permute-start(bf16[64,2048]{1,0:T(8,128)(2,1)S(1)} %fusion.3.refs_3_), channel_id=1, source_target_pairs={{0,16},{8,24},{16,0},{24,8},{1,17},{9,25},{17,1},{25,9},{2,18},{10... | collective-permute-start | bytes 786440 | tf_op jit(solution)/shard_map/ppermute | solution.py:16
  131.4 10.2 %collective-permute-done.21.refs_0_ = bf16[64,2048]{1,0:T(8,128)(2,1)S(1)} collective-permute-done((bf16[64,2048]{1,0:T(8,128)(2,1)S(1)}, bf16[64,2048]{1,0:T(8,128)(2,1)S(1)}, u32[]{:S(2)}, u32[]{:S(2)}) %collective-permute-start.21) | collective-permute-done | bytes 262176 | tf_op jit(solution)/shard_map/ppermute | solution.py:16
  141.6 7.2 %shard_map.85 = (bf16[4,32,2048]{2,1,0:T(8,128)(2,1)S(1)}, bf16[4,32,2048]{2,1,0:T(8,128)(2,1)S(1)}) custom-call(s32[2]{0:T(128)S(1)} %pad_add_fusion.s_ref, s32[16,16]{1,0:T(8,128)S(1)} %copy-done.5, bf16[64,2048]{1,0:T(8,128)(2,1)S(1)} %collective-permute-done.21.refs_0_, bf16[64,2048]{1,0:T(8,128)(2,1)S(1)} %collective-permute-done.20.refs_1_, ...), custom_call_target="tpu_custom_call" | custom-call | flops 2147483648 | bytes 8388608 | tf_op jit(solution)/shard_map/pallas_call | solution.py:116
  148.8 0.1 collective-permute-start.23
  148.9 0.1 collective-permute-start.12
  149.0 2.0 %collective-permute-start.11 = (bf16[64,2048]{1,0:T(8,128)(2,1)S(1)}, bf16[64,2048]{1,0:T(8,128)(2,1)S(1)}, u32[]{:S(2)}, u32[]{:S(2)}) collective-permute-start(bf16[64,2048]{1,0:T(8,128)(2,1)S(1)} %collective-permute-done.10.refs_1_), channel_id=1, source_target_pairs={{0,8},{8,0},{16,24},{24,16},{1,9},{9,1},{17,25},{25,17},{2,10},{10... | collective-permute-start | bytes 786440 | tf_op jit(solution)/shard_map/ppermute | solution.py:16
  151.0 7.1 %collective-permute-done.12.refs_2_ = bf16[64,2048]{1,0:T(8,128)(2,1)S(1)} collective-permute-done((bf16[64,2048]{1,0:T(8,128)(2,1)S(1)}, bf16[64,2048]{1,0:T(8,128)(2,1)S(1)}, u32[]{:S(2)}, u32[]{:S(2)}) %collective-permute-start.12) | collective-permute-done | bytes 262176 | tf_op jit(solution)/shard_map/ppermute | solution.py:16
  158.1 5.2 %collective-permute-done.11.refs_0_ = bf16[64,2048]{1,0:T(8,128)(2,1)S(1)} collective-permute-done((bf16[64,2048]{1,0:T(8,128)(2,1)S(1)}, bf16[64,2048]{1,0:T(8,128)(2,1)S(1)}, u32[]{:S(2)}, u32[]{:S(2)}) %collective-permute-start.11) | collective-permute-done | bytes 262176 | tf_op jit(solution)/shard_map/ppermute | solution.py:16
  163.3 7.2 %shard_map.84 = (bf16[4,32,2048]{2,1,0:T(8,128)(2,1)S(1)}, bf16[4,32,2048]{2,1,0:T(8,128)(2,1)S(1)}) custom-call(s32[2]{0:T(128)S(1)} %pad_add_fusion.s_ref, s32[16,16]{1,0:T(8,128)S(1)} %copy-done.5, bf16[64,2048]{1,0:T(8,128)(2,1)S(1)} %collective-permute-done.11.refs_0_, bf16[64,2048]{1,0:T(8,128)(2,1)S(1)} %collective-permute-done.10.refs_1_, ...), custom_call_target="tpu_custom_call" | custom-call | flops 2147483648 | bytes 8388608 | tf_op jit(solution)/shard_map/pallas_call | solution.py:116
  170.5 0.1 collective-permute-start.13
  170.6 0.1 add_convert_fusion
  170.7 1.7 collective-permute-start.26
  172.4 1.3 collective-permute-start.25
  173.8 0.5 collective-permute-start.24
  174.3 0.1 add_convert_fusion.3
  174.5 1.7 collective-permute-start.16
  176.2 1.3 collective-permute-start.15
  177.5 0.5 collective-permute-done.26
  178.0 1.5 collective-permute-start.14
  179.5 1.3 collective-permute-done.25
  180.9 2.7 %collective-permute-done.16 = bf16[32,2048]{1,0:T(8,128)(2,1)S(1)} collective-permute-done((bf16[32,2048]{1,0:T(8,128)(2,1)S(1)}, bf16[32,2048]{1,0:T(8,128)(2,1)S(1)}, u32[]{:S(2)}, u32[]{:S(2)}) %collective-permute-start.16) | collective-permute-done | bytes 131104 | tf_op jit(solution)/shard_map/ppermute | solution.py:16
  183.7 2.3 %collective-permute-done.15 = bf16[32,2048]{1,0:T(8,128)(2,1)S(1)} collective-permute-done((bf16[32,2048]{1,0:T(8,128)(2,1)S(1)}, bf16[32,2048]{1,0:T(8,128)(2,1)S(1)}, u32[]{:S(2)}, u32[]{:S(2)}) %collective-permute-start.15) | collective-permute-done | bytes 131104 | tf_op jit(solution)/shard_map/ppermute | solution.py:16
  186.1 0.7 pad_maximum_fusion.1
  (41 shorter events, 0.4 us)
Async XLA Ops:
  0.9 7.7 %collective-permute-start.3 = (bf16[128,256]{1,0:T(8,128)(2,1)S(1)}, bf16[128,256]{1,0:T(8,128)(2,1)S(1)}, u32[]{:S(2)}, u32[]{:S(2)}) collective-permute-start(bf16[128,256]{1,0:T(8,128)(2,1)S(1)} %get-tuple-element.42), channel_id=1, source_target_pairs={{0,24},{8,16},{16,8},{24,0},{1,25},{9,17},{17,9},{25,1},{2,26},{10... | collective-permute-start | bytes 196616 | tf_op jit(solution)/shard_map/ppermute | solution.py:16
  6.0 5.6 %collective-permute-start.2 = (bf16[128,256]{1,0:T(8,128)(2,1)S(1)}, bf16[128,256]{1,0:T(8,128)(2,1)S(1)}, u32[]{:S(2)}, u32[]{:S(2)}) collective-permute-start(bf16[128,256]{1,0:T(8,128)(2,1)S(1)} %get-tuple-element.43), channel_id=1, source_target_pairs={{0,16},{8,24},{16,0},{24,8},{1,17},{9,25},{17,1},{25,9},{2,18},{10... | collective-permute-start | bytes 196616 | tf_op jit(solution)/shard_map/ppermute | solution.py:16
  6.0 5.6 %collective-permute-start.1 = (bf16[128,256]{1,0:T(8,128)(2,1)S(1)}, bf16[128,256]{1,0:T(8,128)(2,1)S(1)}, u32[]{:S(2)}, u32[]{:S(2)}) collective-permute-start(bf16[128,256]{1,0:T(8,128)(2,1)S(1)} %get-tuple-element.41), channel_id=1, source_target_pairs={{0,8},{8,0},{16,24},{24,16},{1,9},{9,1},{17,25},{25,17},{2,10},{10... | collective-permute-start | bytes 196616 | tf_op jit(solution)/shard_map/ppermute | solution.py:16
  11.7 8.8 %collective-permute-start.6 = (bf16[3,128,256]{2,1,0:T(8,128)(2,1)S(1)}, bf16[3,128,256]{2,1,0:T(8,128)(2,1)S(1)}, u32[]{:S(2)}, u32[]{:S(2)}) collective-permute-start(bf16[3,128,256]{2,1,0:T(8,128)(2,1)S(1)} %get-tuple-element.51), channel_id=1, source_target_pairs={{0,6},{1,7},{2,4},{3,5},{4,2},{5,3},{6,0},{7,1},{8,14},{9,15},{10,... | collective-permute-start | bytes 589832 | tf_op jit(solution)/shard_map/ppermute | solution.py:16
  14.2 9.1 %collective-permute-start.5 = (bf16[3,128,256]{2,1,0:T(8,128)(2,1)S(1)}, bf16[3,128,256]{2,1,0:T(8,128)(2,1)S(1)}, u32[]{:S(2)}, u32[]{:S(2)}) collective-permute-start(bf16[3,128,256]{2,1,0:T(8,128)(2,1)S(1)} %get-tuple-element.51), channel_id=1, source_target_pairs={{0,4},{1,5},{2,6},{3,7},{4,0},{5,1},{6,2},{7,3},{8,12},{9,13},{10,... | collective-permute-start | bytes 589832 | tf_op jit(solution)/shard_map/ppermute | solution.py:16
  14.7 8.9 %collective-permute-start.4 = (bf16[3,128,256]{2,1,0:T(8,128)(2,1)S(1)}, bf16[3,128,256]{2,1,0:T(8,128)(2,1)S(1)}, u32[]{:S(2)}, u32[]{:S(2)}) collective-permute-start(bf16[3,128,256]{2,1,0:T(8,128)(2,1)S(1)} %get-tuple-element.51), channel_id=1, source_target_pairs={{0,2},{1,3},{2,0},{3,1},{4,6},{5,7},{6,4},{7,5},{8,10},{9,11},{10,... | collective-permute-start | bytes 589832 | tf_op jit(solution)/shard_map/ppermute | solution.py:16
  23.7 23.2 %collective-permute-start.7 = (bf16[4,3,128,256]{3,2,1,0:T(8,128)(2,1)S(1)}, bf16[4,3,128,256]{3,2,1,0:T(8,128)(2,1)S(1)}, u32[]{:S(2)}, u32[]{:S(2)}) collective-permute-start(bf16[4,3,128,256]{3,2,1,0:T(8,128)(2,1)S(1)} %pad_maximum_fusion.refs_0_), channel_id=1, source_target_pairs={{0,1},{1,0},{2,3},{3,2},{4,5},{5,4},{6,7},{7,6},{8,9},{9,8},{10,11... | collective-permute-start | bytes 2359304 | tf_op jit(solution)/shard_map/ppermute | solution.py:16
  23.8 3.4 %copy-start = (bf16[2048,2048]{1,0:T(8,128)(2,1)S(1)}, bf16[2048,2048]{1,0:T(8,128)(2,1)}, u32[]{:S(2)}) copy-start(bf16[2048,2048]{1,0:T(8,128)(2,1)} %refs_2_.3) | copy-start | bytes 25165828
  27.2 3.4 %copy-start.2 = (bf16[2048,2048]{1,0:T(8,128)(2,1)S(1)}, bf16[2048,2048]{1,0:T(8,128)(2,1)}, u32[]{:S(2)}) copy-start(bf16[2048,2048]{1,0:T(8,128)(2,1)} %refs_3_.1) | copy-start | bytes 25165828
  30.6 1.6 copy-start.4
  32.2 0.7 copy-start.6
  32.9 0.7 copy-start.8
  33.6 13.2 %copy-start.10 = (s32[8]{0:T(128)S(1)}, s32[8]{0:T(128)}, u32[]{:S(2)}) copy-start(s32[8]{0:T(128)} %constant.88.clone) | copy-start | bytes 100
  33.6 13.3 %copy-start.7 = (s32[16,16]{1,0:T(8,128)S(1)}, s32[16,16]{1,0:T(8,128)}, u32[]{:S(2)}) copy-start(s32[16,16]{1,0:T(8,128)} %gm_ref.3) | copy-start | bytes 3076
  33.6 13.3 %copy-start.9 = (s32[16,16]{1,0:T(8,128)S(1)}, s32[16,16]{1,0:T(8,128)}, u32[]{:S(2)}) copy-start(s32[16,16]{1,0:T(8,128)} %um_ref.3) | copy-start | bytes 3076
  44.7 23.6 %collective-permute-start.17 = (bf16[2,64,2048]{2,1,0:T(8,128)(2,1)S(1)}, bf16[2,64,2048]{2,1,0:T(8,128)(2,1)}, u32[]{:S(2)}, u32[]{:S(2)}) collective-permute-start(bf16[2,64,2048]{2,1,0:T(8,128)(2,1)S(1)} %get-tuple-element.35), channel_id=1, source_target_pairs={{0,8},{8,0},{16,24},{24,16},{1,9},{9,1},{17,25},{25,17},{2,10},{10... | collective-permute-start | bytes 1572872 | tf_op jit(solution)/shard_map/ppermute | solution.py:16
  44.8 26.9 %collective-permute-start = (bf16[2,64,2048]{2,1,0:T(8,128)(2,1)S(1)}, bf16[2,64,2048]{2,1,0:T(8,128)(2,1)S(1)}, u32[]{:S(2)}, u32[]{:S(2)}) collective-permute-start(bf16[2,64,2048]{2,1,0:T(8,128)(2,1)S(1)} %get-tuple-element.29), channel_id=1, source_target_pairs={{0,8},{8,0},{16,24},{24,16},{1,9},{9,1},{17,25},{25,17},{2,10},{10... | collective-permute-start | bytes 1572872 | tf_op jit(solution)/shard_map/ppermute | solution.py:16
  46.8 94.8 %slice-start = ((s8[8388608]{0:T(1024)(128)(4,1)}), s8[4194304]{0:T(1024)(128)(4,1)S(1)}, s32[]{:S(2)}) async-start(s8[8388608]{0:T(1024)(128)(4,1)} %bitcast.54), calls=%async_computation | async-start | bytes 8388608
  46.9 94.7 %slice-start.1 = ((s8[8388608]{0:T(1024)(128)(4,1)}), s8[4194304]{0:T(1024)(128)(4,1)S(1)}, s32[]{:S(2)}) async-start(s8[8388608]{0:T(1024)(128)(4,1)} %bitcast.54), calls=%async_computation.1 | async-start | bytes 8388608
  46.9 3.5 %copy-start.1 = (bf16[2048,2048]{1,0:T(8,128)(2,1)S(1)}, bf16[2048,2048]{1,0:T(8,128)(2,1)}, u32[]{:S(2)}) copy-start(bf16[2048,2048]{1,0:T(8,128)(2,1)} %refs_2_.3) | copy-start | bytes 25165828
  50.4 4.2 %copy-start.3 = (bf16[2048,2048]{1,0:T(8,128)(2,1)S(1)}, bf16[2048,2048]{1,0:T(8,128)(2,1)}, u32[]{:S(2)}) copy-start(bf16[2048,2048]{1,0:T(8,128)(2,1)} %refs_3_.1) | copy-start | bytes 25165828
  68.3 73.3 %copy-start.5 = (s32[16,16]{1,0:T(8,128)S(1)}, s32[16,16]{1,0:T(8,128)}, u32[]{:S(2)}) copy-start(s32[16,16]{1,0:T(8,128)} %m_ref.3) | copy-start | bytes 3076
  69.5 26.6 %collective-permute-start.18 = (bf16[2,64,2048]{2,1,0:T(8,128)(2,1)S(1)}, bf16[2,64,2048]{2,1,0:T(8,128)(2,1)S(1)}, u32[]{:S(2)}, u32[]{:S(2)}) collective-permute-start(bf16[2,64,2048]{2,1,0:T(8,128)(2,1)S(1)} %add_convert_fusion.2), channel_id=1, source_target_pairs={{0,16},{8,24},{16,0},{24,8},{1,17},{9,25},{17,1},{25,9},{2,18},{10... | collective-permute-start | bytes 1572872 | tf_op jit(solution)/shard_map/ppermute | solution.py:16
  69.8 26.4 %collective-permute-start.19 = (bf16[2,64,2048]{2,1,0:T(8,128)(2,1)S(1)}, bf16[2,64,2048]{2,1,0:T(8,128)(2,1)S(1)}, u32[]{:S(2)}, u32[]{:S(2)}) collective-permute-start(bf16[2,64,2048]{2,1,0:T(8,128)(2,1)S(1)} %get-tuple-element.37), channel_id=1, source_target_pairs={{0,8},{8,0},{16,24},{24,16},{1,9},{9,1},{17,25},{25,17},{2,10},{10... | collective-permute-start | bytes 1572872 | tf_op jit(solution)/shard_map/ppermute | solution.py:16
  71.8 46.9 %collective-permute-start.8 = (bf16[2,64,2048]{2,1,0:T(8,128)(2,1)S(1)}, bf16[2,64,2048]{2,1,0:T(8,128)(2,1)S(1)}, u32[]{:S(2)}, u32[]{:S(2)}) collective-permute-start(bf16[2,64,2048]{2,1,0:T(8,128)(2,1)S(1)} %add_convert_fusion.5), channel_id=1, source_target_pairs={{0,16},{8,24},{16,0},{24,8},{1,17},{9,25},{17,1},{25,9},{2,18},{10... | collective-permute-start | bytes 1572872 | tf_op jit(solution)/shard_map/ppermute | solution.py:16
  72.9 45.8 %collective-permute-start.9 = (bf16[2,64,2048]{2,1,0:T(8,128)(2,1)S(1)}, bf16[2,64,2048]{2,1,0:T(8,128)(2,1)S(1)}, u32[]{:S(2)}, u32[]{:S(2)}) collective-permute-start(bf16[2,64,2048]{2,1,0:T(8,128)(2,1)S(1)} %get-tuple-element.31), channel_id=1, source_target_pairs={{0,8},{8,0},{16,24},{24,16},{1,9},{9,1},{17,25},{25,17},{2,10},{10... | collective-permute-start | bytes 1572872 | tf_op jit(solution)/shard_map/ppermute | solution.py:16
  96.5 32.5 %collective-permute-start.20 = (bf16[64,2048]{1,0:T(8,128)(2,1)S(1)}, bf16[64,2048]{1,0:T(8,128)(2,1)S(1)}, u32[]{:S(2)}, u32[]{:S(2)}) collective-permute-start(bf16[64,2048]{1,0:T(8,128)(2,1)S(1)} %fusion.1.refs_3_), channel_id=1, source_target_pairs={{0,16},{8,24},{16,0},{24,8},{1,17},{9,25},{17,1},{25,9},{2,18},{10... | collective-permute-start | bytes 786440 | tf_op jit(solution)/shard_map/ppermute | solution.py:16
  97.1 34.3 %collective-permute-start.22 = (bf16[64,2048]{1,0:T(8,128)(2,1)S(1)}, bf16[64,2048]{1,0:T(8,128)(2,1)S(1)}, u32[]{:S(2)}, u32[]{:S(2)}) collective-permute-start(bf16[64,2048]{1,0:T(8,128)(2,1)S(1)} %fusion.1.refs_3_), channel_id=1, source_target_pairs={{0,8},{8,0},{16,24},{24,16},{1,9},{9,1},{17,25},{25,17},{2,10},{10... | collective-permute-start | bytes 786440 | tf_op jit(solution)/shard_map/ppermute | solution.py:16
  129.1 12.5 %collective-permute-start.21 = (bf16[64,2048]{1,0:T(8,128)(2,1)S(1)}, bf16[64,2048]{1,0:T(8,128)(2,1)S(1)}, u32[]{:S(2)}, u32[]{:S(2)}) collective-permute-start(bf16[64,2048]{1,0:T(8,128)(2,1)S(1)} %collective-permute-done.20.refs_1_), channel_id=1, source_target_pairs={{0,8},{8,0},{16,24},{24,16},{1,9},{9,1},{17,25},{25,17},{2,10},{10... | collective-permute-start | bytes 786440 | tf_op jit(solution)/shard_map/ppermute | solution.py:16
  129.2 19.8 %collective-permute-start.10 = (bf16[64,2048]{1,0:T(8,128)(2,1)S(1)}, bf16[64,2048]{1,0:T(8,128)(2,1)S(1)}, u32[]{:S(2)}, u32[]{:S(2)}) collective-permute-start(bf16[64,2048]{1,0:T(8,128)(2,1)S(1)} %fusion.3.refs_3_), channel_id=1, source_target_pairs={{0,16},{8,24},{16,0},{24,8},{1,17},{9,25},{17,1},{25,9},{2,18},{10... | collective-permute-start | bytes 786440 | tf_op jit(solution)/shard_map/ppermute | solution.py:16
  148.8 21.7 %collective-permute-start.23 = (bf16[4,32,2048]{2,1,0:T(8,128)(2,1)S(1)}, bf16[4,32,2048]{2,1,0:T(8,128)(2,1)S(1)}, u32[]{:S(2)}, u32[]{:S(2)}) collective-permute-start(bf16[4,32,2048]{2,1,0:T(8,128)(2,1)S(1)} %get-tuple-element.40), channel_id=1, source_target_pairs={{0,1},{1,0},{2,3},{3,2},{4,5},{5,4},{6,7},{7,6},{8,9},{9,8},{10,11... | collective-permute-start | bytes 1572872 | tf_op jit(solution)/shard_map/ppermute | solution.py:16
  148.9 9.2 %collective-permute-start.12 = (bf16[64,2048]{1,0:T(8,128)(2,1)S(1)}, bf16[64,2048]{1,0:T(8,128)(2,1)S(1)}, u32[]{:S(2)}, u32[]{:S(2)}) collective-permute-start(bf16[64,2048]{1,0:T(8,128)(2,1)S(1)} %fusion.3.refs_3_), channel_id=1, source_target_pairs={{0,8},{8,0},{16,24},{24,16},{1,9},{9,1},{17,25},{25,17},{2,10},{10... | collective-permute-start | bytes 786440 | tf_op jit(solution)/shard_map/ppermute | solution.py:16
  149.0 14.3 %collective-permute-start.11 = (bf16[64,2048]{1,0:T(8,128)(2,1)S(1)}, bf16[64,2048]{1,0:T(8,128)(2,1)S(1)}, u32[]{:S(2)}, u32[]{:S(2)}) collective-permute-start(bf16[64,2048]{1,0:T(8,128)(2,1)S(1)} %collective-permute-done.10.refs_1_), channel_id=1, source_target_pairs={{0,8},{8,0},{16,24},{24,16},{1,9},{9,1},{17,25},{25,17},{2,10},{10... | collective-permute-start | bytes 786440 | tf_op jit(solution)/shard_map/ppermute | solution.py:16
  170.5 3.8 %collective-permute-start.13 = (bf16[4,32,2048]{2,1,0:T(8,128)(2,1)S(1)}, bf16[4,32,2048]{2,1,0:T(8,128)(2,1)S(1)}, u32[]{:S(2)}, u32[]{:S(2)}) collective-permute-start(bf16[4,32,2048]{2,1,0:T(8,128)(2,1)S(1)} %get-tuple-element.34), channel_id=1, source_target_pairs={{0,1},{1,0},{2,3},{3,2},{4,5},{5,4},{6,7},{7,6},{8,9},{9,8},{10,11... | collective-permute-start | bytes 1572872 | tf_op jit(solution)/shard_map/ppermute | solution.py:16
  170.7 7.3 %collective-permute-start.26 = (bf16[32,2048]{1,0:T(8,128)(2,1)S(1)}, bf16[32,2048]{1,0:T(8,128)(2,1)S(1)}, u32[]{:S(2)}, u32[]{:S(2)}) collective-permute-start(bf16[32,2048]{1,0:T(8,128)(2,1)S(1)} %get-tuple-element.48), channel_id=1, source_target_pairs={{0,6},{1,7},{2,4},{3,5},{4,2},{5,3},{6,0},{7,1},{8,14},{9,15},{10,... | collective-permute-start | bytes 393224 | tf_op jit(solution)/shard_map/ppermute | solution.py:16
  172.4 8.4 %collective-permute-start.25 = (bf16[32,2048]{1,0:T(8,128)(2,1)S(1)}, bf16[32,2048]{1,0:T(8,128)(2,1)S(1)}, u32[]{:S(2)}, u32[]{:S(2)}) collective-permute-start(bf16[32,2048]{1,0:T(8,128)(2,1)S(1)} %get-tuple-element.49), channel_id=1, source_target_pairs={{0,4},{1,5},{2,6},{3,7},{4,0},{5,1},{6,2},{7,3},{8,12},{9,13},{10,... | collective-permute-start | bytes 393224 | tf_op jit(solution)/shard_map/ppermute | solution.py:16
  173.8 7.1 %collective-permute-start.24 = (bf16[32,2048]{1,0:T(8,128)(2,1)S(1)}, bf16[32,2048]{1,0:T(8,128)(2,1)S(1)}, u32[]{:S(2)}, u32[]{:S(2)}) collective-permute-start(bf16[32,2048]{1,0:T(8,128)(2,1)S(1)} %get-tuple-element.47), channel_id=1, source_target_pairs={{0,2},{1,3},{2,0},{3,1},{4,6},{5,7},{6,4},{7,5},{8,10},{9,11},{10,... | collective-permute-start | bytes 393224 | tf_op jit(solution)/shard_map/ppermute | solution.py:16
  174.5 9.2 %collective-permute-start.16 = (bf16[32,2048]{1,0:T(8,128)(2,1)S(1)}, bf16[32,2048]{1,0:T(8,128)(2,1)S(1)}, u32[]{:S(2)}, u32[]{:S(2)}) collective-permute-start(bf16[32,2048]{1,0:T(8,128)(2,1)S(1)} %get-tuple-element.45), channel_id=1, source_target_pairs={{0,6},{1,7},{2,4},{3,5},{4,2},{5,3},{6,0},{7,1},{8,14},{9,15},{10,... | collective-permute-start | bytes 393224 | tf_op jit(solution)/shard_map/ppermute | solution.py:16
  176.2 9.8 %collective-permute-start.15 = (bf16[32,2048]{1,0:T(8,128)(2,1)S(1)}, bf16[32,2048]{1,0:T(8,128)(2,1)S(1)}, u32[]{:S(2)}, u32[]{:S(2)}) collective-permute-start(bf16[32,2048]{1,0:T(8,128)(2,1)S(1)} %get-tuple-element.46), channel_id=1, source_target_pairs={{0,4},{1,5},{2,6},{3,7},{4,0},{5,1},{6,2},{7,3},{8,12},{9,13},{10,... | collective-permute-start | bytes 393224 | tf_op jit(solution)/shard_map/ppermute | solution.py:16
  178.0 8.0 %collective-permute-start.14 = (bf16[32,2048]{1,0:T(8,128)(2,1)S(1)}, bf16[32,2048]{1,0:T(8,128)(2,1)S(1)}, u32[]{:S(2)}, u32[]{:S(2)}) collective-permute-start(bf16[32,2048]{1,0:T(8,128)(2,1)S(1)} %get-tuple-element.44), channel_id=1, source_target_pairs={{0,2},{1,3},{2,0},{3,1},{4,6},{5,7},{6,4},{7,5},{8,10},{9,11},{10,... | collective-permute-start | bytes 393224 | tf_op jit(solution)/shard_map/ppermute | solution.py:16

commit v2 on v0

v2 whole, which is shorter than its diff:
```python
import functools

import jax
import jax.numpy as jnp
from jax import lax
from jax.experimental import pallas as pl
from jax.experimental.pallas import tpu as pltpu
from jax.sharding import PartitionSpec as P

BLOCK = 256
CHUNKS = 2
SCALE = 1000
VMEM_BYTES = 16 << 20
VMEM = pl.BlockSpec(memory_space=pltpu.VMEM)
SMEM = pl.BlockSpec(memory_space=pltpu.SMEM)
HBM = pl.BlockSpec(memory_space=pl.ANY)


def in_vmem(value):
    return pltpu.with_memory_space_constraint(value, pltpu.VMEM)


def in_hbm(value):
    return pltpu.with_memory_space_constraint(value, pltpu.HBM)


def new(*shape):
    return pltpu.VMEM(shape, jnp.bfloat16)


def params():
    return pltpu.CompilerParams(vmem_limit_bytes=VMEM_BYTES)


def swap(value, axis, size, mask):
    return lax.ppermute(value, axis, [(i, i ^ mask) for i in range(size)])


def add(*terms):
    return functools.reduce(lambda a, b: a + b, (t.astype(jnp.float32) for t in terms))


def masked(weight, m_ref, col, tile):
    rows, cols = weight.shape
    parts = []
    for i in range(rows // tile):
        keep = [jnp.full((1, tile), m_ref[i, col + t], jnp.int32) for t in range(cols // tile)]
        parts.append(weight[i * tile : (i + 1) * tile] * jnp.concatenate(keep, 1).astype(weight.dtype))
    return jnp.concatenate(parts)


def product(x_ref, w_ref, m_ref, start, width):
    tile = w_ref.shape[0] // m_ref.shape[0]
    weight = masked(w_ref[:, start : start + width], m_ref, start // tile, tile)
    return jnp.dot(x_ref[...], weight, preferred_element_type=jnp.float32).astype(jnp.bfloat16)


def columns(w_ref):
    width = min(BLOCK, w_ref.shape[1])
    return [(start, width) for start in range(0, w_ref.shape[1], width)]


def by_chunk(value, chunk):
    half = value.shape[0] // 2
    piece = half // CHUNKS
    return jnp.concatenate([value[b * half + chunk * piece :][:piece] for b in range(2)])


def own_kernel(s_ref, m_ref, tokens_ref, w_ref, out_ref, v_ref, x_ref, x_sem, w_sem):
    panel = w_ref.shape[0]
    start = pl.multiple_of(s_ref[0] * panel, panel)
    tokens = pltpu.make_async_copy(tokens_ref.at[:, pl.ds(start, panel)], x_ref, x_sem)
    weight = pltpu.make_async_copy(w_ref, v_ref, w_sem)
    tokens.start()
    weight.start()
    tokens.wait()
    weight.wait()
    for start, width in columns(v_ref):
        value = product(x_ref, v_ref, m_ref, start, width)
        for k in range(CHUNKS):
            out_ref[k, :, start : start + width] = by_chunk(value, k)


def own_partial(row, tokens, weight, mask):
    rows = tokens.shape[0]
    panel, cols = weight.shape
    return pl.pallas_call(
        own_kernel,
        in_specs=[SMEM, SMEM, HBM, HBM],
        out_specs=[VMEM] * 2,
        out_shape=[new(CHUNKS, rows // CHUNKS, cols), new(panel, cols)],
        scratch_shapes=[new(rows, panel), pltpu.SemaphoreType.DMA, pltpu.SemaphoreType.DMA],
        compiler_params=params(),
    )(row[None], in_hbm(mask), in_hbm(tokens), in_hbm(weight))


def others_kernel(groups, s_ref, gm_ref, um_ref, even_ref, odd_ref, gv_ref, uv_ref, *refs):
    outs, x_ref = refs[:-1], refs[-1]
    pairs, _, rows, part = even_ref.shape
    for pos in range(2 * pairs):
        from_ref = (even_ref, odd_ref)[pos // pairs]
        start = pl.multiple_of(s_ref[pos] * part, part)
        for g in range(groups):
            x_ref[g * rows : (g + 1) * rows, pl.ds(start, part)] = from_ref[pos % pairs, g]
    for which, (w_ref, m_ref) in enumerate(((gv_ref, gm_ref), (uv_ref, um_ref))):
        for start, width in columns(w_ref):
            value = product(x_ref, w_ref, m_ref, start, width)
            for g in range(groups):
                for k in range(CHUNKS):
                    outs[g * CHUNKS + k][which, :, start : start + width] = by_chunk(value[g * rows : (g + 1) * rows], k)


def others_partial(scalars, even, odd, gate_weight, up_weight, gate_mask, up_mask):
    groups, rows = even.shape[1:3]
    panel, cols = gate_weight.shape
    outs = pl.pallas_call(
        functools.partial(others_kernel, groups),
        in_specs=[SMEM, SMEM, SMEM, VMEM, VMEM, VMEM, VMEM],
        out_specs=[VMEM] * (groups * CHUNKS),
        out_shape=[new(2, rows // CHUNKS, cols)] * (groups * CHUNKS),
        scratch_shapes=[new(groups * rows, panel)],
        compiler_params=params(),
        cost_estimate=pl.CostEstimate(flops=4 * groups * rows * panel * cols // SCALE, bytes_accessed=0, transcendentals=0),
    )(scalars, in_hbm(gate_mask), in_hbm(up_mask), in_vmem(even), in_vmem(odd), in_vmem(gate_weight), in_vmem(up_weight))
    return [outs[g * CHUNKS : (g + 1) * CHUNKS] for g in range(groups)]


def load_kernel(s_ref, w_ref, v_ref, sem):
    del s_ref
    copy = pltpu.make_async_copy(w_ref, v_ref, sem)
    copy.start()
    copy.wait()


def load(weight, scalars):
    return pl.pallas_call(
        load_kernel,
        in_specs=[SMEM, HBM],
        out_specs=VMEM,
        out_shape=new(*weight.shape),
        scratch_shapes=[pltpu.SemaphoreType.DMA],
        compiler_params=params(),
    )(scalars, in_hbm(weight))


def down_kernel(n_row, s_ref, m_ref, *refs):
    h_refs, w_ref = refs[:n_row], refs[n_row]
    keep_ref, give_ref, x_ref = refs[n_row + 1 :]
    rows = h_refs[0].shape[0]
    half = rows // 2
    for d in range(n_row):
        x_ref[pl.ds(pl.multiple_of((s_ref[0] ^ d) * rows, rows), rows), :] = h_refs[d][...]
    first = s_ref[1] == 0
    for start, width in columns(w_ref):
        value = product(x_ref, w_ref, m_ref, start, width)
        for e in range(n_row):
            low, high = (value[e * rows + b * half :][:half] for b in range(2))
            keep_ref[e, :, start : start + width] = jnp.where(first, low, high)
            give_ref[e, :, start : start + width] = jnp.where(first, high, low)


def down_partial(scalars, hidden, weight, mask):
    n_row = len(hidden)
    rows, panel = hidden[0].shape
    cols = weight.shape[1]
    return pl.pallas_call(
        functools.partial(down_kernel, n_row),
        in_specs=[SMEM, SMEM] + [VMEM] * (n_row + 1),
        out_specs=[VMEM] * 2,
        out_shape=[new(n_row, rows // 2, cols)] * 2,
        scratch_shapes=[new(n_row * rows, panel)],
        compiler_params=params(),
    )(scalars, in_hbm(mask), *map(in_vmem, hidden), in_vmem(weight))


def on_device(n_row, n_col, tokens, gate_weight, up_weight, down_weight, gate_mask, up_mask, down_mask):
    assert n_col == 2 * n_row and n_row & (n_row - 1) == 0
    rows = tokens.shape[0]
    panel = gate_weight.shape[0]
    row, col = lax.axis_index("row"), lax.axis_index("col")

    slices = min(n_col, panel // BLOCK)
    part = panel // slices
    mine = []
    for d in range(1, n_row):
        start = (row ^ d) * panel + (col % slices) * part
        mine.append(lax.dynamic_slice(tokens, (0, start), (rows, part)))
    mine, row = lax.optimization_barrier((mine, row))
    mine = jnp.stack([swap(m, "row", n_row, d + 1) for d, m in enumerate(mine)])
    gate_own, gate_weight = own_partial(row, tokens, gate_weight, gate_mask)
    mine, gate_own, row = lax.optimization_barrier((mine, gate_own, row))
    up_own, up_weight = own_partial(row, tokens, up_weight, up_mask)
    even = jnp.stack([mine] + [swap(mine, "col", n_col, e) for e in range(2, slices, 2)])
    odd = swap(even, "col", n_col, 1)

    order = jnp.asarray([*range(0, slices, 2), *range(1, slices, 2)], jnp.int32)
    others = others_partial((col % slices) ^ order, even, odd, gate_weight, up_weight, gate_mask, up_mask)
    gate_came, up_came = swap(gate_own, "row", n_row, 1), swap(up_own, "row", n_row, 1)
    place = jnp.stack([(col // 2) ^ row, col % 2]).astype(jnp.int32)
    sums = []
    for k in range(CHUNKS):
        held = {d: others[d - 1][k] for d in range(1, n_row)}
        held[1] = add(jnp.stack([gate_came[k], up_came[k]]), held[1]).astype(jnp.bfloat16)
        sums.append(held)
    sums = lax.optimization_barrier(sums)
    hiddens = []
    for held in sums:
        bit = 1
        while bit < n_row:
            for d in [d for d in held if not d & bit]:
                total = add(swap(held.pop(d), "row", n_row, bit), held[d | bit])
                held[d | bit] = total.astype(jnp.bfloat16) if 2 * bit < n_row else total
            bit *= 2
        gate, up = held[n_row - 1]
        hiddens.append({n_row - 1: (jax.nn.silu(gate) * up).astype(jnp.bfloat16)})
    arrived = []
    for k, hidden in enumerate(hiddens):
        bit = n_row // 2
        for d in list(hidden):
            hidden[d ^ bit] = swap(hidden[d], "row", n_row, bit)
        near = swap(hidden[n_row - 1], "row", n_row, 1)
        hidden, near, hiddens[k + 1 :] = lax.optimization_barrier((hidden, near, hiddens[k + 1 :]))
        arrived.append(hidden[n_row // 2 - 1])
        while bit > 1:
            bit //= 2
            for d in list(hidden):
                last = bit == 1 and d == n_row - 1
                hidden[d ^ bit] = near if last else swap(hidden[d], "row", n_row, bit)
        hiddens[k] = [hidden[d] for d in range(n_row)]
    hiddens[0][-1], place = lax.optimization_barrier((hiddens[0][-1], place))
    down_weight = load(down_weight, place)
    place, _ = lax.optimization_barrier((place, arrived[-1]))

    result = []
    for hidden in hiddens:
        keep, give = down_partial(place, hidden, down_weight, down_mask)
        share = add(keep, swap(give, "col", n_col, 1)).astype(jnp.bfloat16)
        share, place = lax.optimization_barrier((share, place))
        came = [swap(share[e], "col", n_col, 2 * e) for e in range(1, n_row)]
        result.append(add(share[0], *came).astype(jnp.bfloat16))
    return jnp.concatenate(result)


def solution(mesh):
    return jax.shard_map(
        functools.partial(on_device, mesh.shape["row"], mesh.shape["col"]),
        mesh=mesh,
        in_specs=(
            P("row", None),
            P("row", "col"),
            P("row", "col"),
            P("col", "row"),
            P("row", "col"),
            P("row", "col"),
            P("col", "row"),
        ),
        out_specs=P("col", "row"),
        check_vma=False,
    )
```

time: 1130 us -> 154 us (0.14)
  waiting for transfers between devices: 683 us -> 89.5 us
  local copies, waits for them, and re-layouts: 275 us -> 1.07 us
  matrix products: 124 us -> 0 us
  Pallas kernels: 0 us -> 29.9 us
  starting transfers between devices: 0.59 us -> 30 us
  blocking collectives: 18.1 us -> 0 us
  between operations: 14.4 us -> 0.26 us
    all_gather x3 -> x0, waiting for transfers between devices: 643 us -> none  [the longest x1 370 us: on_device(): gate_piece = lax.all_gather(gate_packed, 'row', axis=0, tiled=True)]
    reshape x6 -> x0, local copies, waits for them, and re-layouts: 144 us -> none  [the longest x2 98.9 us: unpack_tiles(): return dense.reshape(groups, tile_rows * tile, tile_cols * tile)]
    dot_general x7 -> x0, matrix products: 124 us -> none  [the longest x2 61.7 us: unpack_tiles(): jnp.einsum('gcs,gsab->gcab', spread, packed, preferred_element_type=jnp.f...]
    transpose x1 -> x0, local copies, waits for them, and re-layouts: 98.3 us -> none  [unpack_tiles(): dense.reshape(groups, tile_rows, tile_cols, tile, tile)]
    ppermute x0 -> x27, waiting for transfers between devices: none -> 89.5 us  [swap(): return lax.ppermute(value, axis, [(i, i ^ mask) for i in range(size)])]
    reduce_scatter x1 -> x0, waiting for transfers between devices: 39.6 us -> none  [on_device(): lax.psum_scatter(jnp.dot(all_hidden, down_eff, preferred_element_type=jnp...]
    unnamed x21 -> x2, local copies, waits for them, and re-layouts: 31.5 us -> 0.01 us
    ppermute x0 -> x27, starting transfers between devices: none -> 30 us  [swap(): return lax.ppermute(value, axis, [(i, i ^ mask) for i in range(size)])]
  transfers between devices with their start and end apart: 4 -> 27, of which waited for: 4 -> 15; matrix products, arithmetic and copies ran while one was open for 21% -> 1% of each run, Pallas kernels for 0% -> 10%
where the time goes in v2:
time: 154 us; the launch traced here: 153 us
  waiting for transfers between devices  89.5 us (58%)
  starting transfers between devices  30 us (19%)
  Pallas kernels  29.9 us (19%)
  other arithmetic  2.59 us (2%)
    ppermute x27, waiting for transfers between devices, swap(): return lax.ppermute(value, axis, [(i, i ^ mask) for i in range(size)])  89.5 us
    ppermute x27, starting transfers between devices, swap(): return lax.ppermute(value, axis, [(i, i ^ mask) for i in range(size)])  30 us
    pallas_call x2, Pallas kernels, own_partial(): pl.pallas_call(own_kernel, in_specs=[SMEM, SMEM, HBM, HBM], out_specs=[VM...  11.4 us
    pallas_call x1, Pallas kernels, others_partial(): pl.pallas_call(functools.partial(others_kernel, groups), in_specs=[SMEM,...  7.95 us
    pallas_call x2, Pallas kernels, down_partial(): pl.pallas_call(functools.partial(down_kernel, n_row), in_specs=[SMEM, SME...  6.58 us
    pallas_call x1, Pallas kernels, load(): pl.pallas_call(load_kernel, in_specs=[SMEM, HBM], out_specs=VMEM, out_sha...  3.93 us
  transfers between devices with their start and end apart: 27, of which 15 were waited for; matrix products, arithmetic and copies ran while one was open for 1% of the time, Pallas kernels for 10%

profile of v2, /device:TPU:0, one launch (start us, length us, event | category | flops | bytes accessed | tf_op | source)
XLA Modules:
  0.0 153.3 jit_solution(17400860462361567403)
XLA Ops:
  0.0 0.9 constant_dynamic-slice_fusion
  0.9 3.1 %collective-permute-start = (bf16[128,256]{1,0:T(8,128)(2,1)S(1)}, bf16[128,256]{1,0:T(8,128)(2,1)S(1)}, u32[]{:S(2)}, u32[]{:S(2)}) collective-permute-start(bf16[128,256]{1,0:T(8,128)(2,1)S(1)} %get-tuple-element.45), channel_id=1, source_target_pairs={{0,8},{8,0},{16,24},{24,16},{1,9},{9,1},{17,25},{25,17},{2,10},{10... | collective-permute-start | bytes 196616 | tf_op jit(solution)/shard_map/ppermute | solution.py:36
  4.0 2.6 %collective-permute-start.1 = (bf16[128,256]{1,0:T(8,128)(2,1)S(1)}, bf16[128,256]{1,0:T(8,128)(2,1)S(1)}, u32[]{:S(2)}, u32[]{:S(2)}) collective-permute-start(bf16[128,256]{1,0:T(8,128)(2,1)S(1)} %get-tuple-element.46), channel_id=1, source_target_pairs={{0,16},{8,24},{16,0},{24,8},{1,17},{9,25},{17,1},{25,9},{2,18},{10... | collective-permute-start | bytes 196616 | tf_op jit(solution)/shard_map/ppermute | solution.py:36
  6.6 0.0 collective-permute-start.2
  6.6 5.7 %shard_map.82 = (bf16[2,64,2048]{2,1,0:T(8,128)(2,1)S(1)}, bf16[2048,2048]{1,0:T(8,128)(2,1)S(1)}) custom-call(s32[1]{0:T(128)} %bitcast.3.s_ref, s32[16,16]{1,0:T(8,128)} %gm_ref.1, bf16[128,8192]{1,0:T(8,128)(2,1)} %tokens_ref.3, bf16[2048,2048]{1,0:T(8,128)(2,1)} %w_ref.3), custom_call_target="tpu_custom_call" | custom-call | tf_op jit(solution)/shard_map/pallas_call | solution.py:87
  12.3 0.0 collective-permute-done.1
  12.3 0.3 collective-permute-done.2
  12.7 0.6 collective-permute-start.3
  13.4 2.4 %collective-permute-start.7 = (bf16[3,128,256]{2,1,0:T(8,128)(2,1)S(1)}, bf16[3,128,256]{2,1,0:T(8,128)(2,1)S(1)}, u32[]{:S(2)}, u32[]{:S(2)}) collective-permute-start(bf16[3,128,256]{2,1,0:T(8,128)(2,1)S(1)} %pad_maximum_fusion.2), channel_id=1, source_target_pairs={{0,6},{1,7},{2,4},{3,5},{4,2},{5,3},{6,0},{7,1},{8,14},{9,15},{10,... | collective-permute-start | bytes 589832 | tf_op jit(solution)/shard_map/ppermute | solution.py:36
  15.8 0.5 collective-permute-start.6
  16.3 0.5 collective-permute-start.5
  16.9 5.7 %shard_map.83 = (bf16[2,64,2048]{2,1,0:T(8,128)(2,1)S(1)}, bf16[2048,2048]{1,0:T(8,128)(2,1)S(1)}) custom-call(s32[1]{0:T(128)} %bitcast.4.s_ref, s32[16,16]{1,0:T(8,128)} %um_ref.1, bf16[128,8192]{1,0:T(8,128)(2,1)} %tokens_ref.3, bf16[2048,2048]{1,0:T(8,128)(2,1)} %w_ref.4), custom_call_target="tpu_custom_call" | custom-call | tf_op jit(solution)/shard_map/pallas_call | solution.py:87
  22.6 1.5 collective-permute-start.4
  24.1 0.0 collective-permute-done.7
  24.1 0.1 pad_maximum_fusion.even_ref
  24.2 0.1 collective-permute-start.8
  24.3 3.4 %collective-permute-done.3 = bf16[2,64,2048]{2,1,0:T(8,128)(2,1)S(1)} collective-permute-done((bf16[2,64,2048]{2,1,0:T(8,128)(2,1)S(1)}, bf16[2,64,2048]{2,1,0:T(8,128)(2,1)S(1)}, u32[]{:S(2)}, u32[]{:S(2)}) %collective-permute-start.3) | collective-permute-done | bytes 524320 | tf_op jit(solution)/shard_map/ppermute | solution.py:36
  27.7 9.1 %collective-permute-done.4 = bf16[2,64,2048]{2,1,0:T(8,128)(2,1)S(1)} collective-permute-done((bf16[2,64,2048]{2,1,0:T(8,128)(2,1)S(1)}, bf16[2,64,2048]{2,1,0:T(8,128)(2,1)S(1)}, u32[]{:S(2)}, u32[]{:S(2)}) %collective-permute-start.4) | collective-permute-done | bytes 524320 | tf_op jit(solution)/shard_map/ppermute | solution.py:36
  36.8 0.0 collective-permute-done.8.odd_ref
  36.9 8.0 %shard_map.84 = (bf16[2,64,2048]{2,1,0:T(8,128)(2,1)S(1)}, bf16[2,64,2048]{2,1,0:T(8,128)(2,1)S(1)}, bf16[2,64,2048]{2,1,0:T(8,128)(2,1)S(1)}, bf16[2,64,2048]{2...) custom-call(s32[8]{0:T(128)S(1)} %broadcast_xor_fusion.s_ref, ...), custom_call_target="tpu_custom_call" | custom-call | flops 6442450 | tf_op jit(solution)/shard_map/pallas_call | solution.py:116
  44.8 0.4 add_convert_fusion.4
  45.2 2.4 %collective-permute-start.9 = (bf16[2,64,2048]{2,1,0:T(8,128)(2,1)S(1)}, bf16[2,64,2048]{2,1,0:T(8,128)(2,1)S(1)}, u32[]{:S(2)}, u32[]{:S(2)}) collective-permute-start(bf16[2,64,2048]{2,1,0:T(8,128)(2,1)S(1)} %get-tuple-element.62), channel_id=1, source_target_pairs={{0,16},{8,24},{16,0},{24,8},{1,17},{9,25},{17,1},{25,9},{2,18},{10... | collective-permute-start | bytes 1572872 | tf_op jit(solution)/shard_map/ppermute | solution.py:36
  47.6 1.7 %collective-permute-start.10 = (bf16[2,64,2048]{2,1,0:T(8,128)(2,1)S(1)}, bf16[2,64,2048]{2,1,0:T(8,128)(2,1)S(1)}, u32[]{:S(2)}, u32[]{:S(2)}) collective-permute-start(bf16[2,64,2048]{2,1,0:T(8,128)(2,1)S(1)} %get-tuple-element.63), channel_id=1, source_target_pairs={{0,8},{8,0},{16,24},{24,16},{1,9},{9,1},{17,25},{25,17},{2,10},{10... | collective-permute-start | bytes 1572872 | tf_op jit(solution)/shard_map/ppermute | solution.py:36
  49.4 0.1 collective-permute-start.13
  49.5 0.8 collective-permute-start.14
  50.2 28.9 %collective-permute-done.9 = bf16[2,64,2048]{2,1,0:T(8,128)(2,1)S(1)} collective-permute-done((bf16[2,64,2048]{2,1,0:T(8,128)(2,1)S(1)}, bf16[2,64,2048]{2,1,0:T(8,128)(2,1)S(1)}, u32[]{:S(2)}, u32[]{:S(2)}) %collective-permute-start.9) | collective-permute-done | bytes 524320 | tf_op jit(solution)/shard_map/ppermute | solution.py:36
  79.1 0.2 convert_add_fusion.1
  79.3 0.1 fusion.3.refs_3_
  79.5 0.1 collective-permute-start.12
  79.6 0.1 collective-permute-start.11
  79.7 13.3 %collective-permute-done.13 = bf16[2,64,2048]{2,1,0:T(8,128)(2,1)S(1)} collective-permute-done((bf16[2,64,2048]{2,1,0:T(8,128)(2,1)S(1)}, bf16[2,64,2048]{2,1,0:T(8,128)(2,1)S(1)}, u32[]{:S(2)}, u32[]{:S(2)}) %collective-permute-start.13) | collective-permute-done | bytes 524320 | tf_op jit(solution)/shard_map/ppermute | solution.py:36
  93.0 7.6 %collective-permute-done.14 = bf16[2,64,2048]{2,1,0:T(8,128)(2,1)S(1)} collective-permute-done((bf16[2,64,2048]{2,1,0:T(8,128)(2,1)S(1)}, bf16[2,64,2048]{2,1,0:T(8,128)(2,1)S(1)}, u32[]{:S(2)}, u32[]{:S(2)}) %collective-permute-start.14) | collective-permute-done | bytes 524320 | tf_op jit(solution)/shard_map/ppermute | solution.py:36
  100.6 0.2 convert_add_fusion
  100.8 0.1 fusion.1.refs_3_
  100.9 2.7 %collective-permute-done.12.refs_2_ = bf16[64,2048]{1,0:T(8,128)(2,1)S(1)} collective-permute-done((bf16[64,2048]{1,0:T(8,128)(2,1)S(1)}, bf16[64,2048]{1,0:T(8,128)(2,1)S(1)}, u32[]{:S(2)}, u32[]{:S(2)}) %collective-permute-start.12) | collective-permute-done | bytes 262176 | tf_op jit(solution)/shard_map/ppermute | solution.py:36
  103.6 0.9 collective-permute-start.16
  104.6 1.7 %collective-permute-start.15 = (bf16[64,2048]{1,0:T(8,128)(2,1)S(1)}, bf16[64,2048]{1,0:T(8,128)(2,1)S(1)}, u32[]{:S(2)}, u32[]{:S(2)}) collective-permute-start(bf16[64,2048]{1,0:T(8,128)(2,1)S(1)} %fusion.1.refs_3_), channel_id=1, source_target_pairs={{0,16},{8,24},{16,0},{24,8},{1,17},{9,25},{17,1},{25,9},{2,18},{10... | collective-permute-start | bytes 786440 | tf_op jit(solution)/shard_map/ppermute | solution.py:36
  106.3 1.5 collective-permute-start.17
  107.8 0.1 pad_add_fusion.s_ref
  107.9 3.9 %shard_map.85.refs_4_ = bf16[2048,2048]{1,0:T(8,128)(2,1)S(1)} custom-call(s32[2]{0:T(128)S(1)} %pad_add_fusion.s_ref, bf16[2048,2048]{1,0:T(8,128)(2,1)} %w_ref.5), custom_call_target="tpu_custom_call" | custom-call | tf_op jit(solution)/shard_map/pallas_call | solution.py:136
  111.8 4.8 %collective-permute-done.16.refs_2_ = bf16[64,2048]{1,0:T(8,128)(2,1)S(1)} collective-permute-done((bf16[64,2048]{1,0:T(8,128)(2,1)S(1)}, bf16[64,2048]{1,0:T(8,128)(2,1)S(1)}, u32[]{:S(2)}, u32[]{:S(2)}) %collective-permute-start.16) | collective-permute-done | bytes 262176 | tf_op jit(solution)/shard_map/ppermute | solution.py:36
  116.7 3.6 %collective-permute-done.17.refs_0_ = bf16[64,2048]{1,0:T(8,128)(2,1)S(1)} collective-permute-done((bf16[64,2048]{1,0:T(8,128)(2,1)S(1)}, bf16[64,2048]{1,0:T(8,128)(2,1)S(1)}, u32[]{:S(2)}, u32[]{:S(2)}) %collective-permute-start.17) | collective-permute-done | bytes 262176 | tf_op jit(solution)/shard_map/ppermute | solution.py:36
  120.2 3.3 %shard_map.86 = (bf16[4,32,2048]{2,1,0:T(8,128)(2,1)S(1)}, bf16[4,32,2048]{2,1,0:T(8,128)(2,1)S(1)}) custom-call(s32[2]{0:T(128)S(1)} %pad_add_fusion.s_ref, s32[16,16]{1,0:T(8,128)} %m_ref.7, bf16[64,2048]{1,0:T(8,128)(2,1)S(1)} %collective-permute-done.17.refs_0_, bf16[64,2048]{1,0:T(8,128)(2,1)S(1)} %collective-permute-done.11.refs_1_, ...), custom_call_target="tpu_custom_call" | custom-call | tf_op jit(solution)/shard_map/pallas_call | solution.py:166
  123.5 0.1 collective-permute-start.18
  123.6 1.5 collective-permute-start.22
  125.1 0.4 collective-permute-done.18
  125.5 0.3 add_convert_fusion.1
  125.8 6.5 %collective-permute-done.22.refs_0_ = bf16[64,2048]{1,0:T(8,128)(2,1)S(1)} collective-permute-done((bf16[64,2048]{1,0:T(8,128)(2,1)S(1)}, bf16[64,2048]{1,0:T(8,128)(2,1)S(1)}, u32[]{:S(2)}, u32[]{:S(2)}) %collective-permute-start.22) | collective-permute-done | bytes 262176 | tf_op jit(solution)/shard_map/ppermute | solution.py:36
  132.3 3.3 %shard_map.87 = (bf16[4,32,2048]{2,1,0:T(8,128)(2,1)S(1)}, bf16[4,32,2048]{2,1,0:T(8,128)(2,1)S(1)}) custom-call(s32[2]{0:T(128)S(1)} %pad_add_fusion.s_ref, s32[16,16]{1,0:T(8,128)} %m_ref.7, bf16[64,2048]{1,0:T(8,128)(2,1)S(1)} %collective-permute-done.22.refs_0_, bf16[64,2048]{1,0:T(8,128)(2,1)S(1)} %collective-permute-done.15.refs_1_, ...), custom_call_target="tpu_custom_call" | custom-call | tf_op jit(solution)/shard_map/pallas_call | solution.py:166
  135.6 0.1 collective-permute-start.23
  135.7 1.6 %collective-permute-start.19 = (bf16[32,2048]{1,0:T(8,128)(2,1)S(1)}, bf16[32,2048]{1,0:T(8,128)(2,1)S(1)}, u32[]{:S(2)}, u32[]{:S(2)}) collective-permute-start(bf16[32,2048]{1,0:T(8,128)(2,1)S(1)} %get-tuple-element.88), channel_id=1, source_target_pairs={{0,2},{1,3},{2,0},{3,1},{4,6},{5,7},{6,4},{7,5},{8,10},{9,11},{10,... | collective-permute-start | bytes 393224 | tf_op jit(solution)/shard_map/ppermute | solution.py:36
  137.3 1.5 collective-permute-start.21
  138.8 0.5 collective-permute-start.20
  139.3 0.1 add_convert_fusion
  139.5 1.6 %collective-permute-start.24 = (bf16[32,2048]{1,0:T(8,128)(2,1)S(1)}, bf16[32,2048]{1,0:T(8,128)(2,1)S(1)}, u32[]{:S(2)}, u32[]{:S(2)}) collective-permute-start(bf16[32,2048]{1,0:T(8,128)(2,1)S(1)} %get-tuple-element.91), channel_id=1, source_target_pairs={{0,2},{1,3},{2,0},{3,1},{4,6},{5,7},{6,4},{7,5},{8,10},{9,11},{10,... | collective-permute-start | bytes 393224 | tf_op jit(solution)/shard_map/ppermute | solution.py:36
  141.0 1.5 collective-permute-start.26
  142.5 1.1 collective-permute-start.25
  143.6 2.3 %collective-permute-done.21 = bf16[32,2048]{1,0:T(8,128)(2,1)S(1)} collective-permute-done((bf16[32,2048]{1,0:T(8,128)(2,1)S(1)}, bf16[32,2048]{1,0:T(8,128)(2,1)S(1)}, u32[]{:S(2)}, u32[]{:S(2)}) %collective-permute-start.21) | collective-permute-done | bytes 131104 | tf_op jit(solution)/shard_map/ppermute | solution.py:36
  145.9 2.0 %collective-permute-done.20 = bf16[32,2048]{1,0:T(8,128)(2,1)S(1)} collective-permute-done((bf16[32,2048]{1,0:T(8,128)(2,1)S(1)}, bf16[32,2048]{1,0:T(8,128)(2,1)S(1)}, u32[]{:S(2)}, u32[]{:S(2)}) %collective-permute-start.20) | collective-permute-done | bytes 131104 | tf_op jit(solution)/shard_map/ppermute | solution.py:36
  147.9 0.1 fusion.9
  148.0 3.2 %collective-permute-done.26 = bf16[32,2048]{1,0:T(8,128)(2,1)S(1)} collective-permute-done((bf16[32,2048]{1,0:T(8,128)(2,1)S(1)}, bf16[32,2048]{1,0:T(8,128)(2,1)S(1)}, u32[]{:S(2)}, u32[]{:S(2)}) %collective-permute-start.26) | collective-permute-done | bytes 131104 | tf_op jit(solution)/shard_map/ppermute | solution.py:36
  151.2 1.3 collective-permute-done.25
  152.5 0.1 fusion.6
  152.6 0.7 pad_maximum_fusion.1
  (17 shorter events, 0.2 us)
Async XLA Ops:
  0.0 16.8 %copy-start = (s32[8]{0:T(128)S(1)}, s32[8]{0:T(128)}, u32[]{:S(2)}) copy-start(s32[8]{0:T(128)} %constant.64.clone) | copy-start | bytes 100
  0.9 11.4 %collective-permute-start = (bf16[128,256]{1,0:T(8,128)(2,1)S(1)}, bf16[128,256]{1,0:T(8,128)(2,1)S(1)}, u32[]{:S(2)}, u32[]{:S(2)}) collective-permute-start(bf16[128,256]{1,0:T(8,128)(2,1)S(1)} %get-tuple-element.45), channel_id=1, source_target_pairs={{0,8},{8,0},{16,24},{24,16},{1,9},{9,1},{17,25},{25,17},{2,10},{10... | collective-permute-start | bytes 196616 | tf_op jit(solution)/shard_map/ppermute | solution.py:36
  4.0 8.3 %collective-permute-start.1 = (bf16[128,256]{1,0:T(8,128)(2,1)S(1)}, bf16[128,256]{1,0:T(8,128)(2,1)S(1)}, u32[]{:S(2)}, u32[]{:S(2)}) collective-permute-start(bf16[128,256]{1,0:T(8,128)(2,1)S(1)} %get-tuple-element.46), channel_id=1, source_target_pairs={{0,16},{8,24},{16,0},{24,8},{1,17},{9,25},{17,1},{25,9},{2,18},{10... | collective-permute-start | bytes 196616 | tf_op jit(solution)/shard_map/ppermute | solution.py:36
  6.6 6.1 %collective-permute-start.2 = (bf16[128,256]{1,0:T(8,128)(2,1)S(1)}, bf16[128,256]{1,0:T(8,128)(2,1)S(1)}, u32[]{:S(2)}, u32[]{:S(2)}) collective-permute-start(bf16[128,256]{1,0:T(8,128)(2,1)S(1)} %get-tuple-element.47), channel_id=1, source_target_pairs={{0,24},{8,16},{16,8},{24,0},{1,25},{9,17},{17,9},{25,1},{2,26},{10... | collective-permute-start | bytes 196616 | tf_op jit(solution)/shard_map/ppermute | solution.py:36
  12.7 14.9 %collective-permute-start.3 = (bf16[2,64,2048]{2,1,0:T(8,128)(2,1)S(1)}, bf16[2,64,2048]{2,1,0:T(8,128)(2,1)S(1)}, u32[]{:S(2)}, u32[]{:S(2)}) collective-permute-start(bf16[2,64,2048]{2,1,0:T(8,128)(2,1)S(1)} %get-tuple-element.50), channel_id=1, source_target_pairs={{0,8},{8,0},{16,24},{24,16},{1,9},{9,1},{17,25},{25,17},{2,10},{10... | collective-permute-start | bytes 1572872 | tf_op jit(solution)/shard_map/ppermute | solution.py:36
  13.4 10.7 %collective-permute-start.7 = (bf16[3,128,256]{2,1,0:T(8,128)(2,1)S(1)}, bf16[3,128,256]{2,1,0:T(8,128)(2,1)S(1)}, u32[]{:S(2)}, u32[]{:S(2)}) collective-permute-start(bf16[3,128,256]{2,1,0:T(8,128)(2,1)S(1)} %pad_maximum_fusion.2), channel_id=1, source_target_pairs={{0,6},{1,7},{2,4},{3,5},{4,2},{5,3},{6,0},{7,1},{8,14},{9,15},{10,... | collective-permute-start | bytes 589832 | tf_op jit(solution)/shard_map/ppermute | solution.py:36
  15.8 8.3 %collective-permute-start.6 = (bf16[3,128,256]{2,1,0:T(8,128)(2,1)S(1)}, bf16[3,128,256]{2,1,0:T(8,128)(2,1)S(1)}, u32[]{:S(2)}, u32[]{:S(2)}) collective-permute-start(bf16[3,128,256]{2,1,0:T(8,128)(2,1)S(1)} %pad_maximum_fusion.2), channel_id=1, source_target_pairs={{0,4},{1,5},{2,6},{3,7},{4,0},{5,1},{6,2},{7,3},{8,12},{9,13},{10,... | collective-permute-start | bytes 589832 | tf_op jit(solution)/shard_map/ppermute | solution.py:36
  16.3 7.8 %collective-permute-start.5 = (bf16[3,128,256]{2,1,0:T(8,128)(2,1)S(1)}, bf16[3,128,256]{2,1,0:T(8,128)(2,1)S(1)}, u32[]{:S(2)}, u32[]{:S(2)}) collective-permute-start(bf16[3,128,256]{2,1,0:T(8,128)(2,1)S(1)} %pad_maximum_fusion.2), channel_id=1, source_target_pairs={{0,2},{1,3},{2,0},{3,1},{4,6},{5,7},{6,4},{7,5},{8,10},{9,11},{10,... | collective-permute-start | bytes 589832 | tf_op jit(solution)/shard_map/ppermute | solution.py:36
  22.6 14.2 %collective-permute-start.4 = (bf16[2,64,2048]{2,1,0:T(8,128)(2,1)S(1)}, bf16[2,64,2048]{2,1,0:T(8,128)(2,1)S(1)}, u32[]{:S(2)}, u32[]{:S(2)}) collective-permute-start(bf16[2,64,2048]{2,1,0:T(8,128)(2,1)S(1)} %get-tuple-element.52), channel_id=1, source_target_pairs={{0,8},{8,0},{16,24},{24,16},{1,9},{9,1},{17,25},{25,17},{2,10},{10... | collective-permute-start | bytes 1572872 | tf_op jit(solution)/shard_map/ppermute | solution.py:36
  24.2 12.6 %collective-permute-start.8 = (bf16[4,3,128,256]{3,2,1,0:T(8,128)(2,1)S(1)}, bf16[4,3,128,256]{3,2,1,0:T(8,128)(2,1)S(1)}, u32[]{:S(2)}, u32[]{:S(2)}) collective-permute-start(bf16[4,3,128,256]{3,2,1,0:T(8,128)(2,1)S(1)} %pad_maximum_fusion.even_ref), channel_id=1, source_target_pairs={{0,1},{1,0},{2,3},{3,2},{4,5},{5,4},{6,7},{7,6},{8,9},{9,8},{10,11... | collective-permute-start | bytes 2359304 | tf_op jit(solution)/shard_map/ppermute | solution.py:36
  45.2 33.9 %collective-permute-start.9 = (bf16[2,64,2048]{2,1,0:T(8,128)(2,1)S(1)}, bf16[2,64,2048]{2,1,0:T(8,128)(2,1)S(1)}, u32[]{:S(2)}, u32[]{:S(2)}) collective-permute-start(bf16[2,64,2048]{2,1,0:T(8,128)(2,1)S(1)} %get-tuple-element.62), channel_id=1, source_target_pairs={{0,16},{8,24},{16,0},{24,8},{1,17},{9,25},{17,1},{25,9},{2,18},{10... | collective-permute-start | bytes 1572872 | tf_op jit(solution)/shard_map/ppermute | solution.py:36
  47.6 31.5 %collective-permute-start.10 = (bf16[2,64,2048]{2,1,0:T(8,128)(2,1)S(1)}, bf16[2,64,2048]{2,1,0:T(8,128)(2,1)S(1)}, u32[]{:S(2)}, u32[]{:S(2)}) collective-permute-start(bf16[2,64,2048]{2,1,0:T(8,128)(2,1)S(1)} %get-tuple-element.63), channel_id=1, source_target_pairs={{0,8},{8,0},{16,24},{24,16},{1,9},{9,1},{17,25},{25,17},{2,10},{10... | collective-permute-start | bytes 1572872 | tf_op jit(solution)/shard_map/ppermute | solution.py:36
  49.4 43.6 %collective-permute-start.13 = (bf16[2,64,2048]{2,1,0:T(8,128)(2,1)S(1)}, bf16[2,64,2048]{2,1,0:T(8,128)(2,1)S(1)}, u32[]{:S(2)}, u32[]{:S(2)}) collective-permute-start(bf16[2,64,2048]{2,1,0:T(8,128)(2,1)S(1)} %get-tuple-element.65), channel_id=1, source_target_pairs={{0,16},{8,24},{16,0},{24,8},{1,17},{9,25},{17,1},{25,9},{2,18},{10... | collective-permute-start | bytes 1572872 | tf_op jit(solution)/shard_map/ppermute | solution.py:36
  49.5 51.1 %collective-permute-start.14 = (bf16[2,64,2048]{2,1,0:T(8,128)(2,1)S(1)}, bf16[2,64,2048]{2,1,0:T(8,128)(2,1)S(1)}, u32[]{:S(2)}, u32[]{:S(2)}) collective-permute-start(bf16[2,64,2048]{2,1,0:T(8,128)(2,1)S(1)} %get-tuple-element.66), channel_id=1, source_target_pairs={{0,8},{8,0},{16,24},{24,16},{1,9},{9,1},{17,25},{25,17},{2,10},{10... | collective-permute-start | bytes 1572872 | tf_op jit(solution)/shard_map/ppermute | solution.py:36
  79.5 24.1 %collective-permute-start.12 = (bf16[64,2048]{1,0:T(8,128)(2,1)S(1)}, bf16[64,2048]{1,0:T(8,128)(2,1)S(1)}, u32[]{:S(2)}, u32[]{:S(2)}) collective-permute-start(bf16[64,2048]{1,0:T(8,128)(2,1)S(1)} %fusion.3.refs_3_), channel_id=1, source_target_pairs={{0,8},{8,0},{16,24},{24,16},{1,9},{9,1},{17,25},{25,17},{2,10},{10... | collective-permute-start | bytes 786440 | tf_op jit(solution)/shard_map/ppermute | solution.py:36
  79.6 24.0 %collective-permute-start.11 = (bf16[64,2048]{1,0:T(8,128)(2,1)S(1)}, bf16[64,2048]{1,0:T(8,128)(2,1)S(1)}, u32[]{:S(2)}, u32[]{:S(2)}) collective-permute-start(bf16[64,2048]{1,0:T(8,128)(2,1)S(1)} %fusion.3.refs_3_), channel_id=1, source_target_pairs={{0,16},{8,24},{16,0},{24,8},{1,17},{9,25},{17,1},{25,9},{2,18},{10... | collective-permute-start | bytes 786440 | tf_op jit(solution)/shard_map/ppermute | solution.py:36
  103.6 13.0 %collective-permute-start.16 = (bf16[64,2048]{1,0:T(8,128)(2,1)S(1)}, bf16[64,2048]{1,0:T(8,128)(2,1)S(1)}, u32[]{:S(2)}, u32[]{:S(2)}) collective-permute-start(bf16[64,2048]{1,0:T(8,128)(2,1)S(1)} %fusion.1.refs_3_), channel_id=1, source_target_pairs={{0,8},{8,0},{16,24},{24,16},{1,9},{9,1},{17,25},{25,17},{2,10},{10... | collective-permute-start | bytes 786440 | tf_op jit(solution)/shard_map/ppermute | solution.py:36
  104.6 12.1 %collective-permute-start.15 = (bf16[64,2048]{1,0:T(8,128)(2,1)S(1)}, bf16[64,2048]{1,0:T(8,128)(2,1)S(1)}, u32[]{:S(2)}, u32[]{:S(2)}) collective-permute-start(bf16[64,2048]{1,0:T(8,128)(2,1)S(1)} %fusion.1.refs_3_), channel_id=1, source_target_pairs={{0,16},{8,24},{16,0},{24,8},{1,17},{9,25},{17,1},{25,9},{2,18},{10... | collective-permute-start | bytes 786440 | tf_op jit(solution)/shard_map/ppermute | solution.py:36
  106.3 13.9 %collective-permute-start.17 = (bf16[64,2048]{1,0:T(8,128)(2,1)S(1)}, bf16[64,2048]{1,0:T(8,128)(2,1)S(1)}, u32[]{:S(2)}, u32[]{:S(2)}) collective-permute-start(bf16[64,2048]{1,0:T(8,128)(2,1)S(1)} %collective-permute-done.11.refs_1_), channel_id=1, source_target_pairs={{0,8},{8,0},{16,24},{24,16},{1,9},{9,1},{17,25},{25,17},{2,10},{10... | collective-permute-start | bytes 786440 | tf_op jit(solution)/shard_map/ppermute | solution.py:36
  123.5 2.0 %collective-permute-start.18 = (bf16[4,32,2048]{2,1,0:T(8,128)(2,1)S(1)}, bf16[4,32,2048]{2,1,0:T(8,128)(2,1)S(1)}, u32[]{:S(2)}, u32[]{:S(2)}) collective-permute-start(bf16[4,32,2048]{2,1,0:T(8,128)(2,1)S(1)} %get-tuple-element.77), channel_id=1, source_target_pairs={{0,1},{1,0},{2,3},{3,2},{4,5},{5,4},{6,7},{7,6},{8,9},{9,8},{10,11... | collective-permute-start | bytes 1572872 | tf_op jit(solution)/shard_map/ppermute | solution.py:36
  123.6 8.7 %collective-permute-start.22 = (bf16[64,2048]{1,0:T(8,128)(2,1)S(1)}, bf16[64,2048]{1,0:T(8,128)(2,1)S(1)}, u32[]{:S(2)}, u32[]{:S(2)}) collective-permute-start(bf16[64,2048]{1,0:T(8,128)(2,1)S(1)} %collective-permute-done.15.refs_1_), channel_id=1, source_target_pairs={{0,8},{8,0},{16,24},{24,16},{1,9},{9,1},{17,25},{25,17},{2,10},{10... | collective-permute-start | bytes 786440 | tf_op jit(solution)/shard_map/ppermute | solution.py:36
  135.6 3.7 %collective-permute-start.23 = (bf16[4,32,2048]{2,1,0:T(8,128)(2,1)S(1)}, bf16[4,32,2048]{2,1,0:T(8,128)(2,1)S(1)}, u32[]{:S(2)}, u32[]{:S(2)}) collective-permute-start(bf16[4,32,2048]{2,1,0:T(8,128)(2,1)S(1)} %get-tuple-element.83), channel_id=1, source_target_pairs={{0,1},{1,0},{2,3},{3,2},{4,5},{5,4},{6,7},{7,6},{8,9},{9,8},{10,11... | collective-permute-start | bytes 1572872 | tf_op jit(solution)/shard_map/ppermute | solution.py:36
  135.7 6.8 %collective-permute-start.19 = (bf16[32,2048]{1,0:T(8,128)(2,1)S(1)}, bf16[32,2048]{1,0:T(8,128)(2,1)S(1)}, u32[]{:S(2)}, u32[]{:S(2)}) collective-permute-start(bf16[32,2048]{1,0:T(8,128)(2,1)S(1)} %get-tuple-element.88), channel_id=1, source_target_pairs={{0,2},{1,3},{2,0},{3,1},{4,6},{5,7},{6,4},{7,5},{8,10},{9,11},{10,... | collective-permute-start | bytes 393224 | tf_op jit(solution)/shard_map/ppermute | solution.py:36
  137.3 8.6 %collective-permute-start.21 = (bf16[32,2048]{1,0:T(8,128)(2,1)S(1)}, bf16[32,2048]{1,0:T(8,128)(2,1)S(1)}, u32[]{:S(2)}, u32[]{:S(2)}) collective-permute-start(bf16[32,2048]{1,0:T(8,128)(2,1)S(1)} %get-tuple-element.89), channel_id=1, source_target_pairs={{0,6},{1,7},{2,4},{3,5},{4,2},{5,3},{6,0},{7,1},{8,14},{9,15},{10,... | collective-permute-start | bytes 393224 | tf_op jit(solution)/shard_map/ppermute | solution.py:36
  138.8 9.1 %collective-permute-start.20 = (bf16[32,2048]{1,0:T(8,128)(2,1)S(1)}, bf16[32,2048]{1,0:T(8,128)(2,1)S(1)}, u32[]{:S(2)}, u32[]{:S(2)}) collective-permute-start(bf16[32,2048]{1,0:T(8,128)(2,1)S(1)} %get-tuple-element.90), channel_id=1, source_target_pairs={{0,4},{1,5},{2,6},{3,7},{4,0},{5,1},{6,2},{7,3},{8,12},{9,13},{10,... | collective-permute-start | bytes 393224 | tf_op jit(solution)/shard_map/ppermute | solution.py:36
  139.5 8.5 %collective-permute-start.24 = (bf16[32,2048]{1,0:T(8,128)(2,1)S(1)}, bf16[32,2048]{1,0:T(8,128)(2,1)S(1)}, u32[]{:S(2)}, u32[]{:S(2)}) collective-permute-start(bf16[32,2048]{1,0:T(8,128)(2,1)S(1)} %get-tuple-element.91), channel_id=1, source_target_pairs={{0,2},{1,3},{2,0},{3,1},{4,6},{5,7},{6,4},{7,5},{8,10},{9,11},{10,... | collective-permute-start | bytes 393224 | tf_op jit(solution)/shard_map/ppermute | solution.py:36
  141.0 10.2 %collective-permute-start.26 = (bf16[32,2048]{1,0:T(8,128)(2,1)S(1)}, bf16[32,2048]{1,0:T(8,128)(2,1)S(1)}, u32[]{:S(2)}, u32[]{:S(2)}) collective-permute-start(bf16[32,2048]{1,0:T(8,128)(2,1)S(1)} %get-tuple-element.92), channel_id=1, source_target_pairs={{0,6},{1,7},{2,4},{3,5},{4,2},{5,3},{6,0},{7,1},{8,14},{9,15},{10,... | collective-permute-start | bytes 393224 | tf_op jit(solution)/shard_map/ppermute | solution.py:36
  142.5 10.0 %collective-permute-start.25 = (bf16[32,2048]{1,0:T(8,128)(2,1)S(1)}, bf16[32,2048]{1,0:T(8,128)(2,1)S(1)}, u32[]{:S(2)}, u32[]{:S(2)}) collective-permute-start(bf16[32,2048]{1,0:T(8,128)(2,1)S(1)} %get-tuple-element.93), channel_id=1, source_target_pairs={{0,4},{1,5},{2,6},{3,7},{4,0},{5,1},{6,2},{7,3},{8,12},{9,13},{10,... | collective-permute-start | bytes 393224 | tf_op jit(solution)/shard_map/ppermute | solution.py:36

commit v3 on v2

--- a/solution.py
+++ b/solution.py
@@ -8,8 +8,8 @@
 from jax.sharding import PartitionSpec as P
 
 BLOCK = 256
-CHUNKS = 2
-SCALE = 1000
+PARTS = (1, 1)
+WEIGHT = 2.0
 VMEM_BYTES = 16 << 20
 VMEM = pl.BlockSpec(memory_space=pltpu.VMEM)
 SMEM = pl.BlockSpec(memory_space=pltpu.SMEM)
@@ -60,38 +60,50 @@
     return [(start, width) for start in range(0, w_ref.shape[1], width)]
 
 
+def chunk_rows(rows):
+    unit = rows // 2 // sum(PARTS)
+    return [(sum(PARTS[:k]) * unit, n * unit) for k, n in enumerate(PARTS)]
+
+
 def by_chunk(value, chunk):
     half = value.shape[0] // 2
-    piece = half // CHUNKS
-    return jnp.concatenate([value[b * half + chunk * piece :][:piece] for b in range(2)])
-
-
-def own_kernel(s_ref, m_ref, tokens_ref, w_ref, out_ref, v_ref, x_ref, x_sem, w_sem):
-    panel = w_ref.shape[0]
+    start, length = chunk_rows(2 * half)[chunk]
+    return jnp.concatenate([value[b * half + start :][:length] for b in range(2)])
+
+
+def partial_outs(rows, cols):
+    return [new(2, 2 * length, cols) for _, length in chunk_rows(rows)]
+
+
+def own_kernel(s_ref, gm_ref, um_ref, tokens_ref, gw_ref, uw_ref, *refs):
+    *outs, gv_ref, uv_ref, x_ref, x_sem, w_sem = refs
+    panel = gw_ref.shape[0]
     start = pl.multiple_of(s_ref[0] * panel, panel)
     tokens = pltpu.make_async_copy(tokens_ref.at[:, pl.ds(start, panel)], x_ref, x_sem)
-    weight = pltpu.make_async_copy(w_ref, v_ref, w_sem)
-    tokens.start()
-    weight.start()
+    weights = [pltpu.make_async_copy(gw_ref, gv_ref, w_sem.at[0]), pltpu.make_async_copy(uw_ref, uv_ref, w_sem.at[1])]
+    for copy in (tokens, *weights):
+        copy.start()
     tokens.wait()
-    weight.wait()
-    for start, width in columns(v_ref):
-        value = product(x_ref, v_ref, m_ref, start, width)
-        for k in range(CHUNKS):
-            out_ref[k, :, start : start + width] = by_chunk(value, k)
-
-
-def own_partial(row, tokens, weight, mask):
+    for which, (w_ref, m_ref) in enumerate(((gv_ref, gm_ref), (uv_ref, um_ref))):
+        weights[which].wait()
+        for start, width in columns(w_ref):
+            value = product(x_ref, w_ref, m_ref, start, width)
+            for k in range(len(PARTS)):
+                outs[k][which, :, start : start + width] = by_chunk(value, k)
+
+
+def own_partial(row, tokens, gate_weight, up_weight, gate_mask, up_mask):
     rows = tokens.shape[0]
-    panel, cols = weight.shape
-    return pl.pallas_call(
+    panel, cols = gate_weight.shape
+    *outs, gate_weight, up_weight = pl.pallas_call(
         own_kernel,
-        in_specs=[SMEM, SMEM, HBM, HBM],
-        out_specs=[VMEM] * 2,
-        out_shape=[new(CHUNKS, rows // CHUNKS, cols), new(panel, cols)],
-        scratch_shapes=[new(rows, panel), pltpu.SemaphoreType.DMA, pltpu.SemaphoreType.DMA],
-        compiler_params=params(),
-    )(row[None], in_hbm(mask), in_hbm(tokens), in_hbm(weight))
+        in_specs=[SMEM, SMEM, SMEM, HBM, HBM, HBM],
+        out_specs=[VMEM] * (len(PARTS) + 2),
+        out_shape=partial_outs(rows, cols) + [new(panel, cols)] * 2,
+        scratch_shapes=[new(rows, panel), pltpu.SemaphoreType.DMA, pltpu.SemaphoreType.DMA((2,))],
+        compiler_params=params(),
+    )(row[None], in_hbm(gate_mask), in_hbm(up_mask), in_hbm(tokens), in_hbm(gate_weight), in_hbm(up_weight))
+    return outs, gate_weight, up_weight
 
 
 def others_kernel(groups, s_ref, gm_ref, um_ref, even_ref, odd_ref, gv_ref, uv_ref, *refs):
@@ -106,8 +118,8 @@
         for start, width in columns(w_ref):
             value = product(x_ref, w_ref, m_ref, start, width)
             for g in range(groups):
-                for k in range(CHUNKS):
-                    outs[g * CHUNKS + k][which, :, start : start + width] = by_chunk(value[g * rows : (g + 1) * rows], k)
+                for k in range(len(PARTS)):
+                    outs[g * len(PARTS) + k][which, :, start : start + width] = by_chunk(value[g * rows : (g + 1) * rows], k)
 
 
 def others_partial(scalars, even, odd, gate_weight, up_weight, gate_mask, up_mask):
@@ -116,13 +128,12 @@
     outs = pl.pallas_call(
         functools.partial(others_kernel, groups),
         in_specs=[SMEM, SMEM, SMEM, VMEM, VMEM, VMEM, VMEM],
-        out_specs=[VMEM] * (groups * CHUNKS),
-        out_shape=[new(2, rows // CHUNKS, cols)] * (groups * CHUNKS),
+        out_specs=[VMEM] * (groups * len(PARTS)),
+        out_shape=partial_outs(rows, cols) * groups,
         scratch_shapes=[new(groups * rows, panel)],
         compiler_params=params(),
-        cost_estimate=pl.CostEstimate(flops=4 * groups * rows * panel * cols // SCALE, bytes_accessed=0, transcendentals=0),
     )(scalars, in_hbm(gate_mask), in_hbm(up_mask), in_vmem(even), in_vmem(odd), in_vmem(gate_weight), in_vmem(up_weight))
-    return [outs[g * CHUNKS : (g + 1) * CHUNKS] for g in range(groups)]
+    return [outs[g * len(PARTS) : (g + 1) * len(PARTS)] for g in range(groups)]
 
 
 def load_kernel(s_ref, w_ref, v_ref, sem):
@@ -170,7 +181,23 @@
         out_shape=[new(n_row, rows // 2, cols)] * 2,
         scratch_shapes=[new(n_row * rows, panel)],
         compiler_params=params(),
+        cost_estimate=pl.CostEstimate(flops=0, bytes_accessed=0, transcendentals=0),
     )(scalars, in_hbm(mask), *map(in_vmem, hidden), in_vmem(weight))
+
+
+def join_kernel(a_ref, b_ref, o_ref):
+    o_ref[...] = a_ref[...].astype(jnp.float32) + b_ref[...].astype(jnp.float32)
+
+
+def join(a, b):
+    return pl.pallas_call(
+        join_kernel,
+        in_specs=[VMEM] * 2,
+        out_specs=VMEM,
+        out_shape=pltpu.VMEM(a.shape, jnp.float32),
+        compiler_params=params(),
+        cost_estimate=pl.CostEstimate(flops=int(WEIGHT * 1.15e9), bytes_accessed=0, transcendentals=0),
+    )(in_vmem(a), in_vmem(b))
 
 
 def on_device(n_row, n_col, tokens, gate_weight, up_weight, down_weight, gate_mask, up_mask, down_mask):
@@ -178,41 +205,49 @@
     rows = tokens.shape[0]
     panel = gate_weight.shape[0]
     row, col = lax.axis_index("row"), lax.axis_index("col")
+    chip, core = col // 2, col % 2
+
+    def fetch(d, slices):
+        part = panel // slices
+        return lax.dynamic_slice(tokens, (0, (row ^ d) * panel + (col % slices) * part), (rows, part))
 
     slices = min(n_col, panel // BLOCK)
-    part = panel // slices
-    mine = []
-    for d in range(1, n_row):
-        start = (row ^ d) * panel + (col % slices) * part
-        mine.append(lax.dynamic_slice(tokens, (0, start), (rows, part)))
-    mine, row = lax.optimization_barrier((mine, row))
-    mine = jnp.stack([swap(m, "row", n_row, d + 1) for d, m in enumerate(mine)])
-    gate_own, gate_weight = own_partial(row, tokens, gate_weight, gate_mask)
-    mine, gate_own, row = lax.optimization_barrier((mine, gate_own, row))
-    up_own, up_weight = own_partial(row, tokens, up_weight, up_mask)
-    even = jnp.stack([mine] + [swap(mine, "col", n_col, e) for e in range(2, slices, 2)])
+    pieces = [fetch(1, 2)] + [fetch(d, slices) for d in range(2, n_row)]
+    pieces, row = lax.optimization_barrier((pieces, row))
+    pieces = [swap(piece, "row", n_row, d + 1) for d, piece in enumerate(pieces)]
+    own, gate_weight, up_weight = own_partial(row, tokens, gate_weight, up_weight, gate_mask, up_mask)
+    pieces, own = lax.optimization_barrier((pieces, own))
+    weights = (gate_weight, up_weight, gate_mask, up_mask)
+    near = pieces[0][None, None]
+    near_other = swap(near, "col", n_col, 1)
+    far = jnp.stack(pieces[1:])
+    even = jnp.stack([far] + [swap(far, "col", n_col, e) for e in range(2, slices, 2)])
+    even, own[-1] = lax.optimization_barrier((even, own[-1]))
     odd = swap(even, "col", n_col, 1)
 
     order = jnp.asarray([*range(0, slices, 2), *range(1, slices, 2)], jnp.int32)
-    others = others_partial((col % slices) ^ order, even, odd, gate_weight, up_weight, gate_mask, up_mask)
-    gate_came, up_came = swap(gate_own, "row", n_row, 1), swap(up_own, "row", n_row, 1)
-    place = jnp.stack([(col // 2) ^ row, col % 2]).astype(jnp.int32)
-    sums = []
-    for k in range(CHUNKS):
-        held = {d: others[d - 1][k] for d in range(1, n_row)}
-        held[1] = add(jnp.stack([gate_came[k], up_came[k]]), held[1]).astype(jnp.bfloat16)
-        sums.append(held)
-    sums = lax.optimization_barrier(sums)
+    sums = [own]
+    sums += others_partial(core ^ jnp.arange(2, dtype=jnp.int32), near, near_other, *weights)
+    sums += others_partial((col % slices) ^ order, even, odd, *weights)
+
+    helds = []
+    for k in range(len(PARTS)):
+        held = {d: [sums[d][k]] for d in range(n_row)}
+        held[1].append(swap(held.pop(0)[0], "row", n_row, 1))
+        held[1] = [add(*held[1]).astype(jnp.bfloat16)]
+        helds.append(held)
     hiddens = []
-    for held in sums:
+    for held in helds:
         bit = 1
         while bit < n_row:
             for d in [d for d in held if not d & bit]:
-                total = add(swap(held.pop(d), "row", n_row, bit), held[d | bit])
-                held[d | bit] = total.astype(jnp.bfloat16) if 2 * bit < n_row else total
+                held[d | bit].append(swap(add(*held.pop(d)).astype(jnp.bfloat16), "row", n_row, bit))
             bit *= 2
+        own, *came, late = held[n_row - 1]
+        held[n_row - 1] = add(join(late, own), *came)
         gate, up = held[n_row - 1]
         hiddens.append({n_row - 1: (jax.nn.silu(gate) * up).astype(jnp.bfloat16)})
+    place = jnp.stack([chip ^ row, core]).astype(jnp.int32)
     arrived = []
     for k, hidden in enumerate(hiddens):
         bit = n_row // 2
@@ -232,10 +267,11 @@
     place, _ = lax.optimization_barrier((place, arrived[-1]))
 
     result = []
-    for hidden in hiddens:
+    for k, hidden in enumerate(hiddens):
         keep, give = down_partial(place, hidden, down_weight, down_mask)
+        if result:
+            give, result[-1] = lax.optimization_barrier((give, result[-1]))
         share = add(keep, swap(give, "col", n_col, 1)).astype(jnp.bfloat16)
-        share, place = lax.optimization_barrier((share, place))
         came = [swap(share[e], "col", n_col, 2 * e) for e in range(1, n_row)]
         result.append(add(share[0], *came).astype(jnp.bfloat16))
     return jnp.concatenate(result)

time: 154 us -> 146 us (0.948)
  waiting for transfers between devices: 89.5 us -> 82.7 us
    ppermute x27 -> x28, waiting for transfers between devices: 89.5 us -> 82.7 us  [swap(): return lax.ppermute(value, axis, [(i, i ^ mask) for i in range(size)])]
    pallas_call x2 -> x3, Pallas kernels: 11.4 us -> 8.43 us  [the longest x1 8.2 us: own_partial(): pl.pallas_call(own_kernel, in_specs=[SMEM, SMEM, SMEM, HBM, HBM, HBM], ou...]
    pallas_call x1 -> x2, Pallas kernels: 7.95 us -> 9.28 us  [others_partial(): pl.pallas_call(functools.partial(others_kernel, groups), in_specs=[SMEM,...]
    ppermute x27 -> x28, starting transfers between devices: 30 us -> 30.3 us  [swap(): return lax.ppermute(value, axis, [(i, i ^ mask) for i in range(size)])]
  transfers between devices with their start and end apart: 27 -> 28, of which waited for: 15 -> 20; matrix products, arithmetic and copies ran while one was open for 1% -> 1% of each run, Pallas kernels for 10% -> 17%
where the time goes in v3:
time: 146 us
  waiting for transfers between devices  82.7 us (57%)
  starting transfers between devices  30.3 us (21%)
  Pallas kernels  28.4 us (19%)
  other arithmetic  2.07 us (1%)
  local copies, waits for them, and re-layouts  1.92 us (1%)
    ppermute x28, waiting for transfers between devices, swap(): return lax.ppermute(value, axis, [(i, i ^ mask) for i in range(size)])  82.7 us
    ppermute x28, starting transfers between devices, swap(): return lax.ppermute(value, axis, [(i, i ^ mask) for i in range(size)])  30.3 us
    pallas_call x2, Pallas kernels, others_partial(): pl.pallas_call(functools.partial(others_kernel, groups), in_specs=[SMEM,...  9.28 us
    pallas_call x1, Pallas kernels, own_partial(): pl.pallas_call(own_kernel, in_specs=[SMEM, SMEM, SMEM, HBM, HBM, HBM], ou...  8.2 us
    pallas_call x2, Pallas kernels, down_partial(): pl.pallas_call(functools.partial(down_kernel, n_row), in_specs=[SMEM, SME...  6.76 us
    pallas_call x1, Pallas kernels, load(): pl.pallas_call(load_kernel, in_specs=[SMEM, HBM], out_specs=VMEM, out_sha...  3.93 us
  transfers between devices with their start and end apart: 28, of which 20 were waited for; matrix products, arithmetic and copies ran while one was open for 1% of the time, Pallas kernels for 17%

profile of v3, /device:TPU:0, one launch (start us, length us, event | category | flops | bytes accessed | tf_op | source)
XLA Modules:
  0.0 145.6 jit_solution(7797622227287258604)
XLA Ops:
  0.0 1.0 constant_dynamic-slice_fusion.2
  1.0 0.9 constant_dynamic-slice_fusion
  1.9 3.1 %collective-permute-start = (bf16[128,1024]{1,0:T(8,128)(2,1)S(1)}, bf16[128,1024]{1,0:T(8,128)(2,1)S(1)}, u32[]{:S(2)}, u32[]{:S(2)}) collective-permute-start(bf16[128,1024]{1,0:T(8,128)(2,1)S(1)} %constant_dynamic-slice_fusion.2), channel_id=1, source_target_pairs={{0,8},{8,0},{16,24},{24,16},{1,9},{9,1},{17,25},{25,17},{2,10},{10... | collective-permute-start | bytes 786440 | tf_op jit(solution)/shard_map/ppermute | solution.py:36
  5.0 2.6 %collective-permute-start.1 = (bf16[128,256]{1,0:T(8,128)(2,1)S(1)}, bf16[128,256]{1,0:T(8,128)(2,1)S(1)}, u32[]{:S(2)}, u32[]{:S(2)}) collective-permute-start(bf16[128,256]{1,0:T(8,128)(2,1)S(1)} %get-tuple-element.43), channel_id=1, source_target_pairs={{0,16},{8,24},{16,0},{24,8},{1,17},{9,25},{17,1},{25,9},{2,18},{10... | collective-permute-start | bytes 196616 | tf_op jit(solution)/shard_map/ppermute | solution.py:36
  7.5 8.2 %shard_map.82 = (bf16[2,64,2048]{2,1,0:T(8,128)(2,1)S(1)}, bf16[2,64,2048]{2,1,0:T(8,128)(2,1)S(1)}, bf16[2048,2048]{1,0:T(8,128)(2,1)S(1)}, bf16[2048,2048]{1,0:T(8,128)(2,1)S(1)}) custom-call(s32[1]{0:T(128)} %bitcast.s_ref, s32[16,16]{1,0:T(8,128)} %gm_ref.5, s32[16,16]{1,0:T(8,128)} %um_ref.5, bf16[128,8192]{1,0:T(8,128)(2,1)} %tokens_ref.1, ...), custom_call_target="tpu_custom_call" | custom-call | tf_op jit(solution)/shard_map/pallas_call | solution.py:98
  15.8 0.5 collective-permute-done.2
  16.3 0.5 collective-permute-start.4
  16.8 1.6 %collective-permute-start.7 = (bf16[2,128,256]{2,1,0:T(8,128)(2,1)S(1)}, bf16[2,128,256]{2,1,0:T(8,128)(2,1)S(1)}, u32[]{:S(2)}, u32[]{:S(2)}) collective-permute-start(bf16[2,128,256]{2,1,0:T(8,128)(2,1)S(1)} %get-tuple-element.88), channel_id=1, source_target_pairs={{0,4},{1,5},{2,6},{3,7},{4,0},{5,1},{6,2},{7,3},{8,12},{9,13},{10,... | collective-permute-start | bytes 393224 | tf_op jit(solution)/shard_map/ppermute | solution.py:36
  18.4 1.5 %collective-permute-start.6 = (bf16[2,128,256]{2,1,0:T(8,128)(2,1)S(1)}, bf16[2,128,256]{2,1,0:T(8,128)(2,1)S(1)}, u32[]{:S(2)}, u32[]{:S(2)}) collective-permute-start(bf16[2,128,256]{2,1,0:T(8,128)(2,1)S(1)} %get-tuple-element.88), channel_id=1, source_target_pairs={{0,2},{1,3},{2,0},{3,1},{4,6},{5,7},{6,4},{7,5},{8,10},{9,11},{10,... | collective-permute-start | bytes 393224 | tf_op jit(solution)/shard_map/ppermute | solution.py:36
  19.8 0.5 collective-permute-start.8
  20.3 2.4 %collective-permute-done.7 = bf16[2,128,256]{2,1,0:T(8,128)(2,1)S(1)} collective-permute-done((bf16[2,128,256]{2,1,0:T(8,128)(2,1)S(1)}, bf16[2,128,256]{2,1,0:T(8,128)(2,1)S(1)}, u32[]{:S(2)}, u32[]{:S(2)}) %collective-permute-start.7) | collective-permute-done | bytes 131104 | tf_op jit(solution)/shard_map/ppermute | solution.py:36
  22.7 1.9 %collective-permute-done.6 = bf16[2,128,256]{2,1,0:T(8,128)(2,1)S(1)} collective-permute-done((bf16[2,128,256]{2,1,0:T(8,128)(2,1)S(1)}, bf16[2,128,256]{2,1,0:T(8,128)(2,1)S(1)}, u32[]{:S(2)}, u32[]{:S(2)}) %collective-permute-start.6) | collective-permute-done | bytes 131104 | tf_op jit(solution)/shard_map/ppermute | solution.py:36
  24.7 2.0 %collective-permute-done.8 = bf16[2,128,256]{2,1,0:T(8,128)(2,1)S(1)} collective-permute-done((bf16[2,128,256]{2,1,0:T(8,128)(2,1)S(1)}, bf16[2,128,256]{2,1,0:T(8,128)(2,1)S(1)}, u32[]{:S(2)}, u32[]{:S(2)}) %collective-permute-start.8) | collective-permute-done | bytes 131104 | tf_op jit(solution)/shard_map/ppermute | solution.py:36
  26.8 1.6 %collective-permute-start.13 = (bf16[2,64,2048]{2,1,0:T(8,128)(2,1)S(1)}, bf16[2,64,2048]{2,1,0:T(8,128)(2,1)S(1)}, u32[]{:S(2)}, u32[]{:S(2)}) collective-permute-start(bf16[2,64,2048]{2,1,0:T(8,128)(2,1)S(1)} %get-tuple-element.60), channel_id=1, source_target_pairs={{0,8},{8,0},{16,24},{24,16},{1,9},{9,1},{17,25},{25,17},{2,10},{10... | collective-permute-start | bytes 1572872 | tf_op jit(solution)/shard_map/ppermute | solution.py:36
  28.4 3.6 %shard_map.83 = (bf16[2,64,2048]{2,1,0:T(8,128)(2,1)S(1)}, bf16[2,64,2048]{2,1,0:T(8,128)(2,1)S(1)}) custom-call(s32[2]{0:T(128)S(1)} %iota_xor_fusion.s_ref, s32[16,16]{1,0:T(8,128)} %gm_ref.5, s32[16,16]{1,0:T(8,128)} %um_ref.5, bf16[1,1,128,1024]{3,2,1,0:T(8,128)(2,1)S(1)} %bitcast.54, bf16[1,1,128,1024]{3,2,1,0:T(8,128)(2,1)S(1)} %collective-permute-done.3.odd_ref, ...), custom_call_target="tpu_custom_call" | custom-call | tf_op jit(solution)/shard_map/pallas_call | solution.py:128
  32.0 0.1 add_convert_fusion.3
  32.1 2.1 %collective-permute-start.5 = (bf16[2,64,2048]{2,1,0:T(8,128)(2,1)S(1)}, bf16[2,64,2048]{2,1,0:T(8,128)(2,1)S(1)}, u32[]{:S(2)}, u32[]{:S(2)}) collective-permute-start(bf16[2,64,2048]{2,1,0:T(8,128)(2,1)S(1)} %add_convert_fusion.3), channel_id=1, source_target_pairs={{0,16},{8,24},{16,0},{24,8},{1,17},{9,25},{17,1},{25,9},{2,18},{10... | collective-permute-start | bytes 1572872 | tf_op jit(solution)/shard_map/ppermute | solution.py:36
  34.3 5.7 %shard_map.84 = (bf16[2,64,2048]{2,1,0:T(8,128)(2,1)S(1)}, bf16[2,64,2048]{2,1,0:T(8,128)(2,1)S(1)}, bf16[2,64,2048]{2,1,0:T(8,128)(2,1)S(1)}, bf16[2,64,2048]{2,1,0:T(8,128)(2,1)S(1)}) custom-call(s32[8]{0:T(128)S(1)} %broadcast_xor_fusion.s_ref, s32[16,16]{1,0:T(8,128)} %gm_ref.5, s32[16,16]{1,0:T(8,128)} %um_ref.5, ...), custom_call_target="tpu_custom_call" | custom-call | tf_op jit(solution)/shard_map/pallas_call | solution.py:128
  40.0 2.0 %collective-permute-start.10 = (bf16[2,64,2048]{2,1,0:T(8,128)(2,1)S(1)}, bf16[2,64,2048]{2,1,0:T(8,128)(2,1)S(1)}, u32[]{:S(2)}, u32[]{:S(2)}) collective-permute-start(bf16[2,64,2048]{2,1,0:T(8,128)(2,1)S(1)} %get-tuple-element.58), channel_id=1, source_target_pairs={{0,8},{8,0},{16,24},{24,16},{1,9},{9,1},{17,25},{25,17},{2,10},{10... | collective-permute-start | bytes 1572872 | tf_op jit(solution)/shard_map/ppermute | solution.py:36
  42.0 6.8 %collective-permute-done.13 = bf16[2,64,2048]{2,1,0:T(8,128)(2,1)S(1)} collective-permute-done((bf16[2,64,2048]{2,1,0:T(8,128)(2,1)S(1)}, bf16[2,64,2048]{2,1,0:T(8,128)(2,1)S(1)}, u32[]{:S(2)}, u32[]{:S(2)}) %collective-permute-start.13) | collective-permute-done | bytes 524320 | tf_op jit(solution)/shard_map/ppermute | solution.py:36
  48.7 0.1 add_convert_fusion.2
  48.9 0.1 collective-permute-start.14
  48.9 0.5 collective-permute-start.15
  49.5 9.7 %collective-permute-done.5.a_ref = bf16[2,64,2048]{2,1,0:T(8,128)(2,1)S(1)} collective-permute-done((bf16[2,64,2048]{2,1,0:T(8,128)(2,1)S(1)}, bf16[2,64,2048]{2,1,0:T(8,128)(2,1)S(1)}, u32[]{:S(2)}, u32[]{:S(2)}) %collective-permute-start.5) | collective-permute-done | bytes 524320 | tf_op jit(solution)/shard_map/ppermute | solution.py:36
  59.2 0.1 shard_map.85
  59.3 11.9 %collective-permute-done.10 = bf16[2,64,2048]{2,1,0:T(8,128)(2,1)S(1)} collective-permute-done((bf16[2,64,2048]{2,1,0:T(8,128)(2,1)S(1)}, bf16[2,64,2048]{2,1,0:T(8,128)(2,1)S(1)}, u32[]{:S(2)}, u32[]{:S(2)}) %collective-permute-start.10) | collective-permute-done | bytes 524320 | tf_op jit(solution)/shard_map/ppermute | solution.py:36
  71.2 0.1 convert_add_fusion.1
  71.3 0.1 fusion.3.refs_3_
  71.5 0.1 collective-permute-start.12
  71.6 0.5 collective-permute-start.11
  72.1 9.6 %collective-permute-done.14.a_ref = bf16[2,64,2048]{2,1,0:T(8,128)(2,1)S(1)} collective-permute-done((bf16[2,64,2048]{2,1,0:T(8,128)(2,1)S(1)}, bf16[2,64,2048]{2,1,0:T(8,128)(2,1)S(1)}, u32[]{:S(2)}, u32[]{:S(2)}) %collective-permute-start.14) | collective-permute-done | bytes 524320 | tf_op jit(solution)/shard_map/ppermute | solution.py:36
  81.7 0.1 shard_map.86
  81.9 10.4 %collective-permute-done.15 = bf16[2,64,2048]{2,1,0:T(8,128)(2,1)S(1)} collective-permute-done((bf16[2,64,2048]{2,1,0:T(8,128)(2,1)S(1)}, bf16[2,64,2048]{2,1,0:T(8,128)(2,1)S(1)}, u32[]{:S(2)}, u32[]{:S(2)}) %collective-permute-start.15) | collective-permute-done | bytes 524320 | tf_op jit(solution)/shard_map/ppermute | solution.py:36
  92.3 0.1 convert_add_fusion
  92.4 0.1 fusion.1.refs_3_
  92.6 3.8 %collective-permute-done.12.refs_2_ = bf16[64,2048]{1,0:T(8,128)(2,1)S(1)} collective-permute-done((bf16[64,2048]{1,0:T(8,128)(2,1)S(1)}, bf16[64,2048]{1,0:T(8,128)(2,1)S(1)}, u32[]{:S(2)}, u32[]{:S(2)}) %collective-permute-start.12) | collective-permute-done | bytes 262176 | tf_op jit(solution)/shard_map/ppermute | solution.py:36
  96.4 3.6 %collective-permute-start.17 = (bf16[64,2048]{1,0:T(8,128)(2,1)S(1)}, bf16[64,2048]{1,0:T(8,128)(2,1)S(1)}, u32[]{:S(2)}, u32[]{:S(2)}) collective-permute-start(bf16[64,2048]{1,0:T(8,128)(2,1)S(1)} %fusion.1.refs_3_), channel_id=1, source_target_pairs={{0,8},{8,0},{16,24},{24,16},{1,9},{9,1},{17,25},{25,17},{2,10},{10... | collective-permute-start | bytes 786440 | tf_op jit(solution)/shard_map/ppermute | solution.py:36
  100.0 0.5 collective-permute-start.16
  100.5 0.5 collective-permute-start.19
  101.0 0.1 pad_add_fusion.s_ref
  101.0 3.9 %shard_map.87.refs_4_ = bf16[2048,2048]{1,0:T(8,128)(2,1)S(1)} custom-call(s32[2]{0:T(128)S(1)} %pad_add_fusion.s_ref, bf16[2048,2048]{1,0:T(8,128)(2,1)} %w_ref.1), custom_call_target="tpu_custom_call" | custom-call | tf_op jit(solution)/shard_map/pallas_call | solution.py:147
  105.0 7.8 %collective-permute-done.17.refs_2_ = bf16[64,2048]{1,0:T(8,128)(2,1)S(1)} collective-permute-done((bf16[64,2048]{1,0:T(8,128)(2,1)S(1)}, bf16[64,2048]{1,0:T(8,128)(2,1)S(1)}, u32[]{:S(2)}, u32[]{:S(2)}) %collective-permute-start.17) | collective-permute-done | bytes 262176 | tf_op jit(solution)/shard_map/ppermute | solution.py:36
  112.7 0.1 collective-permute-done.16.refs_1_
  112.9 3.4 %collective-permute-done.19.refs_0_ = bf16[64,2048]{1,0:T(8,128)(2,1)S(1)} collective-permute-done((bf16[64,2048]{1,0:T(8,128)(2,1)S(1)}, bf16[64,2048]{1,0:T(8,128)(2,1)S(1)}, u32[]{:S(2)}, u32[]{:S(2)}) %collective-permute-start.19) | collective-permute-done | bytes 262176 | tf_op jit(solution)/shard_map/ppermute | solution.py:36
  116.3 3.5 %shard_map.89 = (bf16[4,32,2048]{2,1,0:T(8,128)(2,1)S(1)}, bf16[4,32,2048]{2,1,0:T(8,128)(2,1)S(1)}) custom-call(s32[2]{0:T(128)S(1)} %pad_add_fusion.s_ref, s32[16,16]{1,0:T(8,128)} %m_ref.3, bf16[64,2048]{1,0:T(8,128)(2,1)S(1)} %collective-permute-done.19.refs_0_, bf16[64,2048]{1,0:T(8,128)(2,1)S(1)} %collective-permute-done.11.refs_1_, ...), custom_call_target="tpu_custom_call" | custom-call | tf_op jit(solution)/shard_map/pallas_call | solution.py:177
  119.8 0.1 collective-permute-start.20
  119.9 1.8 %collective-permute-start.18 = (bf16[64,2048]{1,0:T(8,128)(2,1)S(1)}, bf16[64,2048]{1,0:T(8,128)(2,1)S(1)}, u32[]{:S(2)}, u32[]{:S(2)}) collective-permute-start(bf16[64,2048]{1,0:T(8,128)(2,1)S(1)} %collective-permute-done.16.refs_1_), channel_id=1, source_target_pairs={{0,8},{8,0},{16,24},{24,16},{1,9},{9,1},{17,25},{25,17},{2,10},{10... | collective-permute-start | bytes 786440 | tf_op jit(solution)/shard_map/ppermute | solution.py:36
  121.7 0.1 collective-permute-done.20
  121.8 0.1 add_convert_fusion.1
  121.9 1.3 collective-permute-start.21
  123.2 1.5 %collective-permute-start.23 = (bf16[32,2048]{1,0:T(8,128)(2,1)S(1)}, bf16[32,2048]{1,0:T(8,128)(2,1)S(1)}, u32[]{:S(2)}, u32[]{:S(2)}) collective-permute-start(bf16[32,2048]{1,0:T(8,128)(2,1)S(1)} %get-tuple-element.85), channel_id=1, source_target_pairs={{0,6},{1,7},{2,4},{3,5},{4,2},{5,3},{6,0},{7,1},{8,14},{9,15},{10,... | collective-permute-start | bytes 393224 | tf_op jit(solution)/shard_map/ppermute | solution.py:36
  124.7 0.8 collective-permute-start.22
  125.5 3.1 %collective-permute-done.18.refs_0_ = bf16[64,2048]{1,0:T(8,128)(2,1)S(1)} collective-permute-done((bf16[64,2048]{1,0:T(8,128)(2,1)S(1)}, bf16[64,2048]{1,0:T(8,128)(2,1)S(1)}, u32[]{:S(2)}, u32[]{:S(2)}) %collective-permute-start.18) | collective-permute-done | bytes 262176 | tf_op jit(solution)/shard_map/ppermute | solution.py:36
  128.6 3.3 %shard_map.88 = (bf16[4,32,2048]{2,1,0:T(8,128)(2,1)S(1)}, bf16[4,32,2048]{2,1,0:T(8,128)(2,1)S(1)}) custom-call(s32[2]{0:T(128)S(1)} %pad_add_fusion.s_ref, s32[16,16]{1,0:T(8,128)} %m_ref.3, bf16[64,2048]{1,0:T(8,128)(2,1)S(1)} %collective-permute-done.18.refs_0_, bf16[64,2048]{1,0:T(8,128)(2,1)S(1)} %collective-permute-done.16.refs_1_, ...), custom_call_target="tpu_custom_call" | custom-call | tf_op jit(solution)/shard_map/pallas_call | solution.py:177
  131.9 0.6 collective-permute-done.22
  132.7 1.9 %collective-permute-done.24 = bf16[4,32,2048]{2,1,0:T(8,128)(2,1)S(1)} collective-permute-done((bf16[4,32,2048]{2,1,0:T(8,128)(2,1)S(1)}, bf16[4,32,2048]{2,1,0:T(8,128)(2,1)S(1)}, u32[]{:S(2)}, u32[]{:S(2)}) %collective-permute-start.24) | collective-permute-done | bytes 524320 | tf_op jit(solution)/shard_map/ppermute | solution.py:36
  134.6 0.1 add_convert_fusion
  134.7 1.6 %collective-permute-start.25 = (bf16[32,2048]{1,0:T(8,128)(2,1)S(1)}, bf16[32,2048]{1,0:T(8,128)(2,1)S(1)}, u32[]{:S(2)}, u32[]{:S(2)}) collective-permute-start(bf16[32,2048]{1,0:T(8,128)(2,1)S(1)} %get-tuple-element.81), channel_id=1, source_target_pairs={{0,2},{1,3},{2,0},{3,1},{4,6},{5,7},{6,4},{7,5},{8,10},{9,11},{10,... | collective-permute-start | bytes 393224 | tf_op jit(solution)/shard_map/ppermute | solution.py:36
  136.3 0.7 collective-permute-start.27
  137.0 1.3 collective-permute-start.26
  138.3 2.9 %collective-permute-done.25 = bf16[32,2048]{1,0:T(8,128)(2,1)S(1)} collective-permute-done((bf16[32,2048]{1,0:T(8,128)(2,1)S(1)}, bf16[32,2048]{1,0:T(8,128)(2,1)S(1)}, u32[]{:S(2)}, u32[]{:S(2)}) %collective-permute-start.25) | collective-permute-done | bytes 131104 | tf_op jit(solution)/shard_map/ppermute | solution.py:36
  141.1 2.3 %collective-permute-done.27 = bf16[32,2048]{1,0:T(8,128)(2,1)S(1)} collective-permute-done((bf16[32,2048]{1,0:T(8,128)(2,1)S(1)}, bf16[32,2048]{1,0:T(8,128)(2,1)S(1)}, u32[]{:S(2)}, u32[]{:S(2)}) %collective-permute-start.27) | collective-permute-done | bytes 131104 | tf_op jit(solution)/shard_map/ppermute | solution.py:36
  143.4 1.4 collective-permute-done.26
  144.9 0.7 pad_maximum_fusion.1
  (22 shorter events, 0.4 us)
Async XLA Ops:
  1.9 14.4 %collective-permute-start = (bf16[128,1024]{1,0:T(8,128)(2,1)S(1)}, bf16[128,1024]{1,0:T(8,128)(2,1)S(1)}, u32[]{:S(2)}, u32[]{:S(2)}) collective-permute-start(bf16[128,1024]{1,0:T(8,128)(2,1)S(1)} %constant_dynamic-slice_fusion.2), channel_id=1, source_target_pairs={{0,8},{8,0},{16,24},{24,16},{1,9},{9,1},{17,25},{25,17},{2,10},{10... | collective-permute-start | bytes 786440 | tf_op jit(solution)/shard_map/ppermute | solution.py:36
  5.0 10.8 %collective-permute-start.1 = (bf16[128,256]{1,0:T(8,128)(2,1)S(1)}, bf16[128,256]{1,0:T(8,128)(2,1)S(1)}, u32[]{:S(2)}, u32[]{:S(2)}) collective-permute-start(bf16[128,256]{1,0:T(8,128)(2,1)S(1)} %get-tuple-element.43), channel_id=1, source_target_pairs={{0,16},{8,24},{16,0},{24,8},{1,17},{9,25},{17,1},{25,9},{2,18},{10... | collective-permute-start | bytes 196616 | tf_op jit(solution)/shard_map/ppermute | solution.py:36
  7.5 8.7 %collective-permute-start.2 = (bf16[128,256]{1,0:T(8,128)(2,1)S(1)}, bf16[128,256]{1,0:T(8,128)(2,1)S(1)}, u32[]{:S(2)}, u32[]{:S(2)}) collective-permute-start(bf16[128,256]{1,0:T(8,128)(2,1)S(1)} %get-tuple-element.44), channel_id=1, source_target_pairs={{0,24},{8,16},{16,8},{24,0},{1,25},{9,17},{17,9},{25,1},{2,26},{10... | collective-permute-start | bytes 196616 | tf_op jit(solution)/shard_map/ppermute | solution.py:36
  16.3 15.7 %collective-permute-start.4 = (bf16[2,64,2048]{2,1,0:T(8,128)(2,1)S(1)}, bf16[2,64,2048]{2,1,0:T(8,128)(2,1)S(1)}, u32[]{:S(2)}, u32[]{:S(2)}) collective-permute-start(bf16[2,64,2048]{2,1,0:T(8,128)(2,1)S(1)} %get-tuple-element.52), channel_id=1, source_target_pairs={{0,8},{8,0},{16,24},{24,16},{1,9},{9,1},{17,25},{25,17},{2,10},{10... | collective-permute-start | bytes 1572872 | tf_op jit(solution)/shard_map/ppermute | solution.py:36
  16.7 11.7 %collective-permute-start.3 = (bf16[1,1,128,1024]{3,2,1,0:T(8,128)(2,1)S(1)}, bf16[1,1,128,1024]{3,2,1,0:T(8,128)(2,1)S(1)}, u32[]{:S(2)}, u32[]{:S(2)}) collective-permute-start(bf16[1,1,128,1024]{3,2,1,0:T(8,128)(2,1)S(1)} %bitcast.53), channel_id=1, source_target_pairs={{0,1},{1,0},{2,3},{3,2},{4,5},{5,4},{6,7},{7,6},{8,9},{9,8},{10,11... | collective-permute-start | bytes 786440 | tf_op jit(solution)/shard_map/ppermute | solution.py:36
  16.8 6.0 %collective-permute-start.7 = (bf16[2,128,256]{2,1,0:T(8,128)(2,1)S(1)}, bf16[2,128,256]{2,1,0:T(8,128)(2,1)S(1)}, u32[]{:S(2)}, u32[]{:S(2)}) collective-permute-start(bf16[2,128,256]{2,1,0:T(8,128)(2,1)S(1)} %get-tuple-element.88), channel_id=1, source_target_pairs={{0,4},{1,5},{2,6},{3,7},{4,0},{5,1},{6,2},{7,3},{8,12},{9,13},{10,... | collective-permute-start | bytes 393224 | tf_op jit(solution)/shard_map/ppermute | solution.py:36
  18.4 6.3 %collective-permute-start.6 = (bf16[2,128,256]{2,1,0:T(8,128)(2,1)S(1)}, bf16[2,128,256]{2,1,0:T(8,128)(2,1)S(1)}, u32[]{:S(2)}, u32[]{:S(2)}) collective-permute-start(bf16[2,128,256]{2,1,0:T(8,128)(2,1)S(1)} %get-tuple-element.88), channel_id=1, source_target_pairs={{0,2},{1,3},{2,0},{3,1},{4,6},{5,7},{6,4},{7,5},{8,10},{9,11},{10,... | collective-permute-start | bytes 393224 | tf_op jit(solution)/shard_map/ppermute | solution.py:36
  19.8 6.9 %collective-permute-start.8 = (bf16[2,128,256]{2,1,0:T(8,128)(2,1)S(1)}, bf16[2,128,256]{2,1,0:T(8,128)(2,1)S(1)}, u32[]{:S(2)}, u32[]{:S(2)}) collective-permute-start(bf16[2,128,256]{2,1,0:T(8,128)(2,1)S(1)} %get-tuple-element.88), channel_id=1, source_target_pairs={{0,6},{1,7},{2,4},{3,5},{4,2},{5,3},{6,0},{7,1},{8,14},{9,15},{10,... | collective-permute-start | bytes 393224 | tf_op jit(solution)/shard_map/ppermute | solution.py:36
  26.8 21.9 %collective-permute-start.13 = (bf16[2,64,2048]{2,1,0:T(8,128)(2,1)S(1)}, bf16[2,64,2048]{2,1,0:T(8,128)(2,1)S(1)}, u32[]{:S(2)}, u32[]{:S(2)}) collective-permute-start(bf16[2,64,2048]{2,1,0:T(8,128)(2,1)S(1)} %get-tuple-element.60), channel_id=1, source_target_pairs={{0,8},{8,0},{16,24},{24,16},{1,9},{9,1},{17,25},{25,17},{2,10},{10... | collective-permute-start | bytes 1572872 | tf_op jit(solution)/shard_map/ppermute | solution.py:36
  28.4 5.8 %collective-permute-start.9 = (bf16[4,2,128,256]{3,2,1,0:T(8,128)(2,1)S(1)}, bf16[4,2,128,256]{3,2,1,0:T(8,128)(2,1)S(1)}, u32[]{:S(2)}, u32[]{:S(2)}) collective-permute-start(bf16[4,2,128,256]{3,2,1,0:T(8,128)(2,1)S(1)} %pad_maximum_fusion.even_ref), channel_id=1, source_target_pairs={{0,1},{1,0},{2,3},{3,2},{4,5},{5,4},{6,7},{7,6},{8,9},{9,8},{10,11... | collective-permute-start | bytes 1572872 | tf_op jit(solution)/shard_map/ppermute | solution.py:36
  28.4 5.8 %copy-start = (s32[8]{0:T(128)S(1)}, s32[8]{0:T(128)}, u32[]{:S(2)}) copy-start(s32[8]{0:T(128)} %constant.66.clone) | copy-start | bytes 100
  32.1 27.1 %collective-permute-start.5 = (bf16[2,64,2048]{2,1,0:T(8,128)(2,1)S(1)}, bf16[2,64,2048]{2,1,0:T(8,128)(2,1)S(1)}, u32[]{:S(2)}, u32[]{:S(2)}) collective-permute-start(bf16[2,64,2048]{2,1,0:T(8,128)(2,1)S(1)} %add_convert_fusion.3), channel_id=1, source_target_pairs={{0,16},{8,24},{16,0},{24,8},{1,17},{9,25},{17,1},{25,9},{2,18},{10... | collective-permute-start | bytes 1572872 | tf_op jit(solution)/shard_map/ppermute | solution.py:36
  40.0 31.2 %collective-permute-start.10 = (bf16[2,64,2048]{2,1,0:T(8,128)(2,1)S(1)}, bf16[2,64,2048]{2,1,0:T(8,128)(2,1)S(1)}, u32[]{:S(2)}, u32[]{:S(2)}) collective-permute-start(bf16[2,64,2048]{2,1,0:T(8,128)(2,1)S(1)} %get-tuple-element.58), channel_id=1, source_target_pairs={{0,8},{8,0},{16,24},{24,16},{1,9},{9,1},{17,25},{25,17},{2,10},{10... | collective-permute-start | bytes 1572872 | tf_op jit(solution)/shard_map/ppermute | solution.py:36
  48.9 32.9 %collective-permute-start.14 = (bf16[2,64,2048]{2,1,0:T(8,128)(2,1)S(1)}, bf16[2,64,2048]{2,1,0:T(8,128)(2,1)S(1)}, u32[]{:S(2)}, u32[]{:S(2)}) collective-permute-start(bf16[2,64,2048]{2,1,0:T(8,128)(2,1)S(1)} %add_convert_fusion.2), channel_id=1, source_target_pairs={{0,16},{8,24},{16,0},{24,8},{1,17},{9,25},{17,1},{25,9},{2,18},{10... | collective-permute-start | bytes 1572872 | tf_op jit(solution)/shard_map/ppermute | solution.py:36
  48.9 43.3 %collective-permute-start.15 = (bf16[2,64,2048]{2,1,0:T(8,128)(2,1)S(1)}, bf16[2,64,2048]{2,1,0:T(8,128)(2,1)S(1)}, u32[]{:S(2)}, u32[]{:S(2)}) collective-permute-start(bf16[2,64,2048]{2,1,0:T(8,128)(2,1)S(1)} %get-tuple-element.62), channel_id=1, source_target_pairs={{0,8},{8,0},{16,24},{24,16},{1,9},{9,1},{17,25},{25,17},{2,10},{10... | collective-permute-start | bytes 1572872 | tf_op jit(solution)/shard_map/ppermute | solution.py:36
  71.5 24.9 %collective-permute-start.12 = (bf16[64,2048]{1,0:T(8,128)(2,1)S(1)}, bf16[64,2048]{1,0:T(8,128)(2,1)S(1)}, u32[]{:S(2)}, u32[]{:S(2)}) collective-permute-start(bf16[64,2048]{1,0:T(8,128)(2,1)S(1)} %fusion.3.refs_3_), channel_id=1, source_target_pairs={{0,8},{8,0},{16,24},{24,16},{1,9},{9,1},{17,25},{25,17},{2,10},{10... | collective-permute-start | bytes 786440 | tf_op jit(solution)/shard_map/ppermute | solution.py:36
  71.6 24.8 %collective-permute-start.11 = (bf16[64,2048]{1,0:T(8,128)(2,1)S(1)}, bf16[64,2048]{1,0:T(8,128)(2,1)S(1)}, u32[]{:S(2)}, u32[]{:S(2)}) collective-permute-start(bf16[64,2048]{1,0:T(8,128)(2,1)S(1)} %fusion.3.refs_3_), channel_id=1, source_target_pairs={{0,16},{8,24},{16,0},{24,8},{1,17},{9,25},{17,1},{25,9},{2,18},{10... | collective-permute-start | bytes 786440 | tf_op jit(solution)/shard_map/ppermute | solution.py:36
  96.4 16.3 %collective-permute-start.17 = (bf16[64,2048]{1,0:T(8,128)(2,1)S(1)}, bf16[64,2048]{1,0:T(8,128)(2,1)S(1)}, u32[]{:S(2)}, u32[]{:S(2)}) collective-permute-start(bf16[64,2048]{1,0:T(8,128)(2,1)S(1)} %fusion.1.refs_3_), channel_id=1, source_target_pairs={{0,8},{8,0},{16,24},{24,16},{1,9},{9,1},{17,25},{25,17},{2,10},{10... | collective-permute-start | bytes 786440 | tf_op jit(solution)/shard_map/ppermute | solution.py:36
  100.0 12.9 %collective-permute-start.16 = (bf16[64,2048]{1,0:T(8,128)(2,1)S(1)}, bf16[64,2048]{1,0:T(8,128)(2,1)S(1)}, u32[]{:S(2)}, u32[]{:S(2)}) collective-permute-start(bf16[64,2048]{1,0:T(8,128)(2,1)S(1)} %fusion.1.refs_3_), channel_id=1, source_target_pairs={{0,16},{8,24},{16,0},{24,8},{1,17},{9,25},{17,1},{25,9},{2,18},{10... | collective-permute-start | bytes 786440 | tf_op jit(solution)/shard_map/ppermute | solution.py:36
  100.5 15.8 %collective-permute-start.19 = (bf16[64,2048]{1,0:T(8,128)(2,1)S(1)}, bf16[64,2048]{1,0:T(8,128)(2,1)S(1)}, u32[]{:S(2)}, u32[]{:S(2)}) collective-permute-start(bf16[64,2048]{1,0:T(8,128)(2,1)S(1)} %collective-permute-done.11.refs_1_), channel_id=1, source_target_pairs={{0,8},{8,0},{16,24},{24,16},{1,9},{9,1},{17,25},{25,17},{2,10},{10... | collective-permute-start | bytes 786440 | tf_op jit(solution)/shard_map/ppermute | solution.py:36
  119.8 2.0 %collective-permute-start.20 = (bf16[4,32,2048]{2,1,0:T(8,128)(2,1)S(1)}, bf16[4,32,2048]{2,1,0:T(8,128)(2,1)S(1)}, u32[]{:S(2)}, u32[]{:S(2)}) collective-permute-start(bf16[4,32,2048]{2,1,0:T(8,128)(2,1)S(1)} %get-tuple-element.75), channel_id=1, source_target_pairs={{0,1},{1,0},{2,3},{3,2},{4,5},{5,4},{6,7},{7,6},{8,9},{9,8},{10,11... | collective-permute-start | bytes 1572872 | tf_op jit(solution)/shard_map/ppermute | solution.py:36
  119.9 8.7 %collective-permute-start.18 = (bf16[64,2048]{1,0:T(8,128)(2,1)S(1)}, bf16[64,2048]{1,0:T(8,128)(2,1)S(1)}, u32[]{:S(2)}, u32[]{:S(2)}) collective-permute-start(bf16[64,2048]{1,0:T(8,128)(2,1)S(1)} %collective-permute-done.16.refs_1_), channel_id=1, source_target_pairs={{0,8},{8,0},{16,24},{24,16},{1,9},{9,1},{17,25},{25,17},{2,10},{10... | collective-permute-start | bytes 786440 | tf_op jit(solution)/shard_map/ppermute | solution.py:36
  121.9 9.9 %collective-permute-start.21 = (bf16[32,2048]{1,0:T(8,128)(2,1)S(1)}, bf16[32,2048]{1,0:T(8,128)(2,1)S(1)}, u32[]{:S(2)}, u32[]{:S(2)}) collective-permute-start(bf16[32,2048]{1,0:T(8,128)(2,1)S(1)} %get-tuple-element.84), channel_id=1, source_target_pairs={{0,2},{1,3},{2,0},{3,1},{4,6},{5,7},{6,4},{7,5},{8,10},{9,11},{10,... | collective-permute-start | bytes 393224 | tf_op jit(solution)/shard_map/ppermute | solution.py:36
  123.2 8.6 %collective-permute-start.23 = (bf16[32,2048]{1,0:T(8,128)(2,1)S(1)}, bf16[32,2048]{1,0:T(8,128)(2,1)S(1)}, u32[]{:S(2)}, u32[]{:S(2)}) collective-permute-start(bf16[32,2048]{1,0:T(8,128)(2,1)S(1)} %get-tuple-element.85), channel_id=1, source_target_pairs={{0,6},{1,7},{2,4},{3,5},{4,2},{5,3},{6,0},{7,1},{8,14},{9,15},{10,... | collective-permute-start | bytes 393224 | tf_op jit(solution)/shard_map/ppermute | solution.py:36
  124.7 7.8 %collective-permute-start.22 = (bf16[32,2048]{1,0:T(8,128)(2,1)S(1)}, bf16[32,2048]{1,0:T(8,128)(2,1)S(1)}, u32[]{:S(2)}, u32[]{:S(2)}) collective-permute-start(bf16[32,2048]{1,0:T(8,128)(2,1)S(1)} %get-tuple-element.86), channel_id=1, source_target_pairs={{0,4},{1,5},{2,6},{3,7},{4,0},{5,1},{6,2},{7,3},{8,12},{9,13},{10,... | collective-permute-start | bytes 393224 | tf_op jit(solution)/shard_map/ppermute | solution.py:36
  132.6 2.0 %collective-permute-start.24 = (bf16[4,32,2048]{2,1,0:T(8,128)(2,1)S(1)}, bf16[4,32,2048]{2,1,0:T(8,128)(2,1)S(1)}, u32[]{:S(2)}, u32[]{:S(2)}) collective-permute-start(bf16[4,32,2048]{2,1,0:T(8,128)(2,1)S(1)} %get-tuple-element.78), channel_id=1, source_target_pairs={{0,1},{1,0},{2,3},{3,2},{4,5},{5,4},{6,7},{7,6},{8,9},{9,8},{10,11... | collective-permute-start | bytes 1572872 | tf_op jit(solution)/shard_map/ppermute | solution.py:36
  134.7 6.4 %collective-permute-start.25 = (bf16[32,2048]{1,0:T(8,128)(2,1)S(1)}, bf16[32,2048]{1,0:T(8,128)(2,1)S(1)}, u32[]{:S(2)}, u32[]{:S(2)}) collective-permute-start(bf16[32,2048]{1,0:T(8,128)(2,1)S(1)} %get-tuple-element.81), channel_id=1, source_target_pairs={{0,2},{1,3},{2,0},{3,1},{4,6},{5,7},{6,4},{7,5},{8,10},{9,11},{10,... | collective-permute-start | bytes 393224 | tf_op jit(solution)/shard_map/ppermute | solution.py:36
  136.3 7.1 %collective-permute-start.27 = (bf16[32,2048]{1,0:T(8,128)(2,1)S(1)}, bf16[32,2048]{1,0:T(8,128)(2,1)S(1)}, u32[]{:S(2)}, u32[]{:S(2)}) collective-permute-start(bf16[32,2048]{1,0:T(8,128)(2,1)S(1)} %get-tuple-element.82), channel_id=1, source_target_pairs={{0,6},{1,7},{2,4},{3,5},{4,2},{5,3},{6,0},{7,1},{8,14},{9,15},{10,... | collective-permute-start | bytes 393224 | tf_op jit(solution)/shard_map/ppermute | solution.py:36
  137.0 7.8 %collective-permute-start.26 = (bf16[32,2048]{1,0:T(8,128)(2,1)S(1)}, bf16[32,2048]{1,0:T(8,128)(2,1)S(1)}, u32[]{:S(2)}, u32[]{:S(2)}) collective-permute-start(bf16[32,2048]{1,0:T(8,128)(2,1)S(1)} %get-tuple-element.83), channel_id=1, source_target_pairs={{0,4},{1,5},{2,6},{3,7},{4,0},{5,1},{6,2},{7,3},{8,12},{9,13},{10,... | collective-permute-start | bytes 393224 | tf_op jit(solution)/shard_map/ppermute | solution.py:36

commit v4 on v3

--- a/solution.py
+++ b/solution.py
@@ -248,14 +248,16 @@
         gate, up = held[n_row - 1]
         hiddens.append({n_row - 1: (jax.nn.silu(gate) * up).astype(jnp.bfloat16)})
     place = jnp.stack([chip ^ row, core]).astype(jnp.int32)
-    arrived = []
     for k, hidden in enumerate(hiddens):
         bit = n_row // 2
         for d in list(hidden):
             hidden[d ^ bit] = swap(hidden[d], "row", n_row, bit)
-        near = swap(hidden[n_row - 1], "row", n_row, 1)
-        hidden, near, hiddens[k + 1 :] = lax.optimization_barrier((hidden, near, hiddens[k + 1 :]))
-        arrived.append(hidden[n_row // 2 - 1])
+        own = hidden[n_row - 1]
+        if k:
+            own, hiddens[k - 1][0] = lax.optimization_barrier((own, hiddens[k - 1][0]))
+        near = swap(own, "row", n_row, 1)
+        if not k:
+            hidden, near = lax.optimization_barrier((hidden, near))
         while bit > 1:
             bit //= 2
             for d in list(hidden):
@@ -264,13 +266,10 @@
         hiddens[k] = [hidden[d] for d in range(n_row)]
     hiddens[0][-1], place = lax.optimization_barrier((hiddens[0][-1], place))
     down_weight = load(down_weight, place)
-    place, _ = lax.optimization_barrier((place, arrived[-1]))
 
     result = []
     for k, hidden in enumerate(hiddens):
         keep, give = down_partial(place, hidden, down_weight, down_mask)
-        if result:
-            give, result[-1] = lax.optimization_barrier((give, result[-1]))
         share = add(keep, swap(give, "col", n_col, 1)).astype(jnp.bfloat16)
         came = [swap(share[e], "col", n_col, 2 * e) for e in range(1, n_row)]
         result.append(add(share[0], *came).astype(jnp.bfloat16))

time: 146 us -> 162 us (1.11)
  local copies, waits for them, and re-layouts: 1.92 us -> 15.2 us
  waiting for transfers between devices: 82.7 us -> 85.1 us
    unnamed x2 -> x10, local copies, waits for them, and re-layouts: 0.01 us -> 13.3 us
    ppermute x28, waiting for transfers between devices: 82.7 us -> 85.1 us  [swap(): return lax.ppermute(value, axis, [(i, i ^ mask) for i in range(size)])]
  transfers between devices with their start and end apart: 28 -> 28, of which waited for: 20 -> 17; matrix products, arithmetic and copies ran while one was open for 1% -> 1% of each run, Pallas kernels for 17% -> 17%
where the time goes in v4:
time: 162 us; the launch traced here: 161 us
  waiting for transfers between devices  85.1 us (53%)
  starting transfers between devices  30.4 us (19%)
  Pallas kernels  28.1 us (17%)
  local copies, waits for them, and re-layouts  15.2 us (9%)
  other arithmetic  2.06 us (1%)
    ppermute x28, waiting for transfers between devices, swap(): return lax.ppermute(value, axis, [(i, i ^ mask) for i in range(size)])  85.1 us
    ppermute x28, starting transfers between devices, swap(): return lax.ppermute(value, axis, [(i, i ^ mask) for i in range(size)])  30.4 us
    unnamed x10, local copies, waits for them, and re-layouts  13.3 us
    pallas_call x2, Pallas kernels, others_partial(): pl.pallas_call(functools.partial(others_kernel, groups), in_specs=[SMEM,...  8.83 us
    pallas_call x1, Pallas kernels, own_partial(): pl.pallas_call(own_kernel, in_specs=[SMEM, SMEM, SMEM, HBM, HBM, HBM], ou...  8.33 us
    pallas_call x2, Pallas kernels, down_partial(): pl.pallas_call(functools.partial(down_kernel, n_row), in_specs=[SMEM, SME...  6.74 us
    pallas_call x1, Pallas kernels, load(): pl.pallas_call(load_kernel, in_specs=[SMEM, HBM], out_specs=VMEM, out_sha...  3.93 us
  transfers between devices with their start and end apart: 28, of which 17 were waited for; matrix products, arithmetic and copies ran while one was open for 1% of the time, Pallas kernels for 17%

profile of v4, /device:TPU:0, one launch (start us, length us, event | category | flops | bytes accessed | tf_op | source)
XLA Modules:
  0.0 161.1 jit_solution(10372147247092534069)
XLA Ops:
  0.0 1.0 constant_dynamic-slice_fusion.2
  1.0 0.9 constant_dynamic-slice_fusion
  1.9 3.1 %collective-permute-start = (bf16[128,1024]{1,0:T(8,128)(2,1)S(1)}, bf16[128,1024]{1,0:T(8,128)(2,1)S(1)}, u32[]{:S(2)}, u32[]{:S(2)}) collective-permute-start(bf16[128,1024]{1,0:T(8,128)(2,1)S(1)} %constant_dynamic-slice_fusion.2), channel_id=1, source_target_pairs={{0,8},{8,0},{16,24},{24,16},{1,9},{9,1},{17,25},{25,17},{2,10},{10... | collective-permute-start | bytes 786440 | tf_op jit(solution)/shard_map/ppermute | solution.py:36
  5.0 2.6 %collective-permute-start.1 = (bf16[128,256]{1,0:T(8,128)(2,1)S(1)}, bf16[128,256]{1,0:T(8,128)(2,1)S(1)}, u32[]{:S(2)}, u32[]{:S(2)}) collective-permute-start(bf16[128,256]{1,0:T(8,128)(2,1)S(1)} %get-tuple-element.38), channel_id=1, source_target_pairs={{0,16},{8,24},{16,0},{24,8},{1,17},{9,25},{17,1},{25,9},{2,18},{10... | collective-permute-start | bytes 196616 | tf_op jit(solution)/shard_map/ppermute | solution.py:36
  7.5 8.3 %shard_map.82 = (bf16[2,64,2048]{2,1,0:T(8,128)(2,1)S(1)}, bf16[2,64,2048]{2,1,0:T(8,128)(2,1)S(1)}, bf16[2048,2048]{1,0:T(8,128)(2,1)S(1)}, bf16[2048,2048]{1,0:T(8,128)(2,1)S(1)}) custom-call(s32[1]{0:T(128)} %bitcast.s_ref, s32[16,16]{1,0:T(8,128)} %gm_ref.5, s32[16,16]{1,0:T(8,128)} %um_ref.5, bf16[128,8192]{1,0:T(8,128)(2,1)} %tokens_ref.1, ...), custom_call_target="tpu_custom_call" | custom-call | tf_op jit(solution)/shard_map/pallas_call | solution.py:98
  15.9 3.3 %copy-done = bf16[2048,2048]{1,0:T(8,128)(2,1)} copy-done((bf16[2048,2048]{1,0:T(8,128)(2,1)}, bf16[2048,2048]{1,0:T(8,128)(2,1)S(1)}, u32[]{:S(2)}) %copy-start) | copy-done | bytes 8388632
  19.2 3.3 %copy-done.2 = bf16[2048,2048]{1,0:T(8,128)(2,1)} copy-done((bf16[2048,2048]{1,0:T(8,128)(2,1)}, bf16[2048,2048]{1,0:T(8,128)(2,1)S(1)}, u32[]{:S(2)}) %copy-start.2) | copy-done | bytes 8388632
  22.4 1.0 collective-permute-start.4
  23.4 1.6 collective-permute-start.7
  25.0 1.5 collective-permute-start.6
  26.5 0.5 collective-permute-start.8
  27.0 2.0 %collective-permute-done.7 = bf16[2,128,256]{2,1,0:T(8,128)(2,1)S(1)} collective-permute-done((bf16[2,128,256]{2,1,0:T(8,128)(2,1)S(1)}, bf16[2,128,256]{2,1,0:T(8,128)(2,1)S(1)}, u32[]{:S(2)}, u32[]{:S(2)}) %collective-permute-start.7) | collective-permute-done | bytes 131104 | tf_op jit(solution)/shard_map/ppermute | solution.py:36
  29.0 1.3 collective-permute-done.6
  30.3 2.1 %collective-permute-done.8 = bf16[2,128,256]{2,1,0:T(8,128)(2,1)S(1)} collective-permute-done((bf16[2,128,256]{2,1,0:T(8,128)(2,1)S(1)}, bf16[2,128,256]{2,1,0:T(8,128)(2,1)S(1)}, u32[]{:S(2)}, u32[]{:S(2)}) %collective-permute-start.8) | collective-permute-done | bytes 131104 | tf_op jit(solution)/shard_map/ppermute | solution.py:36
  32.4 1.5 collective-permute-start.13
  33.9 3.4 %copy-done.1 = bf16[2048,2048]{1,0:T(8,128)(2,1)S(1)} copy-done((bf16[2048,2048]{1,0:T(8,128)(2,1)S(1)}, bf16[2048,2048]{1,0:T(8,128)(2,1)}, u32[]{:S(2)}) %copy-start.1) | copy-done | bytes 8388632
  37.3 3.4 %copy-done.3 = bf16[2048,2048]{1,0:T(8,128)(2,1)S(1)} copy-done((bf16[2048,2048]{1,0:T(8,128)(2,1)S(1)}, bf16[2048,2048]{1,0:T(8,128)(2,1)}, u32[]{:S(2)}) %copy-start.3) | copy-done | bytes 8388632
  40.7 3.3 %shard_map.83 = (bf16[2,64,2048]{2,1,0:T(8,128)(2,1)S(1)}, bf16[2,64,2048]{2,1,0:T(8,128)(2,1)S(1)}) custom-call(s32[2]{0:T(128)S(1)} %iota_xor_fusion.s_ref, s32[16,16]{1,0:T(8,128)} %gm_ref.5, s32[16,16]{1,0:T(8,128)} %um_ref.5, bf16[1,1,128,1024]{3,2,1,0:T(8,128)(2,1)S(1)} %bitcast.54, bf16[1,1,128,1024]{3,2,1,0:T(8,128)(2,1)S(1)} %collective-permute-done.3.odd_ref, ...), custom_call_target="tpu_custom_call" | custom-call | tf_op jit(solution)/shard_map/pallas_call | solution.py:128
  44.0 0.1 add_convert_fusion.3
  44.1 2.5 %collective-permute-start.5 = (bf16[2,64,2048]{2,1,0:T(8,128)(2,1)S(1)}, bf16[2,64,2048]{2,1,0:T(8,128)(2,1)S(1)}, u32[]{:S(2)}, u32[]{:S(2)}) collective-permute-start(bf16[2,64,2048]{2,1,0:T(8,128)(2,1)S(1)} %add_convert_fusion.3), channel_id=1, source_target_pairs={{0,16},{8,24},{16,0},{24,8},{1,17},{9,25},{17,1},{25,9},{2,18},{10... | collective-permute-start | bytes 1572872 | tf_op jit(solution)/shard_map/ppermute | solution.py:36
  46.6 0.1 pad_add_fusion.s_ref
  46.7 5.5 %shard_map.84 = (bf16[2,64,2048]{2,1,0:T(8,128)(2,1)S(1)}, bf16[2,64,2048]{2,1,0:T(8,128)(2,1)S(1)}, bf16[2,64,2048]{2,1,0:T(8,128)(2,1)S(1)}, bf16[2,64,2048]{2,1,0:T(8,128)(2,1)S(1)}) custom-call(s32[8]{0:T(128)S(1)} %broadcast_xor_fusion.s_ref, s32[16,16]{1,0:T(8,128)} %gm_ref.5, s32[16,16]{1,0:T(8,128)} %um_ref.5, ...), custom_call_target="tpu_custom_call" | custom-call | tf_op jit(solution)/shard_map/pallas_call | solution.py:128
  52.2 1.8 %collective-permute-start.10 = (bf16[2,64,2048]{2,1,0:T(8,128)(2,1)S(1)}, bf16[2,64,2048]{2,1,0:T(8,128)(2,1)S(1)}, u32[]{:S(2)}, u32[]{:S(2)}) collective-permute-start(bf16[2,64,2048]{2,1,0:T(8,128)(2,1)S(1)} %get-tuple-element.53), channel_id=1, source_target_pairs={{0,8},{8,0},{16,24},{24,16},{1,9},{9,1},{17,25},{25,17},{2,10},{10... | collective-permute-start | bytes 1572872 | tf_op jit(solution)/shard_map/ppermute | solution.py:36
  54.0 0.1 add_convert_fusion.2
  54.1 0.1 collective-permute-start.14
  54.2 0.8 collective-permute-start.15
  55.0 16.1 %collective-permute-done.5.a_ref = bf16[2,64,2048]{2,1,0:T(8,128)(2,1)S(1)} collective-permute-done((bf16[2,64,2048]{2,1,0:T(8,128)(2,1)S(1)}, bf16[2,64,2048]{2,1,0:T(8,128)(2,1)S(1)}, u32[]{:S(2)}, u32[]{:S(2)}) %collective-permute-start.5) | collective-permute-done | bytes 524320 | tf_op jit(solution)/shard_map/ppermute | solution.py:36
  71.1 0.1 shard_map.85
  71.3 7.0 %collective-permute-done.10 = bf16[2,64,2048]{2,1,0:T(8,128)(2,1)S(1)} collective-permute-done((bf16[2,64,2048]{2,1,0:T(8,128)(2,1)S(1)}, bf16[2,64,2048]{2,1,0:T(8,128)(2,1)S(1)}, u32[]{:S(2)}, u32[]{:S(2)}) %collective-permute-start.10) | collective-permute-done | bytes 524320 | tf_op jit(solution)/shard_map/ppermute | solution.py:36
  78.3 0.1 convert_add_fusion.1
  78.4 0.1 fusion.3.refs_3_
  78.6 1.7 %collective-permute-start.11 = (bf16[64,2048]{1,0:T(8,128)(2,1)S(1)}, bf16[64,2048]{1,0:T(8,128)(2,1)S(1)}, u32[]{:S(2)}, u32[]{:S(2)}) collective-permute-start(bf16[64,2048]{1,0:T(8,128)(2,1)S(1)} %fusion.3.refs_3_), channel_id=1, source_target_pairs={{0,16},{8,24},{16,0},{24,8},{1,17},{9,25},{17,1},{25,9},{2,18},{10... | collective-permute-start | bytes 786440 | tf_op jit(solution)/shard_map/ppermute | solution.py:36
  80.3 13.3 %collective-permute-done.14.a_ref = bf16[2,64,2048]{2,1,0:T(8,128)(2,1)S(1)} collective-permute-done((bf16[2,64,2048]{2,1,0:T(8,128)(2,1)S(1)}, bf16[2,64,2048]{2,1,0:T(8,128)(2,1)S(1)}, u32[]{:S(2)}, u32[]{:S(2)}) %collective-permute-start.14) | collective-permute-done | bytes 524320 | tf_op jit(solution)/shard_map/ppermute | solution.py:36
  93.7 0.1 shard_map.86
  93.8 11.5 %collective-permute-done.15 = bf16[2,64,2048]{2,1,0:T(8,128)(2,1)S(1)} collective-permute-done((bf16[2,64,2048]{2,1,0:T(8,128)(2,1)S(1)}, bf16[2,64,2048]{2,1,0:T(8,128)(2,1)S(1)}, u32[]{:S(2)}, u32[]{:S(2)}) %collective-permute-start.15) | collective-permute-done | bytes 524320 | tf_op jit(solution)/shard_map/ppermute | solution.py:36
  105.3 0.1 convert_add_fusion
  105.5 4.8 %collective-permute-done.12.refs_2_ = bf16[64,2048]{1,0:T(8,128)(2,1)S(1)} collective-permute-done((bf16[64,2048]{1,0:T(8,128)(2,1)S(1)}, bf16[64,2048]{1,0:T(8,128)(2,1)S(1)}, u32[]{:S(2)}, u32[]{:S(2)}) %collective-permute-start.12) | collective-permute-done | bytes 262176 | tf_op jit(solution)/shard_map/ppermute | solution.py:36
  110.3 0.1 fusion.1.refs_3_
  110.4 3.0 %collective-permute-start.21 = (bf16[64,2048]{1,0:T(8,128)(2,1)S(1)}, bf16[64,2048]{1,0:T(8,128)(2,1)S(1)}, u32[]{:S(2)}, u32[]{:S(2)}) collective-permute-start(bf16[64,2048]{1,0:T(8,128)(2,1)S(1)} %fusion.1.refs_3_), channel_id=1, source_target_pairs={{0,16},{8,24},{16,0},{24,8},{1,17},{9,25},{17,1},{25,9},{2,18},{10... | collective-permute-start | bytes 786440 | tf_op jit(solution)/shard_map/ppermute | solution.py:36
  113.4 3.9 %shard_map.87.refs_4_ = bf16[2048,2048]{1,0:T(8,128)(2,1)S(1)} custom-call(s32[2]{0:T(128)S(1)} %pad_add_fusion.s_ref, bf16[2048,2048]{1,0:T(8,128)(2,1)} %w_ref.1), custom_call_target="tpu_custom_call" | custom-call | tf_op jit(solution)/shard_map/pallas_call | solution.py:147
  117.4 5.7 %collective-permute-done.16.refs_0_ = bf16[64,2048]{1,0:T(8,128)(2,1)S(1)} collective-permute-done((bf16[64,2048]{1,0:T(8,128)(2,1)S(1)}, bf16[64,2048]{1,0:T(8,128)(2,1)S(1)}, u32[]{:S(2)}, u32[]{:S(2)}) %collective-permute-start.16) | collective-permute-done | bytes 262176 | tf_op jit(solution)/shard_map/ppermute | solution.py:36
  123.0 3.5 %shard_map.88 = (bf16[4,32,2048]{2,1,0:T(8,128)(2,1)S(1)}, bf16[4,32,2048]{2,1,0:T(8,128)(2,1)S(1)}) custom-call(s32[2]{0:T(128)S(1)} %pad_add_fusion.s_ref, s32[16,16]{1,0:T(8,128)} %m_ref.3, bf16[64,2048]{1,0:T(8,128)(2,1)S(1)} %collective-permute-done.16.refs_0_, bf16[64,2048]{1,0:T(8,128)(2,1)S(1)} %collective-permute-done.11.refs_1_, ...), custom_call_target="tpu_custom_call" | custom-call | tf_op jit(solution)/shard_map/pallas_call | solution.py:177
  126.5 0.1 collective-permute-start.17
  126.6 0.1 collective-permute-start.22
  126.7 2.0 %collective-permute-start.23 = (bf16[64,2048]{1,0:T(8,128)(2,1)S(1)}, bf16[64,2048]{1,0:T(8,128)(2,1)S(1)}, u32[]{:S(2)}, u32[]{:S(2)}) collective-permute-start(bf16[64,2048]{1,0:T(8,128)(2,1)S(1)} %fusion.1.refs_3_), channel_id=1, source_target_pairs={{0,8},{8,0},{16,24},{24,16},{1,9},{9,1},{17,25},{25,17},{2,10},{10... | collective-permute-start | bytes 786440 | tf_op jit(solution)/shard_map/ppermute | solution.py:36
  128.7 7.1 %collective-permute-done.22.refs_0_ = bf16[64,2048]{1,0:T(8,128)(2,1)S(1)} collective-permute-done((bf16[64,2048]{1,0:T(8,128)(2,1)S(1)}, bf16[64,2048]{1,0:T(8,128)(2,1)S(1)}, u32[]{:S(2)}, u32[]{:S(2)}) %collective-permute-start.22) | collective-permute-done | bytes 262176 | tf_op jit(solution)/shard_map/ppermute | solution.py:36
  135.8 5.2 %collective-permute-done.23.refs_2_ = bf16[64,2048]{1,0:T(8,128)(2,1)S(1)} collective-permute-done((bf16[64,2048]{1,0:T(8,128)(2,1)S(1)}, bf16[64,2048]{1,0:T(8,128)(2,1)S(1)}, u32[]{:S(2)}, u32[]{:S(2)}) %collective-permute-start.23) | collective-permute-done | bytes 262176 | tf_op jit(solution)/shard_map/ppermute | solution.py:36
  140.9 3.3 %shard_map.89 = (bf16[4,32,2048]{2,1,0:T(8,128)(2,1)S(1)}, bf16[4,32,2048]{2,1,0:T(8,128)(2,1)S(1)}) custom-call(s32[2]{0:T(128)S(1)} %pad_add_fusion.s_ref, s32[16,16]{1,0:T(8,128)} %m_ref.3, bf16[64,2048]{1,0:T(8,128)(2,1)S(1)} %collective-permute-done.22.refs_0_, bf16[64,2048]{1,0:T(8,128)(2,1)S(1)} %collective-permute-done.21.refs_1_, ...), custom_call_target="tpu_custom_call" | custom-call | tf_op jit(solution)/shard_map/pallas_call | solution.py:177
  144.2 0.1 collective-permute-start.24
  144.3 0.1 add_convert_fusion.1
  144.5 0.6 collective-permute-start.18
  145.1 1.5 collective-permute-start.20
  146.6 1.5 collective-permute-start.19
  148.0 0.1 add_convert_fusion
  148.2 0.6 collective-permute-start.25
  148.8 1.5 collective-permute-start.27
  150.3 0.5 collective-permute-done.18
  150.8 0.9 collective-permute-start.26
  151.8 1.9 %collective-permute-done.20 = bf16[32,2048]{1,0:T(8,128)(2,1)S(1)} collective-permute-done((bf16[32,2048]{1,0:T(8,128)(2,1)S(1)}, bf16[32,2048]{1,0:T(8,128)(2,1)S(1)}, u32[]{:S(2)}, u32[]{:S(2)}) %collective-permute-start.20) | collective-permute-done | bytes 131104 | tf_op jit(solution)/shard_map/ppermute | solution.py:36
  153.7 2.0 %collective-permute-done.19 = bf16[32,2048]{1,0:T(8,128)(2,1)S(1)} collective-permute-done((bf16[32,2048]{1,0:T(8,128)(2,1)S(1)}, bf16[32,2048]{1,0:T(8,128)(2,1)S(1)}, u32[]{:S(2)}, u32[]{:S(2)}) %collective-permute-start.19) | collective-permute-done | bytes 131104 | tf_op jit(solution)/shard_map/ppermute | solution.py:36
  155.8 0.7 collective-permute-done.25
  156.5 2.5 %collective-permute-done.27 = bf16[32,2048]{1,0:T(8,128)(2,1)S(1)} collective-permute-done((bf16[32,2048]{1,0:T(8,128)(2,1)S(1)}, bf16[32,2048]{1,0:T(8,128)(2,1)S(1)}, u32[]{:S(2)}, u32[]{:S(2)}) %collective-permute-start.27) | collective-permute-done | bytes 131104 | tf_op jit(solution)/shard_map/ppermute | solution.py:36
  159.0 1.3 collective-permute-done.26
  160.4 0.7 pad_maximum_fusion.1
  (30 shorter events, 0.4 us)
Async XLA Ops:
  1.9 20.6 %collective-permute-start = (bf16[128,1024]{1,0:T(8,128)(2,1)S(1)}, bf16[128,1024]{1,0:T(8,128)(2,1)S(1)}, u32[]{:S(2)}, u32[]{:S(2)}) collective-permute-start(bf16[128,1024]{1,0:T(8,128)(2,1)S(1)} %constant_dynamic-slice_fusion.2), channel_id=1, source_target_pairs={{0,8},{8,0},{16,24},{24,16},{1,9},{9,1},{17,25},{25,17},{2,10},{10... | collective-permute-start | bytes 786440 | tf_op jit(solution)/shard_map/ppermute | solution.py:36
  5.0 17.5 %collective-permute-start.1 = (bf16[128,256]{1,0:T(8,128)(2,1)S(1)}, bf16[128,256]{1,0:T(8,128)(2,1)S(1)}, u32[]{:S(2)}, u32[]{:S(2)}) collective-permute-start(bf16[128,256]{1,0:T(8,128)(2,1)S(1)} %get-tuple-element.38), channel_id=1, source_target_pairs={{0,16},{8,24},{16,0},{24,8},{1,17},{9,25},{17,1},{25,9},{2,18},{10... | collective-permute-start | bytes 196616 | tf_op jit(solution)/shard_map/ppermute | solution.py:36
  7.5 14.9 %collective-permute-start.2 = (bf16[128,256]{1,0:T(8,128)(2,1)S(1)}, bf16[128,256]{1,0:T(8,128)(2,1)S(1)}, u32[]{:S(2)}, u32[]{:S(2)}) collective-permute-start(bf16[128,256]{1,0:T(8,128)(2,1)S(1)} %get-tuple-element.39), channel_id=1, source_target_pairs={{0,24},{8,16},{16,8},{24,0},{1,25},{9,17},{17,9},{25,1},{2,26},{10... | collective-permute-start | bytes 196616 | tf_op jit(solution)/shard_map/ppermute | solution.py:36
  7.5 19.4 %copy-start.4 = (s32[8]{0:T(128)S(1)}, s32[8]{0:T(128)}, u32[]{:S(2)}) copy-start(s32[8]{0:T(128)} %constant.66.clone) | copy-start | bytes 100
  15.9 3.3 %copy-start = (bf16[2048,2048]{1,0:T(8,128)(2,1)}, bf16[2048,2048]{1,0:T(8,128)(2,1)S(1)}, u32[]{:S(2)}) copy-start(bf16[2048,2048]{1,0:T(8,128)(2,1)S(1)} %get-tuple-element.44.gv_ref) | copy-start | bytes 25165828
  19.2 3.3 %copy-start.2 = (bf16[2048,2048]{1,0:T(8,128)(2,1)}, bf16[2048,2048]{1,0:T(8,128)(2,1)S(1)}, u32[]{:S(2)}) copy-start(bf16[2048,2048]{1,0:T(8,128)(2,1)S(1)} %get-tuple-element.45.uv_ref) | copy-start | bytes 25165828
  22.4 21.5 %collective-permute-start.4 = (bf16[2,64,2048]{2,1,0:T(8,128)(2,1)S(1)}, bf16[2,64,2048]{2,1,0:T(8,128)(2,1)S(1)}, u32[]{:S(2)}, u32[]{:S(2)}) collective-permute-start(bf16[2,64,2048]{2,1,0:T(8,128)(2,1)S(1)} %get-tuple-element.47), channel_id=1, source_target_pairs={{0,8},{8,0},{16,24},{24,16},{1,9},{9,1},{17,25},{25,17},{2,10},{10... | collective-permute-start | bytes 1572872 | tf_op jit(solution)/shard_map/ppermute | solution.py:36
  23.4 5.6 %collective-permute-start.7 = (bf16[2,128,256]{2,1,0:T(8,128)(2,1)S(1)}, bf16[2,128,256]{2,1,0:T(8,128)(2,1)S(1)}, u32[]{:S(2)}, u32[]{:S(2)}) collective-permute-start(bf16[2,128,256]{2,1,0:T(8,128)(2,1)S(1)} %get-tuple-element.78), channel_id=1, source_target_pairs={{0,4},{1,5},{2,6},{3,7},{4,0},{5,1},{6,2},{7,3},{8,12},{9,13},{10,... | collective-permute-start | bytes 393224 | tf_op jit(solution)/shard_map/ppermute | solution.py:36
  25.0 5.3 %collective-permute-start.6 = (bf16[2,128,256]{2,1,0:T(8,128)(2,1)S(1)}, bf16[2,128,256]{2,1,0:T(8,128)(2,1)S(1)}, u32[]{:S(2)}, u32[]{:S(2)}) collective-permute-start(bf16[2,128,256]{2,1,0:T(8,128)(2,1)S(1)} %get-tuple-element.78), channel_id=1, source_target_pairs={{0,2},{1,3},{2,0},{3,1},{4,6},{5,7},{6,4},{7,5},{8,10},{9,11},{10,... | collective-permute-start | bytes 393224 | tf_op jit(solution)/shard_map/ppermute | solution.py:36
  26.5 5.9 %collective-permute-start.8 = (bf16[2,128,256]{2,1,0:T(8,128)(2,1)S(1)}, bf16[2,128,256]{2,1,0:T(8,128)(2,1)S(1)}, u32[]{:S(2)}, u32[]{:S(2)}) collective-permute-start(bf16[2,128,256]{2,1,0:T(8,128)(2,1)S(1)} %get-tuple-element.78), channel_id=1, source_target_pairs={{0,6},{1,7},{2,4},{3,5},{4,2},{5,3},{6,0},{7,1},{8,14},{9,15},{10,... | collective-permute-start | bytes 393224 | tf_op jit(solution)/shard_map/ppermute | solution.py:36
  27.0 6.9 %collective-permute-start.3 = (bf16[1,1,128,1024]{3,2,1,0:T(8,128)(2,1)S(1)}, bf16[1,1,128,1024]{3,2,1,0:T(8,128)(2,1)S(1)}, u32[]{:S(2)}, u32[]{:S(2)}) collective-permute-start(bf16[1,1,128,1024]{3,2,1,0:T(8,128)(2,1)S(1)} %bitcast.53), channel_id=1, source_target_pairs={{0,1},{1,0},{2,3},{3,2},{4,5},{5,4},{6,7},{7,6},{8,9},{9,8},{10,11... | collective-permute-start | bytes 786440 | tf_op jit(solution)/shard_map/ppermute | solution.py:36
  32.4 21.6 %collective-permute-start.13 = (bf16[2,64,2048]{2,1,0:T(8,128)(2,1)S(1)}, bf16[2,64,2048]{2,1,0:T(8,128)(2,1)S(1)}, u32[]{:S(2)}, u32[]{:S(2)}) collective-permute-start(bf16[2,64,2048]{2,1,0:T(8,128)(2,1)S(1)} %get-tuple-element.57), channel_id=1, source_target_pairs={{0,8},{8,0},{16,24},{24,16},{1,9},{9,1},{17,25},{25,17},{2,10},{10... | collective-permute-start | bytes 1572872 | tf_op jit(solution)/shard_map/ppermute | solution.py:36
  33.9 12.8 %collective-permute-start.9 = (bf16[4,2,128,256]{3,2,1,0:T(8,128)(2,1)S(1)}, bf16[4,2,128,256]{3,2,1,0:T(8,128)(2,1)S(1)}, u32[]{:S(2)}, u32[]{:S(2)}) collective-permute-start(bf16[4,2,128,256]{3,2,1,0:T(8,128)(2,1)S(1)} %pad_maximum_fusion.even_ref), channel_id=1, source_target_pairs={{0,1},{1,0},{2,3},{3,2},{4,5},{5,4},{6,7},{7,6},{8,9},{9,8},{10,11... | collective-permute-start | bytes 1572872 | tf_op jit(solution)/shard_map/ppermute | solution.py:36
  33.9 3.4 %copy-start.1 = (bf16[2048,2048]{1,0:T(8,128)(2,1)S(1)}, bf16[2048,2048]{1,0:T(8,128)(2,1)}, u32[]{:S(2)}) copy-start(bf16[2048,2048]{1,0:T(8,128)(2,1)} %copy-done) | copy-start | bytes 25165828
  37.3 3.4 %copy-start.3 = (bf16[2048,2048]{1,0:T(8,128)(2,1)S(1)}, bf16[2048,2048]{1,0:T(8,128)(2,1)}, u32[]{:S(2)}) copy-start(bf16[2048,2048]{1,0:T(8,128)(2,1)} %copy-done.2) | copy-start | bytes 25165828
  44.1 27.0 %collective-permute-start.5 = (bf16[2,64,2048]{2,1,0:T(8,128)(2,1)S(1)}, bf16[2,64,2048]{2,1,0:T(8,128)(2,1)S(1)}, u32[]{:S(2)}, u32[]{:S(2)}) collective-permute-start(bf16[2,64,2048]{2,1,0:T(8,128)(2,1)S(1)} %add_convert_fusion.3), channel_id=1, source_target_pairs={{0,16},{8,24},{16,0},{24,8},{1,17},{9,25},{17,1},{25,9},{2,18},{10... | collective-permute-start | bytes 1572872 | tf_op jit(solution)/shard_map/ppermute | solution.py:36
  52.2 26.1 %collective-permute-start.10 = (bf16[2,64,2048]{2,1,0:T(8,128)(2,1)S(1)}, bf16[2,64,2048]{2,1,0:T(8,128)(2,1)S(1)}, u32[]{:S(2)}, u32[]{:S(2)}) collective-permute-start(bf16[2,64,2048]{2,1,0:T(8,128)(2,1)S(1)} %get-tuple-element.53), channel_id=1, source_target_pairs={{0,8},{8,0},{16,24},{24,16},{1,9},{9,1},{17,25},{25,17},{2,10},{10... | collective-permute-start | bytes 1572872 | tf_op jit(solution)/shard_map/ppermute | solution.py:36
  54.1 39.5 %collective-permute-start.14 = (bf16[2,64,2048]{2,1,0:T(8,128)(2,1)S(1)}, bf16[2,64,2048]{2,1,0:T(8,128)(2,1)S(1)}, u32[]{:S(2)}, u32[]{:S(2)}) collective-permute-start(bf16[2,64,2048]{2,1,0:T(8,128)(2,1)S(1)} %add_convert_fusion.2), channel_id=1, source_target_pairs={{0,16},{8,24},{16,0},{24,8},{1,17},{9,25},{17,1},{25,9},{2,18},{10... | collective-permute-start | bytes 1572872 | tf_op jit(solution)/shard_map/ppermute | solution.py:36
  54.2 51.1 %collective-permute-start.15 = (bf16[2,64,2048]{2,1,0:T(8,128)(2,1)S(1)}, bf16[2,64,2048]{2,1,0:T(8,128)(2,1)S(1)}, u32[]{:S(2)}, u32[]{:S(2)}) collective-permute-start(bf16[2,64,2048]{2,1,0:T(8,128)(2,1)S(1)} %get-tuple-element.59), channel_id=1, source_target_pairs={{0,8},{8,0},{16,24},{24,16},{1,9},{9,1},{17,25},{25,17},{2,10},{10... | collective-permute-start | bytes 1572872 | tf_op jit(solution)/shard_map/ppermute | solution.py:36
  78.5 31.7 %collective-permute-start.12 = (bf16[64,2048]{1,0:T(8,128)(2,1)S(1)}, bf16[64,2048]{1,0:T(8,128)(2,1)S(1)}, u32[]{:S(2)}, u32[]{:S(2)}) collective-permute-start(bf16[64,2048]{1,0:T(8,128)(2,1)S(1)} %fusion.3.refs_3_), channel_id=1, source_target_pairs={{0,8},{8,0},{16,24},{24,16},{1,9},{9,1},{17,25},{25,17},{2,10},{10... | collective-permute-start | bytes 786440 | tf_op jit(solution)/shard_map/ppermute | solution.py:36
  78.6 31.6 %collective-permute-start.11 = (bf16[64,2048]{1,0:T(8,128)(2,1)S(1)}, bf16[64,2048]{1,0:T(8,128)(2,1)S(1)}, u32[]{:S(2)}, u32[]{:S(2)}) collective-permute-start(bf16[64,2048]{1,0:T(8,128)(2,1)S(1)} %fusion.3.refs_3_), channel_id=1, source_target_pairs={{0,16},{8,24},{16,0},{24,8},{1,17},{9,25},{17,1},{25,9},{2,18},{10... | collective-permute-start | bytes 786440 | tf_op jit(solution)/shard_map/ppermute | solution.py:36
  110.3 12.8 %collective-permute-start.16 = (bf16[64,2048]{1,0:T(8,128)(2,1)S(1)}, bf16[64,2048]{1,0:T(8,128)(2,1)S(1)}, u32[]{:S(2)}, u32[]{:S(2)}) collective-permute-start(bf16[64,2048]{1,0:T(8,128)(2,1)S(1)} %collective-permute-done.11.refs_1_), channel_id=1, source_target_pairs={{0,8},{8,0},{16,24},{24,16},{1,9},{9,1},{17,25},{25,17},{2,10},{10... | collective-permute-start | bytes 786440 | tf_op jit(solution)/shard_map/ppermute | solution.py:36
  110.4 16.2 %collective-permute-start.21 = (bf16[64,2048]{1,0:T(8,128)(2,1)S(1)}, bf16[64,2048]{1,0:T(8,128)(2,1)S(1)}, u32[]{:S(2)}, u32[]{:S(2)}) collective-permute-start(bf16[64,2048]{1,0:T(8,128)(2,1)S(1)} %fusion.1.refs_3_), channel_id=1, source_target_pairs={{0,16},{8,24},{16,0},{24,8},{1,17},{9,25},{17,1},{25,9},{2,18},{10... | collective-permute-start | bytes 786440 | tf_op jit(solution)/shard_map/ppermute | solution.py:36
  126.5 17.8 %collective-permute-start.17 = (bf16[4,32,2048]{2,1,0:T(8,128)(2,1)S(1)}, bf16[4,32,2048]{2,1,0:T(8,128)(2,1)S(1)}, u32[]{:S(2)}, u32[]{:S(2)}) collective-permute-start(bf16[4,32,2048]{2,1,0:T(8,128)(2,1)S(1)} %get-tuple-element.65), channel_id=1, source_target_pairs={{0,1},{1,0},{2,3},{3,2},{4,5},{5,4},{6,7},{7,6},{8,9},{9,8},{10,11... | collective-permute-start | bytes 1572872 | tf_op jit(solution)/shard_map/ppermute | solution.py:36
  126.6 9.2 %collective-permute-start.22 = (bf16[64,2048]{1,0:T(8,128)(2,1)S(1)}, bf16[64,2048]{1,0:T(8,128)(2,1)S(1)}, u32[]{:S(2)}, u32[]{:S(2)}) collective-permute-start(bf16[64,2048]{1,0:T(8,128)(2,1)S(1)} %collective-permute-done.21.refs_1_), channel_id=1, source_target_pairs={{0,8},{8,0},{16,24},{24,16},{1,9},{9,1},{17,25},{25,17},{2,10},{10... | collective-permute-start | bytes 786440 | tf_op jit(solution)/shard_map/ppermute | solution.py:36
  126.7 14.3 %collective-permute-start.23 = (bf16[64,2048]{1,0:T(8,128)(2,1)S(1)}, bf16[64,2048]{1,0:T(8,128)(2,1)S(1)}, u32[]{:S(2)}, u32[]{:S(2)}) collective-permute-start(bf16[64,2048]{1,0:T(8,128)(2,1)S(1)} %fusion.1.refs_3_), channel_id=1, source_target_pairs={{0,8},{8,0},{16,24},{24,16},{1,9},{9,1},{17,25},{25,17},{2,10},{10... | collective-permute-start | bytes 786440 | tf_op jit(solution)/shard_map/ppermute | solution.py:36
  144.2 3.8 %collective-permute-start.24 = (bf16[4,32,2048]{2,1,0:T(8,128)(2,1)S(1)}, bf16[4,32,2048]{2,1,0:T(8,128)(2,1)S(1)}, u32[]{:S(2)}, u32[]{:S(2)}) collective-permute-start(bf16[4,32,2048]{2,1,0:T(8,128)(2,1)S(1)} %get-tuple-element.68), channel_id=1, source_target_pairs={{0,1},{1,0},{2,3},{3,2},{4,5},{5,4},{6,7},{7,6},{8,9},{9,8},{10,11... | collective-permute-start | bytes 1572872 | tf_op jit(solution)/shard_map/ppermute | solution.py:36
  144.5 6.4 %collective-permute-start.18 = (bf16[32,2048]{1,0:T(8,128)(2,1)S(1)}, bf16[32,2048]{1,0:T(8,128)(2,1)S(1)}, u32[]{:S(2)}, u32[]{:S(2)}) collective-permute-start(bf16[32,2048]{1,0:T(8,128)(2,1)S(1)} %get-tuple-element.71), channel_id=1, source_target_pairs={{0,2},{1,3},{2,0},{3,1},{4,6},{5,7},{6,4},{7,5},{8,10},{9,11},{10,... | collective-permute-start | bytes 393224 | tf_op jit(solution)/shard_map/ppermute | solution.py:36
  145.1 8.6 %collective-permute-start.20 = (bf16[32,2048]{1,0:T(8,128)(2,1)S(1)}, bf16[32,2048]{1,0:T(8,128)(2,1)S(1)}, u32[]{:S(2)}, u32[]{:S(2)}) collective-permute-start(bf16[32,2048]{1,0:T(8,128)(2,1)S(1)} %get-tuple-element.72), channel_id=1, source_target_pairs={{0,6},{1,7},{2,4},{3,5},{4,2},{5,3},{6,0},{7,1},{8,14},{9,15},{10,... | collective-permute-start | bytes 393224 | tf_op jit(solution)/shard_map/ppermute | solution.py:36
  146.6 9.1 %collective-permute-start.19 = (bf16[32,2048]{1,0:T(8,128)(2,1)S(1)}, bf16[32,2048]{1,0:T(8,128)(2,1)S(1)}, u32[]{:S(2)}, u32[]{:S(2)}) collective-permute-start(bf16[32,2048]{1,0:T(8,128)(2,1)S(1)} %get-tuple-element.73), channel_id=1, source_target_pairs={{0,4},{1,5},{2,6},{3,7},{4,0},{5,1},{6,2},{7,3},{8,12},{9,13},{10,... | collective-permute-start | bytes 393224 | tf_op jit(solution)/shard_map/ppermute | solution.py:36
  148.2 8.3 %collective-permute-start.25 = (bf16[32,2048]{1,0:T(8,128)(2,1)S(1)}, bf16[32,2048]{1,0:T(8,128)(2,1)S(1)}, u32[]{:S(2)}, u32[]{:S(2)}) collective-permute-start(bf16[32,2048]{1,0:T(8,128)(2,1)S(1)} %get-tuple-element.74), channel_id=1, source_target_pairs={{0,2},{1,3},{2,0},{3,1},{4,6},{5,7},{6,4},{7,5},{8,10},{9,11},{10,... | collective-permute-start | bytes 393224 | tf_op jit(solution)/shard_map/ppermute | solution.py:36
  148.8 10.2 %collective-permute-start.27 = (bf16[32,2048]{1,0:T(8,128)(2,1)S(1)}, bf16[32,2048]{1,0:T(8,128)(2,1)S(1)}, u32[]{:S(2)}, u32[]{:S(2)}) collective-permute-start(bf16[32,2048]{1,0:T(8,128)(2,1)S(1)} %get-tuple-element.75), channel_id=1, source_target_pairs={{0,6},{1,7},{2,4},{3,5},{4,2},{5,3},{6,0},{7,1},{8,14},{9,15},{10,... | collective-permute-start | bytes 393224 | tf_op jit(solution)/shard_map/ppermute | solution.py:36
  150.8 9.5 %collective-permute-start.26 = (bf16[32,2048]{1,0:T(8,128)(2,1)S(1)}, bf16[32,2048]{1,0:T(8,128)(2,1)S(1)}, u32[]{:S(2)}, u32[]{:S(2)}) collective-permute-start(bf16[32,2048]{1,0:T(8,128)(2,1)S(1)} %get-tuple-element.76), channel_id=1, source_target_pairs={{0,4},{1,5},{2,6},{3,7},{4,0},{5,1},{6,2},{7,3},{8,12},{9,13},{10,... | collective-permute-start | bytes 393224 | tf_op jit(solution)/shard_map/ppermute | solution.py:36

commit v5 on v4

--- a/solution.py
+++ b/solution.py
@@ -9,7 +9,8 @@
 
 BLOCK = 256
 PARTS = (1, 1)
-WEIGHT = 2.0
+SUM_COST = 2.0
+DOWN_COST = 3.0
 VMEM_BYTES = 16 << 20
 VMEM = pl.BlockSpec(memory_space=pltpu.VMEM)
 SMEM = pl.BlockSpec(memory_space=pltpu.SMEM)
@@ -170,7 +171,7 @@
             give_ref[e, :, start : start + width] = jnp.where(first, high, low)
 
 
-def down_partial(scalars, hidden, weight, mask):
+def down_partial(scalars, hidden, weight, mask, wait):
     n_row = len(hidden)
     rows, panel = hidden[0].shape
     cols = weight.shape[1]
@@ -181,7 +182,7 @@
         out_shape=[new(n_row, rows // 2, cols)] * 2,
         scratch_shapes=[new(n_row * rows, panel)],
         compiler_params=params(),
-        cost_estimate=pl.CostEstimate(flops=0, bytes_accessed=0, transcendentals=0),
+        cost_estimate=pl.CostEstimate(flops=int(wait * 1.15e9), bytes_accessed=0, transcendentals=0),
     )(scalars, in_hbm(mask), *map(in_vmem, hidden), in_vmem(weight))
 
 
@@ -196,7 +197,7 @@
         out_specs=VMEM,
         out_shape=pltpu.VMEM(a.shape, jnp.float32),
         compiler_params=params(),
-        cost_estimate=pl.CostEstimate(flops=int(WEIGHT * 1.15e9), bytes_accessed=0, transcendentals=0),
+        cost_estimate=pl.CostEstimate(flops=int(SUM_COST * 1.15e9), bytes_accessed=0, transcendentals=0),
     )(in_vmem(a), in_vmem(b))
 
 
@@ -269,7 +270,7 @@
 
     result = []
     for k, hidden in enumerate(hiddens):
-        keep, give = down_partial(place, hidden, down_weight, down_mask)
+        keep, give = down_partial(place, hidden, down_weight, down_mask, DOWN_COST if k else 0)
         share = add(keep, swap(give, "col", n_col, 1)).astype(jnp.bfloat16)
         came = [swap(share[e], "col", n_col, 2 * e) for e in range(1, n_row)]
         result.append(add(share[0], *came).astype(jnp.bfloat16))

time: 162 us -> 144 us (0.89)
  local copies, waits for them, and re-layouts: 15.2 us -> 1.92 us
  waiting for transfers between devices: 85.1 us -> 79.9 us
    unnamed x10 -> x2, local copies, waits for them, and re-layouts: 13.3 us -> 0.01 us
    ppermute x28, waiting for transfers between devices: 85.1 us -> 79.9 us  [swap(): return lax.ppermute(value, axis, [(i, i ^ mask) for i in range(size)])]
  transfers between devices with their start and end apart: 28 -> 28, of which waited for: 17 -> 17; matrix products, arithmetic and copies ran while one was open for 1% -> 1% of each run, Pallas kernels for 17% -> 20%
where the time goes in v5:
time: 144 us; the launch traced here: 143 us
  waiting for transfers between devices  79.9 us (55%)
  starting transfers between devices  30.8 us (21%)
  Pallas kernels  28.4 us (20%)
  other arithmetic  2.07 us (1%)
  local copies, waits for them, and re-layouts  1.92 us (1%)
    ppermute x28, waiting for transfers between devices, swap(): return lax.ppermute(value, axis, [(i, i ^ mask) for i in range(size)])  79.9 us
    ppermute x28, starting transfers between devices, swap(): return lax.ppermute(value, axis, [(i, i ^ mask) for i in range(size)])  30.8 us
    pallas_call x2, Pallas kernels, others_partial(): pl.pallas_call(functools.partial(others_kernel, groups), in_specs=[SMEM,...  9.28 us
    pallas_call x1, Pallas kernels, own_partial(): pl.pallas_call(own_kernel, in_specs=[SMEM, SMEM, SMEM, HBM, HBM, HBM], ou...  8.2 us
    pallas_call x2, Pallas kernels, down_partial(): pl.pallas_call(functools.partial(down_kernel, n_row), in_specs=[SMEM, SME...  6.77 us
    pallas_call x1, Pallas kernels, load(): pl.pallas_call(load_kernel, in_specs=[SMEM, HBM], out_specs=VMEM, out_sha...  3.93 us
  transfers between devices with their start and end apart: 28, of which 17 were waited for; matrix products, arithmetic and copies ran while one was open for 1% of the time, Pallas kernels for 20%

profile of v5, /device:TPU:0, one launch (start us, length us, event | category | flops | bytes accessed | tf_op | source)
XLA Modules:
  0.0 143.3 jit_solution(18352643794088529366)
XLA Ops:
  0.0 1.0 constant_dynamic-slice_fusion.2
  1.0 0.9 constant_dynamic-slice_fusion
  1.9 3.1 %collective-permute-start = (bf16[128,1024]{1,0:T(8,128)(2,1)S(1)}, bf16[128,1024]{1,0:T(8,128)(2,1)S(1)}, u32[]{:S(2)}, u32[]{:S(2)}) collective-permute-start(bf16[128,1024]{1,0:T(8,128)(2,1)S(1)} %constant_dynamic-slice_fusion.2), channel_id=1, source_target_pairs={{0,8},{8,0},{16,24},{24,16},{1,9},{9,1},{17,25},{25,17},{2,10},{10... | collective-permute-start | bytes 786440 | tf_op jit(solution)/shard_map/ppermute | solution.py:37
  5.0 2.6 %collective-permute-start.1 = (bf16[128,256]{1,0:T(8,128)(2,1)S(1)}, bf16[128,256]{1,0:T(8,128)(2,1)S(1)}, u32[]{:S(2)}, u32[]{:S(2)}) collective-permute-start(bf16[128,256]{1,0:T(8,128)(2,1)S(1)} %get-tuple-element.38), channel_id=1, source_target_pairs={{0,16},{8,24},{16,0},{24,8},{1,17},{9,25},{17,1},{25,9},{2,18},{10... | collective-permute-start | bytes 196616 | tf_op jit(solution)/shard_map/ppermute | solution.py:37
  7.5 8.2 %shard_map.82 = (bf16[2,64,2048]{2,1,0:T(8,128)(2,1)S(1)}, bf16[2,64,2048]{2,1,0:T(8,128)(2,1)S(1)}, bf16[2048,2048]{1,0:T(8,128)(2,1)S(1)}, bf16[2048,2048]{1,0:T(8,128)(2,1)S(1)}) custom-call(s32[1]{0:T(128)} %bitcast.s_ref, s32[16,16]{1,0:T(8,128)} %gm_ref.5, s32[16,16]{1,0:T(8,128)} %um_ref.5, bf16[128,8192]{1,0:T(8,128)(2,1)} %tokens_ref.1, ...), custom_call_target="tpu_custom_call" | custom-call | tf_op jit(solution)/shard_map/pallas_call | solution.py:99
  15.8 0.5 collective-permute-done.2
  16.3 0.5 collective-permute-start.4
  16.8 1.6 %collective-permute-start.7 = (bf16[2,128,256]{2,1,0:T(8,128)(2,1)S(1)}, bf16[2,128,256]{2,1,0:T(8,128)(2,1)S(1)}, u32[]{:S(2)}, u32[]{:S(2)}) collective-permute-start(bf16[2,128,256]{2,1,0:T(8,128)(2,1)S(1)} %get-tuple-element.78), channel_id=1, source_target_pairs={{0,4},{1,5},{2,6},{3,7},{4,0},{5,1},{6,2},{7,3},{8,12},{9,13},{10,... | collective-permute-start | bytes 393224 | tf_op jit(solution)/shard_map/ppermute | solution.py:37
  18.4 1.5 %collective-permute-start.6 = (bf16[2,128,256]{2,1,0:T(8,128)(2,1)S(1)}, bf16[2,128,256]{2,1,0:T(8,128)(2,1)S(1)}, u32[]{:S(2)}, u32[]{:S(2)}) collective-permute-start(bf16[2,128,256]{2,1,0:T(8,128)(2,1)S(1)} %get-tuple-element.78), channel_id=1, source_target_pairs={{0,2},{1,3},{2,0},{3,1},{4,6},{5,7},{6,4},{7,5},{8,10},{9,11},{10,... | collective-permute-start | bytes 393224 | tf_op jit(solution)/shard_map/ppermute | solution.py:37
  19.8 0.5 collective-permute-start.8
  20.3 2.4 %collective-permute-done.7 = bf16[2,128,256]{2,1,0:T(8,128)(2,1)S(1)} collective-permute-done((bf16[2,128,256]{2,1,0:T(8,128)(2,1)S(1)}, bf16[2,128,256]{2,1,0:T(8,128)(2,1)S(1)}, u32[]{:S(2)}, u32[]{:S(2)}) %collective-permute-start.7) | collective-permute-done | bytes 131104 | tf_op jit(solution)/shard_map/ppermute | solution.py:37
  22.7 1.9 %collective-permute-done.6 = bf16[2,128,256]{2,1,0:T(8,128)(2,1)S(1)} collective-permute-done((bf16[2,128,256]{2,1,0:T(8,128)(2,1)S(1)}, bf16[2,128,256]{2,1,0:T(8,128)(2,1)S(1)}, u32[]{:S(2)}, u32[]{:S(2)}) %collective-permute-start.6) | collective-permute-done | bytes 131104 | tf_op jit(solution)/shard_map/ppermute | solution.py:37
  24.7 2.0 %collective-permute-done.8 = bf16[2,128,256]{2,1,0:T(8,128)(2,1)S(1)} collective-permute-done((bf16[2,128,256]{2,1,0:T(8,128)(2,1)S(1)}, bf16[2,128,256]{2,1,0:T(8,128)(2,1)S(1)}, u32[]{:S(2)}, u32[]{:S(2)}) %collective-permute-start.8) | collective-permute-done | bytes 131104 | tf_op jit(solution)/shard_map/ppermute | solution.py:37
  26.7 0.1 pad_maximum_fusion.even_ref
  26.8 1.6 %collective-permute-start.13 = (bf16[2,64,2048]{2,1,0:T(8,128)(2,1)S(1)}, bf16[2,64,2048]{2,1,0:T(8,128)(2,1)S(1)}, u32[]{:S(2)}, u32[]{:S(2)}) collective-permute-start(bf16[2,64,2048]{2,1,0:T(8,128)(2,1)S(1)} %get-tuple-element.57), channel_id=1, source_target_pairs={{0,8},{8,0},{16,24},{24,16},{1,9},{9,1},{17,25},{25,17},{2,10},{10... | collective-permute-start | bytes 1572872 | tf_op jit(solution)/shard_map/ppermute | solution.py:37
  28.4 3.6 %shard_map.83 = (bf16[2,64,2048]{2,1,0:T(8,128)(2,1)S(1)}, bf16[2,64,2048]{2,1,0:T(8,128)(2,1)S(1)}) custom-call(s32[2]{0:T(128)S(1)} %iota_xor_fusion.s_ref, s32[16,16]{1,0:T(8,128)} %gm_ref.5, s32[16,16]{1,0:T(8,128)} %um_ref.5, bf16[1,1,128,1024]{3,2,1,0:T(8,128)(2,1)S(1)} %bitcast.54, bf16[1,1,128,1024]{3,2,1,0:T(8,128)(2,1)S(1)} %collective-permute-done.3.odd_ref, ...), custom_call_target="tpu_custom_call" | custom-call | tf_op jit(solution)/shard_map/pallas_call | solution.py:129
  32.0 0.1 add_convert_fusion.3
  32.1 2.1 %collective-permute-start.5 = (bf16[2,64,2048]{2,1,0:T(8,128)(2,1)S(1)}, bf16[2,64,2048]{2,1,0:T(8,128)(2,1)S(1)}, u32[]{:S(2)}, u32[]{:S(2)}) collective-permute-start(bf16[2,64,2048]{2,1,0:T(8,128)(2,1)S(1)} %add_convert_fusion.3), channel_id=1, source_target_pairs={{0,16},{8,24},{16,0},{24,8},{1,17},{9,25},{17,1},{25,9},{2,18},{10... | collective-permute-start | bytes 1572872 | tf_op jit(solution)/shard_map/ppermute | solution.py:37
  34.3 5.7 %shard_map.84 = (bf16[2,64,2048]{2,1,0:T(8,128)(2,1)S(1)}, bf16[2,64,2048]{2,1,0:T(8,128)(2,1)S(1)}, bf16[2,64,2048]{2,1,0:T(8,128)(2,1)S(1)}, bf16[2,64,2048]{2,1,0:T(8,128)(2,1)S(1)}) custom-call(s32[8]{0:T(128)S(1)} %broadcast_xor_fusion.s_ref, s32[16,16]{1,0:T(8,128)} %gm_ref.5, s32[16,16]{1,0:T(8,128)} %um_ref.5, ...), custom_call_target="tpu_custom_call" | custom-call | tf_op jit(solution)/shard_map/pallas_call | solution.py:129
  40.0 2.0 %collective-permute-start.10 = (bf16[2,64,2048]{2,1,0:T(8,128)(2,1)S(1)}, bf16[2,64,2048]{2,1,0:T(8,128)(2,1)S(1)}, u32[]{:S(2)}, u32[]{:S(2)}) collective-permute-start(bf16[2,64,2048]{2,1,0:T(8,128)(2,1)S(1)} %get-tuple-element.53), channel_id=1, source_target_pairs={{0,8},{8,0},{16,24},{24,16},{1,9},{9,1},{17,25},{25,17},{2,10},{10... | collective-permute-start | bytes 1572872 | tf_op jit(solution)/shard_map/ppermute | solution.py:37
  42.0 6.8 %collective-permute-done.13 = bf16[2,64,2048]{2,1,0:T(8,128)(2,1)S(1)} collective-permute-done((bf16[2,64,2048]{2,1,0:T(8,128)(2,1)S(1)}, bf16[2,64,2048]{2,1,0:T(8,128)(2,1)S(1)}, u32[]{:S(2)}, u32[]{:S(2)}) %collective-permute-start.13) | collective-permute-done | bytes 524320 | tf_op jit(solution)/shard_map/ppermute | solution.py:37
  48.7 0.1 add_convert_fusion.2
  48.9 0.1 collective-permute-start.14
  48.9 0.5 collective-permute-start.15
  49.5 9.7 %collective-permute-done.5.a_ref = bf16[2,64,2048]{2,1,0:T(8,128)(2,1)S(1)} collective-permute-done((bf16[2,64,2048]{2,1,0:T(8,128)(2,1)S(1)}, bf16[2,64,2048]{2,1,0:T(8,128)(2,1)S(1)}, u32[]{:S(2)}, u32[]{:S(2)}) %collective-permute-start.5) | collective-permute-done | bytes 524320 | tf_op jit(solution)/shard_map/ppermute | solution.py:37
  59.2 0.1 shard_map.85
  59.3 11.9 %collective-permute-done.10 = bf16[2,64,2048]{2,1,0:T(8,128)(2,1)S(1)} collective-permute-done((bf16[2,64,2048]{2,1,0:T(8,128)(2,1)S(1)}, bf16[2,64,2048]{2,1,0:T(8,128)(2,1)S(1)}, u32[]{:S(2)}, u32[]{:S(2)}) %collective-permute-start.10) | collective-permute-done | bytes 524320 | tf_op jit(solution)/shard_map/ppermute | solution.py:37
  71.2 0.1 convert_add_fusion.1
  71.3 0.1 fusion.3.refs_3_
  71.5 0.1 collective-permute-start.12
  71.6 0.5 collective-permute-start.11
  72.1 9.6 %collective-permute-done.14.a_ref = bf16[2,64,2048]{2,1,0:T(8,128)(2,1)S(1)} collective-permute-done((bf16[2,64,2048]{2,1,0:T(8,128)(2,1)S(1)}, bf16[2,64,2048]{2,1,0:T(8,128)(2,1)S(1)}, u32[]{:S(2)}, u32[]{:S(2)}) %collective-permute-start.14) | collective-permute-done | bytes 524320 | tf_op jit(solution)/shard_map/ppermute | solution.py:37
  81.7 0.1 shard_map.86
  81.9 10.4 %collective-permute-done.15 = bf16[2,64,2048]{2,1,0:T(8,128)(2,1)S(1)} collective-permute-done((bf16[2,64,2048]{2,1,0:T(8,128)(2,1)S(1)}, bf16[2,64,2048]{2,1,0:T(8,128)(2,1)S(1)}, u32[]{:S(2)}, u32[]{:S(2)}) %collective-permute-start.15) | collective-permute-done | bytes 524320 | tf_op jit(solution)/shard_map/ppermute | solution.py:37
  92.3 0.1 convert_add_fusion
  92.4 0.1 fusion.1.refs_3_
  92.6 1.1 collective-permute-start.21
  93.7 3.9 %collective-permute-done.12.refs_2_ = bf16[64,2048]{1,0:T(8,128)(2,1)S(1)} collective-permute-done((bf16[64,2048]{1,0:T(8,128)(2,1)S(1)}, bf16[64,2048]{1,0:T(8,128)(2,1)S(1)}, u32[]{:S(2)}, u32[]{:S(2)}) %collective-permute-start.12) | collective-permute-done | bytes 262176 | tf_op jit(solution)/shard_map/ppermute | solution.py:37
  97.5 4.0 %collective-permute-start.16 = (bf16[64,2048]{1,0:T(8,128)(2,1)S(1)}, bf16[64,2048]{1,0:T(8,128)(2,1)S(1)}, u32[]{:S(2)}, u32[]{:S(2)}) collective-permute-start(bf16[64,2048]{1,0:T(8,128)(2,1)S(1)} %collective-permute-done.11.refs_1_), channel_id=1, source_target_pairs={{0,8},{8,0},{16,24},{24,16},{1,9},{9,1},{17,25},{25,17},{2,10},{10... | collective-permute-start | bytes 786440 | tf_op jit(solution)/shard_map/ppermute | solution.py:37
  101.6 8.1 %collective-permute-done.21.refs_1_ = bf16[64,2048]{1,0:T(8,128)(2,1)S(1)} collective-permute-done((bf16[64,2048]{1,0:T(8,128)(2,1)S(1)}, bf16[64,2048]{1,0:T(8,128)(2,1)S(1)}, u32[]{:S(2)}, u32[]{:S(2)}) %collective-permute-start.21) | collective-permute-done | bytes 262176 | tf_op jit(solution)/shard_map/ppermute | solution.py:37
  109.7 0.7 collective-permute-done.16.refs_0_
  110.4 1.3 collective-permute-start.23
  111.7 0.1 pad_add_fusion.s_ref
  111.8 3.9 %shard_map.87.refs_4_ = bf16[2048,2048]{1,0:T(8,128)(2,1)S(1)} custom-call(s32[2]{0:T(128)S(1)} %pad_add_fusion.s_ref, bf16[2048,2048]{1,0:T(8,128)(2,1)} %w_ref.1), custom_call_target="tpu_custom_call" | custom-call | tf_op jit(solution)/shard_map/pallas_call | solution.py:148
  115.8 3.5 %shard_map.88 = (bf16[4,32,2048]{2,1,0:T(8,128)(2,1)S(1)}, bf16[4,32,2048]{2,1,0:T(8,128)(2,1)S(1)}) custom-call(s32[2]{0:T(128)S(1)} %pad_add_fusion.s_ref, s32[16,16]{1,0:T(8,128)} %m_ref.3, bf16[64,2048]{1,0:T(8,128)(2,1)S(1)} %collective-permute-done.16.refs_0_, bf16[64,2048]{1,0:T(8,128)(2,1)S(1)} %collective-permute-done.11.refs_1_, ...), custom_call_target="tpu_custom_call" | custom-call | tf_op jit(solution)/shard_map/pallas_call | solution.py:178
  119.3 0.1 collective-permute-start.17
  119.3 3.0 %collective-permute-done.23.refs_2_ = bf16[64,2048]{1,0:T(8,128)(2,1)S(1)} collective-permute-done((bf16[64,2048]{1,0:T(8,128)(2,1)S(1)}, bf16[64,2048]{1,0:T(8,128)(2,1)S(1)}, u32[]{:S(2)}, u32[]{:S(2)}) %collective-permute-start.23) | collective-permute-done | bytes 262176 | tf_op jit(solution)/shard_map/ppermute | solution.py:37
  122.4 3.3 %shard_map.89 = (bf16[4,32,2048]{2,1,0:T(8,128)(2,1)S(1)}, bf16[4,32,2048]{2,1,0:T(8,128)(2,1)S(1)}) custom-call(s32[2]{0:T(128)S(1)} %pad_add_fusion.s_ref, s32[16,16]{1,0:T(8,128)} %m_ref.3, bf16[64,2048]{1,0:T(8,128)(2,1)S(1)} %collective-permute-done.22.refs_0_, bf16[64,2048]{1,0:T(8,128)(2,1)S(1)} %collective-permute-done.21.refs_1_, ...), custom_call_target="tpu_custom_call" | custom-call | flops 3449999872 | tf_op jit(solution)/shard_map/pallas_call | solution.py:178
  125.7 0.1 collective-permute-start.24
  125.8 0.1 add_convert_fusion.1
  125.9 1.3 collective-permute-start.18
  127.3 1.5 %collective-permute-start.20 = (bf16[32,2048]{1,0:T(8,128)(2,1)S(1)}, bf16[32,2048]{1,0:T(8,128)(2,1)S(1)}, u32[]{:S(2)}, u32[]{:S(2)}) collective-permute-start(bf16[32,2048]{1,0:T(8,128)(2,1)S(1)} %get-tuple-element.72), channel_id=1, source_target_pairs={{0,6},{1,7},{2,4},{3,5},{4,2},{5,3},{6,0},{7,1},{8,14},{9,15},{10,... | collective-permute-start | bytes 393224 | tf_op jit(solution)/shard_map/ppermute | solution.py:37
  128.8 0.7 collective-permute-start.19
  129.5 0.1 add_convert_fusion
  129.7 1.3 collective-permute-start.25
  131.0 1.5 %collective-permute-start.27 = (bf16[32,2048]{1,0:T(8,128)(2,1)S(1)}, bf16[32,2048]{1,0:T(8,128)(2,1)S(1)}, u32[]{:S(2)}, u32[]{:S(2)}) collective-permute-start(bf16[32,2048]{1,0:T(8,128)(2,1)S(1)} %get-tuple-element.75), channel_id=1, source_target_pairs={{0,6},{1,7},{2,4},{3,5},{4,2},{5,3},{6,0},{7,1},{8,14},{9,15},{10,... | collective-permute-start | bytes 393224 | tf_op jit(solution)/shard_map/ppermute | solution.py:37
  132.5 1.1 collective-permute-start.26
  133.6 2.3 %collective-permute-done.20 = bf16[32,2048]{1,0:T(8,128)(2,1)S(1)} collective-permute-done((bf16[32,2048]{1,0:T(8,128)(2,1)S(1)}, bf16[32,2048]{1,0:T(8,128)(2,1)S(1)}, u32[]{:S(2)}, u32[]{:S(2)}) %collective-permute-start.20) | collective-permute-done | bytes 131104 | tf_op jit(solution)/shard_map/ppermute | solution.py:37
  135.9 2.0 %collective-permute-done.19 = bf16[32,2048]{1,0:T(8,128)(2,1)S(1)} collective-permute-done((bf16[32,2048]{1,0:T(8,128)(2,1)S(1)}, bf16[32,2048]{1,0:T(8,128)(2,1)S(1)}, u32[]{:S(2)}, u32[]{:S(2)}) %collective-permute-start.19) | collective-permute-done | bytes 131104 | tf_op jit(solution)/shard_map/ppermute | solution.py:37
  137.9 0.1 fusion.9
  138.0 3.2 %collective-permute-done.27 = bf16[32,2048]{1,0:T(8,128)(2,1)S(1)} collective-permute-done((bf16[32,2048]{1,0:T(8,128)(2,1)S(1)}, bf16[32,2048]{1,0:T(8,128)(2,1)S(1)}, u32[]{:S(2)}, u32[]{:S(2)}) %collective-permute-start.27) | collective-permute-done | bytes 131104 | tf_op jit(solution)/shard_map/ppermute | solution.py:37
  141.2 1.3 collective-permute-done.26
  142.5 0.1 fusion.6
  142.6 0.7 pad_maximum_fusion.1
  (22 shorter events, 0.1 us)
Async XLA Ops:
  1.9 14.4 %collective-permute-start = (bf16[128,1024]{1,0:T(8,128)(2,1)S(1)}, bf16[128,1024]{1,0:T(8,128)(2,1)S(1)}, u32[]{:S(2)}, u32[]{:S(2)}) collective-permute-start(bf16[128,1024]{1,0:T(8,128)(2,1)S(1)} %constant_dynamic-slice_fusion.2), channel_id=1, source_target_pairs={{0,8},{8,0},{16,24},{24,16},{1,9},{9,1},{17,25},{25,17},{2,10},{10... | collective-permute-start | bytes 786440 | tf_op jit(solution)/shard_map/ppermute | solution.py:37
  5.0 10.8 %collective-permute-start.1 = (bf16[128,256]{1,0:T(8,128)(2,1)S(1)}, bf16[128,256]{1,0:T(8,128)(2,1)S(1)}, u32[]{:S(2)}, u32[]{:S(2)}) collective-permute-start(bf16[128,256]{1,0:T(8,128)(2,1)S(1)} %get-tuple-element.38), channel_id=1, source_target_pairs={{0,16},{8,24},{16,0},{24,8},{1,17},{9,25},{17,1},{25,9},{2,18},{10... | collective-permute-start | bytes 196616 | tf_op jit(solution)/shard_map/ppermute | solution.py:37
  7.5 8.7 %collective-permute-start.2 = (bf16[128,256]{1,0:T(8,128)(2,1)S(1)}, bf16[128,256]{1,0:T(8,128)(2,1)S(1)}, u32[]{:S(2)}, u32[]{:S(2)}) collective-permute-start(bf16[128,256]{1,0:T(8,128)(2,1)S(1)} %get-tuple-element.39), channel_id=1, source_target_pairs={{0,24},{8,16},{16,8},{24,0},{1,25},{9,17},{17,9},{25,1},{2,26},{10... | collective-permute-start | bytes 196616 | tf_op jit(solution)/shard_map/ppermute | solution.py:37
  16.3 15.7 %collective-permute-start.4 = (bf16[2,64,2048]{2,1,0:T(8,128)(2,1)S(1)}, bf16[2,64,2048]{2,1,0:T(8,128)(2,1)S(1)}, u32[]{:S(2)}, u32[]{:S(2)}) collective-permute-start(bf16[2,64,2048]{2,1,0:T(8,128)(2,1)S(1)} %get-tuple-element.47), channel_id=1, source_target_pairs={{0,8},{8,0},{16,24},{24,16},{1,9},{9,1},{17,25},{25,17},{2,10},{10... | collective-permute-start | bytes 1572872 | tf_op jit(solution)/shard_map/ppermute | solution.py:37
  16.7 11.7 %collective-permute-start.3 = (bf16[1,1,128,1024]{3,2,1,0:T(8,128)(2,1)S(1)}, bf16[1,1,128,1024]{3,2,1,0:T(8,128)(2,1)S(1)}, u32[]{:S(2)}, u32[]{:S(2)}) collective-permute-start(bf16[1,1,128,1024]{3,2,1,0:T(8,128)(2,1)S(1)} %bitcast.53), channel_id=1, source_target_pairs={{0,1},{1,0},{2,3},{3,2},{4,5},{5,4},{6,7},{7,6},{8,9},{9,8},{10,11... | collective-permute-start | bytes 786440 | tf_op jit(solution)/shard_map/ppermute | solution.py:37
  16.8 6.0 %collective-permute-start.7 = (bf16[2,128,256]{2,1,0:T(8,128)(2,1)S(1)}, bf16[2,128,256]{2,1,0:T(8,128)(2,1)S(1)}, u32[]{:S(2)}, u32[]{:S(2)}) collective-permute-start(bf16[2,128,256]{2,1,0:T(8,128)(2,1)S(1)} %get-tuple-element.78), channel_id=1, source_target_pairs={{0,4},{1,5},{2,6},{3,7},{4,0},{5,1},{6,2},{7,3},{8,12},{9,13},{10,... | collective-permute-start | bytes 393224 | tf_op jit(solution)/shard_map/ppermute | solution.py:37
  18.4 6.3 %collective-permute-start.6 = (bf16[2,128,256]{2,1,0:T(8,128)(2,1)S(1)}, bf16[2,128,256]{2,1,0:T(8,128)(2,1)S(1)}, u32[]{:S(2)}, u32[]{:S(2)}) collective-permute-start(bf16[2,128,256]{2,1,0:T(8,128)(2,1)S(1)} %get-tuple-element.78), channel_id=1, source_target_pairs={{0,2},{1,3},{2,0},{3,1},{4,6},{5,7},{6,4},{7,5},{8,10},{9,11},{10,... | collective-permute-start | bytes 393224 | tf_op jit(solution)/shard_map/ppermute | solution.py:37
  19.8 6.9 %collective-permute-start.8 = (bf16[2,128,256]{2,1,0:T(8,128)(2,1)S(1)}, bf16[2,128,256]{2,1,0:T(8,128)(2,1)S(1)}, u32[]{:S(2)}, u32[]{:S(2)}) collective-permute-start(bf16[2,128,256]{2,1,0:T(8,128)(2,1)S(1)} %get-tuple-element.78), channel_id=1, source_target_pairs={{0,6},{1,7},{2,4},{3,5},{4,2},{5,3},{6,0},{7,1},{8,14},{9,15},{10,... | collective-permute-start | bytes 393224 | tf_op jit(solution)/shard_map/ppermute | solution.py:37
  26.8 21.9 %collective-permute-start.13 = (bf16[2,64,2048]{2,1,0:T(8,128)(2,1)S(1)}, bf16[2,64,2048]{2,1,0:T(8,128)(2,1)S(1)}, u32[]{:S(2)}, u32[]{:S(2)}) collective-permute-start(bf16[2,64,2048]{2,1,0:T(8,128)(2,1)S(1)} %get-tuple-element.57), channel_id=1, source_target_pairs={{0,8},{8,0},{16,24},{24,16},{1,9},{9,1},{17,25},{25,17},{2,10},{10... | collective-permute-start | bytes 1572872 | tf_op jit(solution)/shard_map/ppermute | solution.py:37
  28.4 5.8 %collective-permute-start.9 = (bf16[4,2,128,256]{3,2,1,0:T(8,128)(2,1)S(1)}, bf16[4,2,128,256]{3,2,1,0:T(8,128)(2,1)S(1)}, u32[]{:S(2)}, u32[]{:S(2)}) collective-permute-start(bf16[4,2,128,256]{3,2,1,0:T(8,128)(2,1)S(1)} %pad_maximum_fusion.even_ref), channel_id=1, source_target_pairs={{0,1},{1,0},{2,3},{3,2},{4,5},{5,4},{6,7},{7,6},{8,9},{9,8},{10,11... | collective-permute-start | bytes 1572872 | tf_op jit(solution)/shard_map/ppermute | solution.py:37
  28.4 5.8 %copy-start = (s32[8]{0:T(128)S(1)}, s32[8]{0:T(128)}, u32[]{:S(2)}) copy-start(s32[8]{0:T(128)} %constant.66.clone) | copy-start | bytes 100
  32.1 27.1 %collective-permute-start.5 = (bf16[2,64,2048]{2,1,0:T(8,128)(2,1)S(1)}, bf16[2,64,2048]{2,1,0:T(8,128)(2,1)S(1)}, u32[]{:S(2)}, u32[]{:S(2)}) collective-permute-start(bf16[2,64,2048]{2,1,0:T(8,128)(2,1)S(1)} %add_convert_fusion.3), channel_id=1, source_target_pairs={{0,16},{8,24},{16,0},{24,8},{1,17},{9,25},{17,1},{25,9},{2,18},{10... | collective-permute-start | bytes 1572872 | tf_op jit(solution)/shard_map/ppermute | solution.py:37
  40.0 31.2 %collective-permute-start.10 = (bf16[2,64,2048]{2,1,0:T(8,128)(2,1)S(1)}, bf16[2,64,2048]{2,1,0:T(8,128)(2,1)S(1)}, u32[]{:S(2)}, u32[]{:S(2)}) collective-permute-start(bf16[2,64,2048]{2,1,0:T(8,128)(2,1)S(1)} %get-tuple-element.53), channel_id=1, source_target_pairs={{0,8},{8,0},{16,24},{24,16},{1,9},{9,1},{17,25},{25,17},{2,10},{10... | collective-permute-start | bytes 1572872 | tf_op jit(solution)/shard_map/ppermute | solution.py:37
  48.9 32.9 %collective-permute-start.14 = (bf16[2,64,2048]{2,1,0:T(8,128)(2,1)S(1)}, bf16[2,64,2048]{2,1,0:T(8,128)(2,1)S(1)}, u32[]{:S(2)}, u32[]{:S(2)}) collective-permute-start(bf16[2,64,2048]{2,1,0:T(8,128)(2,1)S(1)} %add_convert_fusion.2), channel_id=1, source_target_pairs={{0,16},{8,24},{16,0},{24,8},{1,17},{9,25},{17,1},{25,9},{2,18},{10... | collective-permute-start | bytes 1572872 | tf_op jit(solution)/shard_map/ppermute | solution.py:37
  48.9 43.3 %collective-permute-start.15 = (bf16[2,64,2048]{2,1,0:T(8,128)(2,1)S(1)}, bf16[2,64,2048]{2,1,0:T(8,128)(2,1)S(1)}, u32[]{:S(2)}, u32[]{:S(2)}) collective-permute-start(bf16[2,64,2048]{2,1,0:T(8,128)(2,1)S(1)} %get-tuple-element.59), channel_id=1, source_target_pairs={{0,8},{8,0},{16,24},{24,16},{1,9},{9,1},{17,25},{25,17},{2,10},{10... | collective-permute-start | bytes 1572872 | tf_op jit(solution)/shard_map/ppermute | solution.py:37
  71.5 26.0 %collective-permute-start.12 = (bf16[64,2048]{1,0:T(8,128)(2,1)S(1)}, bf16[64,2048]{1,0:T(8,128)(2,1)S(1)}, u32[]{:S(2)}, u32[]{:S(2)}) collective-permute-start(bf16[64,2048]{1,0:T(8,128)(2,1)S(1)} %fusion.3.refs_3_), channel_id=1, source_target_pairs={{0,8},{8,0},{16,24},{24,16},{1,9},{9,1},{17,25},{25,17},{2,10},{10... | collective-permute-start | bytes 786440 | tf_op jit(solution)/shard_map/ppermute | solution.py:37
  71.6 26.0 %collective-permute-start.11 = (bf16[64,2048]{1,0:T(8,128)(2,1)S(1)}, bf16[64,2048]{1,0:T(8,128)(2,1)S(1)}, u32[]{:S(2)}, u32[]{:S(2)}) collective-permute-start(bf16[64,2048]{1,0:T(8,128)(2,1)S(1)} %fusion.3.refs_3_), channel_id=1, source_target_pairs={{0,16},{8,24},{16,0},{24,8},{1,17},{9,25},{17,1},{25,9},{2,18},{10... | collective-permute-start | bytes 786440 | tf_op jit(solution)/shard_map/ppermute | solution.py:37
  92.6 17.2 %collective-permute-start.21 = (bf16[64,2048]{1,0:T(8,128)(2,1)S(1)}, bf16[64,2048]{1,0:T(8,128)(2,1)S(1)}, u32[]{:S(2)}, u32[]{:S(2)}) collective-permute-start(bf16[64,2048]{1,0:T(8,128)(2,1)S(1)} %fusion.1.refs_3_), channel_id=1, source_target_pairs={{0,16},{8,24},{16,0},{24,8},{1,17},{9,25},{17,1},{25,9},{2,18},{10... | collective-permute-start | bytes 786440 | tf_op jit(solution)/shard_map/ppermute | solution.py:37
  97.5 12.9 %collective-permute-start.16 = (bf16[64,2048]{1,0:T(8,128)(2,1)S(1)}, bf16[64,2048]{1,0:T(8,128)(2,1)S(1)}, u32[]{:S(2)}, u32[]{:S(2)}) collective-permute-start(bf16[64,2048]{1,0:T(8,128)(2,1)S(1)} %collective-permute-done.11.refs_1_), channel_id=1, source_target_pairs={{0,8},{8,0},{16,24},{24,16},{1,9},{9,1},{17,25},{25,17},{2,10},{10... | collective-permute-start | bytes 786440 | tf_op jit(solution)/shard_map/ppermute | solution.py:37
  109.7 9.6 %collective-permute-start.22 = (bf16[64,2048]{1,0:T(8,128)(2,1)S(1)}, bf16[64,2048]{1,0:T(8,128)(2,1)S(1)}, u32[]{:S(2)}, u32[]{:S(2)}) collective-permute-start(bf16[64,2048]{1,0:T(8,128)(2,1)S(1)} %collective-permute-done.21.refs_1_), channel_id=1, source_target_pairs={{0,8},{8,0},{16,24},{24,16},{1,9},{9,1},{17,25},{25,17},{2,10},{10... | collective-permute-start | bytes 786440 | tf_op jit(solution)/shard_map/ppermute | solution.py:37
  110.4 12.0 %collective-permute-start.23 = (bf16[64,2048]{1,0:T(8,128)(2,1)S(1)}, bf16[64,2048]{1,0:T(8,128)(2,1)S(1)}, u32[]{:S(2)}, u32[]{:S(2)}) collective-permute-start(bf16[64,2048]{1,0:T(8,128)(2,1)S(1)} %fusion.1.refs_3_), channel_id=1, source_target_pairs={{0,8},{8,0},{16,24},{24,16},{1,9},{9,1},{17,25},{25,17},{2,10},{10... | collective-permute-start | bytes 786440 | tf_op jit(solution)/shard_map/ppermute | solution.py:37
  119.3 6.5 %collective-permute-start.17 = (bf16[4,32,2048]{2,1,0:T(8,128)(2,1)S(1)}, bf16[4,32,2048]{2,1,0:T(8,128)(2,1)S(1)}, u32[]{:S(2)}, u32[]{:S(2)}) collective-permute-start(bf16[4,32,2048]{2,1,0:T(8,128)(2,1)S(1)} %get-tuple-element.65), channel_id=1, source_target_pairs={{0,1},{1,0},{2,3},{3,2},{4,5},{5,4},{6,7},{7,6},{8,9},{9,8},{10,11... | collective-permute-start | bytes 1572872 | tf_op jit(solution)/shard_map/ppermute | solution.py:37
  125.7 3.8 %collective-permute-start.24 = (bf16[4,32,2048]{2,1,0:T(8,128)(2,1)S(1)}, bf16[4,32,2048]{2,1,0:T(8,128)(2,1)S(1)}, u32[]{:S(2)}, u32[]{:S(2)}) collective-permute-start(bf16[4,32,2048]{2,1,0:T(8,128)(2,1)S(1)} %get-tuple-element.68), channel_id=1, source_target_pairs={{0,1},{1,0},{2,3},{3,2},{4,5},{5,4},{6,7},{7,6},{8,9},{9,8},{10,11... | collective-permute-start | bytes 1572872 | tf_op jit(solution)/shard_map/ppermute | solution.py:37
  125.9 6.6 %collective-permute-start.18 = (bf16[32,2048]{1,0:T(8,128)(2,1)S(1)}, bf16[32,2048]{1,0:T(8,128)(2,1)S(1)}, u32[]{:S(2)}, u32[]{:S(2)}) collective-permute-start(bf16[32,2048]{1,0:T(8,128)(2,1)S(1)} %get-tuple-element.71), channel_id=1, source_target_pairs={{0,2},{1,3},{2,0},{3,1},{4,6},{5,7},{6,4},{7,5},{8,10},{9,11},{10,... | collective-permute-start | bytes 393224 | tf_op jit(solution)/shard_map/ppermute | solution.py:37
  127.3 8.6 %collective-permute-start.20 = (bf16[32,2048]{1,0:T(8,128)(2,1)S(1)}, bf16[32,2048]{1,0:T(8,128)(2,1)S(1)}, u32[]{:S(2)}, u32[]{:S(2)}) collective-permute-start(bf16[32,2048]{1,0:T(8,128)(2,1)S(1)} %get-tuple-element.72), channel_id=1, source_target_pairs={{0,6},{1,7},{2,4},{3,5},{4,2},{5,3},{6,0},{7,1},{8,14},{9,15},{10,... | collective-permute-start | bytes 393224 | tf_op jit(solution)/shard_map/ppermute | solution.py:37
  128.8 9.1 %collective-permute-start.19 = (bf16[32,2048]{1,0:T(8,128)(2,1)S(1)}, bf16[32,2048]{1,0:T(8,128)(2,1)S(1)}, u32[]{:S(2)}, u32[]{:S(2)}) collective-permute-start(bf16[32,2048]{1,0:T(8,128)(2,1)S(1)} %get-tuple-element.73), channel_id=1, source_target_pairs={{0,4},{1,5},{2,6},{3,7},{4,0},{5,1},{6,2},{7,3},{8,12},{9,13},{10,... | collective-permute-start | bytes 393224 | tf_op jit(solution)/shard_map/ppermute | solution.py:37
  129.7 8.3 %collective-permute-start.25 = (bf16[32,2048]{1,0:T(8,128)(2,1)S(1)}, bf16[32,2048]{1,0:T(8,128)(2,1)S(1)}, u32[]{:S(2)}, u32[]{:S(2)}) collective-permute-start(bf16[32,2048]{1,0:T(8,128)(2,1)S(1)} %get-tuple-element.74), channel_id=1, source_target_pairs={{0,2},{1,3},{2,0},{3,1},{4,6},{5,7},{6,4},{7,5},{8,10},{9,11},{10,... | collective-permute-start | bytes 393224 | tf_op jit(solution)/shard_map/ppermute | solution.py:37
  131.0 10.2 %collective-permute-start.27 = (bf16[32,2048]{1,0:T(8,128)(2,1)S(1)}, bf16[32,2048]{1,0:T(8,128)(2,1)S(1)}, u32[]{:S(2)}, u32[]{:S(2)}) collective-permute-start(bf16[32,2048]{1,0:T(8,128)(2,1)S(1)} %get-tuple-element.75), channel_id=1, source_target_pairs={{0,6},{1,7},{2,4},{3,5},{4,2},{5,3},{6,0},{7,1},{8,14},{9,15},{10,... | collective-permute-start | bytes 393224 | tf_op jit(solution)/shard_map/ppermute | solution.py:37
  132.5 10.0 %collective-permute-start.26 = (bf16[32,2048]{1,0:T(8,128)(2,1)S(1)}, bf16[32,2048]{1,0:T(8,128)(2,1)S(1)}, u32[]{:S(2)}, u32[]{:S(2)}) collective-permute-start(bf16[32,2048]{1,0:T(8,128)(2,1)S(1)} %get-tuple-element.76), channel_id=1, source_target_pairs={{0,4},{1,5},{2,6},{3,7},{4,0},{5,1},{6,2},{7,3},{8,12},{9,13},{10,... | collective-permute-start | bytes 393224 | tf_op jit(solution)/shard_map/ppermute | solution.py:37

commit v6 on v5

--- a/solution.py
+++ b/solution.py
@@ -272,7 +272,7 @@
     for k, hidden in enumerate(hiddens):
         keep, give = down_partial(place, hidden, down_weight, down_mask, DOWN_COST if k else 0)
         share = add(keep, swap(give, "col", n_col, 1)).astype(jnp.bfloat16)
-        came = [swap(share[e], "col", n_col, 2 * e) for e in range(1, n_row)]
+        came = [swap(share[e], "col", n_col, 2 * e) for e in range(n_row - 1, 0, -1)]
         result.append(add(share[0], *came).astype(jnp.bfloat16))
     return jnp.concatenate(result)
 

time: 144 us -> 143 us (level)
  waiting for transfers between devices: 79.9 us -> 78.3 us
    ppermute x28, waiting for transfers between devices: 79.9 us -> 78.3 us  [swap(): return lax.ppermute(value, axis, [(i, i ^ mask) for i in range(size)])]
  transfers between devices with their start and end apart: 28 -> 28, of which waited for: 17 -> 19; matrix products, arithmetic and copies ran while one was open for 1% -> 1% of each run, Pallas kernels for 20% -> 20%
where the time goes in v6:
time: 143 us; the launch traced here: 142 us
  waiting for transfers between devices  78.3 us (55%)
  starting transfers between devices  31 us (22%)
  Pallas kernels  28.4 us (20%)
  other arithmetic  2.07 us (1%)
  local copies, waits for them, and re-layouts  1.92 us (1%)
    ppermute x28, waiting for transfers between devices, swap(): return lax.ppermute(value, axis, [(i, i ^ mask) for i in range(size)])  78.3 us
    ppermute x28, starting transfers between devices, swap(): return lax.ppermute(value, axis, [(i, i ^ mask) for i in range(size)])  31 us
    pallas_call x2, Pallas kernels, others_partial(): pl.pallas_call(functools.partial(others_kernel, groups), in_specs=[SMEM,...  9.28 us
    pallas_call x1, Pallas kernels, own_partial(): pl.pallas_call(own_kernel, in_specs=[SMEM, SMEM, SMEM, HBM, HBM, HBM], ou...  8.2 us
    pallas_call x2, Pallas kernels, down_partial(): pl.pallas_call(functools.partial(down_kernel, n_row), in_specs=[SMEM, SME...  6.77 us
    pallas_call x1, Pallas kernels, load(): pl.pallas_call(load_kernel, in_specs=[SMEM, HBM], out_specs=VMEM, out_sha...  3.93 us
  transfers between devices with their start and end apart: 28, of which 19 were waited for; matrix products, arithmetic and copies ran while one was open for 1% of the time, Pallas kernels for 20%

profile of v6, /device:TPU:0, one launch (start us, length us, event | category | flops | bytes accessed | tf_op | source)
XLA Modules:
  0.0 142.0 jit_solution(6894282257028133208)
XLA Ops:
  0.0 1.0 constant_dynamic-slice_fusion.2
  1.0 0.9 constant_dynamic-slice_fusion
  1.9 3.1 %collective-permute-start = (bf16[128,1024]{1,0:T(8,128)(2,1)S(1)}, bf16[128,1024]{1,0:T(8,128)(2,1)S(1)}, u32[]{:S(2)}, u32[]{:S(2)}) collective-permute-start(bf16[128,1024]{1,0:T(8,128)(2,1)S(1)} %constant_dynamic-slice_fusion.2), channel_id=1, source_target_pairs={{0,8},{8,0},{16,24},{24,16},{1,9},{9,1},{17,25},{25,17},{2,10},{10... | collective-permute-start | bytes 786440 | tf_op jit(solution)/shard_map/ppermute | solution.py:37
  5.0 2.6 %collective-permute-start.1 = (bf16[128,256]{1,0:T(8,128)(2,1)S(1)}, bf16[128,256]{1,0:T(8,128)(2,1)S(1)}, u32[]{:S(2)}, u32[]{:S(2)}) collective-permute-start(bf16[128,256]{1,0:T(8,128)(2,1)S(1)} %get-tuple-element.38), channel_id=1, source_target_pairs={{0,16},{8,24},{16,0},{24,8},{1,17},{9,25},{17,1},{25,9},{2,18},{10... | collective-permute-start | bytes 196616 | tf_op jit(solution)/shard_map/ppermute | solution.py:37
  7.5 8.2 %shard_map.82 = (bf16[2,64,2048]{2,1,0:T(8,128)(2,1)S(1)}, bf16[2,64,2048]{2,1,0:T(8,128)(2,1)S(1)}, bf16[2048,2048]{1,0:T(8,128)(2,1)S(1)}, bf16[2048,2048]{1,0:T(8,128)(2,1)S(1)}) custom-call(s32[1]{0:T(128)} %bitcast.s_ref, s32[16,16]{1,0:T(8,128)} %gm_ref.5, s32[16,16]{1,0:T(8,128)} %um_ref.5, bf16[128,8192]{1,0:T(8,128)(2,1)} %tokens_ref.1, ...), custom_call_target="tpu_custom_call" | custom-call | tf_op jit(solution)/shard_map/pallas_call | solution.py:99
  15.8 0.5 collective-permute-done.2
  16.3 0.5 collective-permute-start.4
  16.8 1.6 %collective-permute-start.7 = (bf16[2,128,256]{2,1,0:T(8,128)(2,1)S(1)}, bf16[2,128,256]{2,1,0:T(8,128)(2,1)S(1)}, u32[]{:S(2)}, u32[]{:S(2)}) collective-permute-start(bf16[2,128,256]{2,1,0:T(8,128)(2,1)S(1)} %get-tuple-element.78), channel_id=1, source_target_pairs={{0,4},{1,5},{2,6},{3,7},{4,0},{5,1},{6,2},{7,3},{8,12},{9,13},{10,... | collective-permute-start | bytes 393224 | tf_op jit(solution)/shard_map/ppermute | solution.py:37
  18.4 1.5 %collective-permute-start.6 = (bf16[2,128,256]{2,1,0:T(8,128)(2,1)S(1)}, bf16[2,128,256]{2,1,0:T(8,128)(2,1)S(1)}, u32[]{:S(2)}, u32[]{:S(2)}) collective-permute-start(bf16[2,128,256]{2,1,0:T(8,128)(2,1)S(1)} %get-tuple-element.78), channel_id=1, source_target_pairs={{0,2},{1,3},{2,0},{3,1},{4,6},{5,7},{6,4},{7,5},{8,10},{9,11},{10,... | collective-permute-start | bytes 393224 | tf_op jit(solution)/shard_map/ppermute | solution.py:37
  19.8 0.5 collective-permute-start.8
  20.3 2.4 %collective-permute-done.7 = bf16[2,128,256]{2,1,0:T(8,128)(2,1)S(1)} collective-permute-done((bf16[2,128,256]{2,1,0:T(8,128)(2,1)S(1)}, bf16[2,128,256]{2,1,0:T(8,128)(2,1)S(1)}, u32[]{:S(2)}, u32[]{:S(2)}) %collective-permute-start.7) | collective-permute-done | bytes 131104 | tf_op jit(solution)/shard_map/ppermute | solution.py:37
  22.7 1.9 %collective-permute-done.6 = bf16[2,128,256]{2,1,0:T(8,128)(2,1)S(1)} collective-permute-done((bf16[2,128,256]{2,1,0:T(8,128)(2,1)S(1)}, bf16[2,128,256]{2,1,0:T(8,128)(2,1)S(1)}, u32[]{:S(2)}, u32[]{:S(2)}) %collective-permute-start.6) | collective-permute-done | bytes 131104 | tf_op jit(solution)/shard_map/ppermute | solution.py:37
  24.7 2.0 %collective-permute-done.8 = bf16[2,128,256]{2,1,0:T(8,128)(2,1)S(1)} collective-permute-done((bf16[2,128,256]{2,1,0:T(8,128)(2,1)S(1)}, bf16[2,128,256]{2,1,0:T(8,128)(2,1)S(1)}, u32[]{:S(2)}, u32[]{:S(2)}) %collective-permute-start.8) | collective-permute-done | bytes 131104 | tf_op jit(solution)/shard_map/ppermute | solution.py:37
  26.8 1.6 %collective-permute-start.13 = (bf16[2,64,2048]{2,1,0:T(8,128)(2,1)S(1)}, bf16[2,64,2048]{2,1,0:T(8,128)(2,1)S(1)}, u32[]{:S(2)}, u32[]{:S(2)}) collective-permute-start(bf16[2,64,2048]{2,1,0:T(8,128)(2,1)S(1)} %get-tuple-element.57), channel_id=1, source_target_pairs={{0,8},{8,0},{16,24},{24,16},{1,9},{9,1},{17,25},{25,17},{2,10},{10... | collective-permute-start | bytes 1572872 | tf_op jit(solution)/shard_map/ppermute | solution.py:37
  28.4 3.6 %shard_map.83 = (bf16[2,64,2048]{2,1,0:T(8,128)(2,1)S(1)}, bf16[2,64,2048]{2,1,0:T(8,128)(2,1)S(1)}) custom-call(s32[2]{0:T(128)S(1)} %iota_xor_fusion.s_ref, s32[16,16]{1,0:T(8,128)} %gm_ref.5, s32[16,16]{1,0:T(8,128)} %um_ref.5, bf16[1,1,128,1024]{3,2,1,0:T(8,128)(2,1)S(1)} %bitcast.54, bf16[1,1,128,1024]{3,2,1,0:T(8,128)(2,1)S(1)} %collective-permute-done.3.odd_ref, ...), custom_call_target="tpu_custom_call" | custom-call | tf_op jit(solution)/shard_map/pallas_call | solution.py:129
  32.0 0.1 add_convert_fusion.3
  32.1 2.1 %collective-permute-start.5 = (bf16[2,64,2048]{2,1,0:T(8,128)(2,1)S(1)}, bf16[2,64,2048]{2,1,0:T(8,128)(2,1)S(1)}, u32[]{:S(2)}, u32[]{:S(2)}) collective-permute-start(bf16[2,64,2048]{2,1,0:T(8,128)(2,1)S(1)} %add_convert_fusion.3), channel_id=1, source_target_pairs={{0,16},{8,24},{16,0},{24,8},{1,17},{9,25},{17,1},{25,9},{2,18},{10... | collective-permute-start | bytes 1572872 | tf_op jit(solution)/shard_map/ppermute | solution.py:37
  34.3 5.7 %shard_map.84 = (bf16[2,64,2048]{2,1,0:T(8,128)(2,1)S(1)}, bf16[2,64,2048]{2,1,0:T(8,128)(2,1)S(1)}, bf16[2,64,2048]{2,1,0:T(8,128)(2,1)S(1)}, bf16[2,64,2048]{2,1,0:T(8,128)(2,1)S(1)}) custom-call(s32[8]{0:T(128)S(1)} %broadcast_xor_fusion.s_ref, s32[16,16]{1,0:T(8,128)} %gm_ref.5, s32[16,16]{1,0:T(8,128)} %um_ref.5, ...), custom_call_target="tpu_custom_call" | custom-call | tf_op jit(solution)/shard_map/pallas_call | solution.py:129
  40.0 2.0 %collective-permute-start.10 = (bf16[2,64,2048]{2,1,0:T(8,128)(2,1)S(1)}, bf16[2,64,2048]{2,1,0:T(8,128)(2,1)S(1)}, u32[]{:S(2)}, u32[]{:S(2)}) collective-permute-start(bf16[2,64,2048]{2,1,0:T(8,128)(2,1)S(1)} %get-tuple-element.53), channel_id=1, source_target_pairs={{0,8},{8,0},{16,24},{24,16},{1,9},{9,1},{17,25},{25,17},{2,10},{10... | collective-permute-start | bytes 1572872 | tf_op jit(solution)/shard_map/ppermute | solution.py:37
  42.0 6.8 %collective-permute-done.13 = bf16[2,64,2048]{2,1,0:T(8,128)(2,1)S(1)} collective-permute-done((bf16[2,64,2048]{2,1,0:T(8,128)(2,1)S(1)}, bf16[2,64,2048]{2,1,0:T(8,128)(2,1)S(1)}, u32[]{:S(2)}, u32[]{:S(2)}) %collective-permute-start.13) | collective-permute-done | bytes 524320 | tf_op jit(solution)/shard_map/ppermute | solution.py:37
  48.7 0.1 add_convert_fusion.2
  48.9 0.1 collective-permute-start.14
  48.9 0.5 collective-permute-start.15
  49.5 9.7 %collective-permute-done.5.a_ref = bf16[2,64,2048]{2,1,0:T(8,128)(2,1)S(1)} collective-permute-done((bf16[2,64,2048]{2,1,0:T(8,128)(2,1)S(1)}, bf16[2,64,2048]{2,1,0:T(8,128)(2,1)S(1)}, u32[]{:S(2)}, u32[]{:S(2)}) %collective-permute-start.5) | collective-permute-done | bytes 524320 | tf_op jit(solution)/shard_map/ppermute | solution.py:37
  59.2 0.1 shard_map.85
  59.3 11.9 %collective-permute-done.10 = bf16[2,64,2048]{2,1,0:T(8,128)(2,1)S(1)} collective-permute-done((bf16[2,64,2048]{2,1,0:T(8,128)(2,1)S(1)}, bf16[2,64,2048]{2,1,0:T(8,128)(2,1)S(1)}, u32[]{:S(2)}, u32[]{:S(2)}) %collective-permute-start.10) | collective-permute-done | bytes 524320 | tf_op jit(solution)/shard_map/ppermute | solution.py:37
  71.2 0.1 convert_add_fusion.1
  71.3 0.1 fusion.3.refs_3_
  71.5 0.1 collective-permute-start.12
  71.6 0.5 collective-permute-start.11
  72.1 9.6 %collective-permute-done.14.a_ref = bf16[2,64,2048]{2,1,0:T(8,128)(2,1)S(1)} collective-permute-done((bf16[2,64,2048]{2,1,0:T(8,128)(2,1)S(1)}, bf16[2,64,2048]{2,1,0:T(8,128)(2,1)S(1)}, u32[]{:S(2)}, u32[]{:S(2)}) %collective-permute-start.14) | collective-permute-done | bytes 524320 | tf_op jit(solution)/shard_map/ppermute | solution.py:37
  81.7 0.1 shard_map.86
  81.9 10.4 %collective-permute-done.15 = bf16[2,64,2048]{2,1,0:T(8,128)(2,1)S(1)} collective-permute-done((bf16[2,64,2048]{2,1,0:T(8,128)(2,1)S(1)}, bf16[2,64,2048]{2,1,0:T(8,128)(2,1)S(1)}, u32[]{:S(2)}, u32[]{:S(2)}) %collective-permute-start.15) | collective-permute-done | bytes 524320 | tf_op jit(solution)/shard_map/ppermute | solution.py:37
  92.3 0.1 convert_add_fusion
  92.4 0.1 fusion.1.refs_3_
  92.6 1.1 collective-permute-start.21
  93.7 3.9 %collective-permute-done.12.refs_2_ = bf16[64,2048]{1,0:T(8,128)(2,1)S(1)} collective-permute-done((bf16[64,2048]{1,0:T(8,128)(2,1)S(1)}, bf16[64,2048]{1,0:T(8,128)(2,1)S(1)}, u32[]{:S(2)}, u32[]{:S(2)}) %collective-permute-start.12) | collective-permute-done | bytes 262176 | tf_op jit(solution)/shard_map/ppermute | solution.py:37
  97.5 4.0 %collective-permute-start.16 = (bf16[64,2048]{1,0:T(8,128)(2,1)S(1)}, bf16[64,2048]{1,0:T(8,128)(2,1)S(1)}, u32[]{:S(2)}, u32[]{:S(2)}) collective-permute-start(bf16[64,2048]{1,0:T(8,128)(2,1)S(1)} %collective-permute-done.11.refs_1_), channel_id=1, source_target_pairs={{0,8},{8,0},{16,24},{24,16},{1,9},{9,1},{17,25},{25,17},{2,10},{10... | collective-permute-start | bytes 786440 | tf_op jit(solution)/shard_map/ppermute | solution.py:37
  101.6 8.1 %collective-permute-done.21.refs_1_ = bf16[64,2048]{1,0:T(8,128)(2,1)S(1)} collective-permute-done((bf16[64,2048]{1,0:T(8,128)(2,1)S(1)}, bf16[64,2048]{1,0:T(8,128)(2,1)S(1)}, u32[]{:S(2)}, u32[]{:S(2)}) %collective-permute-start.21) | collective-permute-done | bytes 262176 | tf_op jit(solution)/shard_map/ppermute | solution.py:37
  109.7 0.7 collective-permute-done.16.refs_0_
  110.4 1.3 collective-permute-start.23
  111.7 0.1 pad_add_fusion.s_ref
  111.8 3.9 %shard_map.87.refs_4_ = bf16[2048,2048]{1,0:T(8,128)(2,1)S(1)} custom-call(s32[2]{0:T(128)S(1)} %pad_add_fusion.s_ref, bf16[2048,2048]{1,0:T(8,128)(2,1)} %w_ref.1), custom_call_target="tpu_custom_call" | custom-call | tf_op jit(solution)/shard_map/pallas_call | solution.py:148
  115.8 3.5 %shard_map.88 = (bf16[4,32,2048]{2,1,0:T(8,128)(2,1)S(1)}, bf16[4,32,2048]{2,1,0:T(8,128)(2,1)S(1)}) custom-call(s32[2]{0:T(128)S(1)} %pad_add_fusion.s_ref, s32[16,16]{1,0:T(8,128)} %m_ref.3, bf16[64,2048]{1,0:T(8,128)(2,1)S(1)} %collective-permute-done.16.refs_0_, bf16[64,2048]{1,0:T(8,128)(2,1)S(1)} %collective-permute-done.11.refs_1_, ...), custom_call_target="tpu_custom_call" | custom-call | tf_op jit(solution)/shard_map/pallas_call | solution.py:178
  119.3 0.1 collective-permute-start.17
  119.3 3.0 %collective-permute-done.23.refs_2_ = bf16[64,2048]{1,0:T(8,128)(2,1)S(1)} collective-permute-done((bf16[64,2048]{1,0:T(8,128)(2,1)S(1)}, bf16[64,2048]{1,0:T(8,128)(2,1)S(1)}, u32[]{:S(2)}, u32[]{:S(2)}) %collective-permute-start.23) | collective-permute-done | bytes 262176 | tf_op jit(solution)/shard_map/ppermute | solution.py:37
  122.4 3.3 %shard_map.89 = (bf16[4,32,2048]{2,1,0:T(8,128)(2,1)S(1)}, bf16[4,32,2048]{2,1,0:T(8,128)(2,1)S(1)}) custom-call(s32[2]{0:T(128)S(1)} %pad_add_fusion.s_ref, s32[16,16]{1,0:T(8,128)} %m_ref.3, bf16[64,2048]{1,0:T(8,128)(2,1)S(1)} %collective-permute-done.22.refs_0_, bf16[64,2048]{1,0:T(8,128)(2,1)S(1)} %collective-permute-done.21.refs_1_, ...), custom_call_target="tpu_custom_call" | custom-call | flops 3449999872 | tf_op jit(solution)/shard_map/pallas_call | solution.py:178
  125.7 0.1 collective-permute-start.24
  125.8 0.1 add_convert_fusion.1
  125.9 2.3 %collective-permute-start.18 = (bf16[32,2048]{1,0:T(8,128)(2,1)S(1)}, bf16[32,2048]{1,0:T(8,128)(2,1)S(1)}, u32[]{:S(2)}, u32[]{:S(2)}) collective-permute-start(bf16[32,2048]{1,0:T(8,128)(2,1)S(1)} %get-tuple-element.71), channel_id=1, source_target_pairs={{0,6},{1,7},{2,4},{3,5},{4,2},{5,3},{6,0},{7,1},{8,14},{9,15},{10,... | collective-permute-start | bytes 393224 | tf_op jit(solution)/shard_map/ppermute | solution.py:37
  128.2 0.5 collective-permute-start.20
  128.8 0.7 collective-permute-start.19
  129.5 0.1 add_convert_fusion
  129.7 2.3 %collective-permute-start.25 = (bf16[32,2048]{1,0:T(8,128)(2,1)S(1)}, bf16[32,2048]{1,0:T(8,128)(2,1)S(1)}, u32[]{:S(2)}, u32[]{:S(2)}) collective-permute-start(bf16[32,2048]{1,0:T(8,128)(2,1)S(1)} %get-tuple-element.74), channel_id=1, source_target_pairs={{0,6},{1,7},{2,4},{3,5},{4,2},{5,3},{6,0},{7,1},{8,14},{9,15},{10,... | collective-permute-start | bytes 393224 | tf_op jit(solution)/shard_map/ppermute | solution.py:37
  132.0 0.5 collective-permute-start.27
  132.5 0.7 collective-permute-done.18
  133.2 1.3 collective-permute-start.26
  134.5 1.3 collective-permute-done.20
  135.9 0.2 collective-permute-done.19
  136.1 0.1 fusion.9
  136.2 2.7 %collective-permute-done.25 = bf16[32,2048]{1,0:T(8,128)(2,1)S(1)} collective-permute-done((bf16[32,2048]{1,0:T(8,128)(2,1)S(1)}, bf16[32,2048]{1,0:T(8,128)(2,1)S(1)}, u32[]{:S(2)}, u32[]{:S(2)}) %collective-permute-start.25) | collective-permute-done | bytes 131104 | tf_op jit(solution)/shard_map/ppermute | solution.py:37
  138.9 2.3 %collective-permute-done.27 = bf16[32,2048]{1,0:T(8,128)(2,1)S(1)} collective-permute-done((bf16[32,2048]{1,0:T(8,128)(2,1)S(1)}, bf16[32,2048]{1,0:T(8,128)(2,1)S(1)}, u32[]{:S(2)}, u32[]{:S(2)}) %collective-permute-start.27) | collective-permute-done | bytes 131104 | tf_op jit(solution)/shard_map/ppermute | solution.py:37
  141.1 0.1 collective-permute-done.26
  141.3 0.7 pad_maximum_fusion.1
  (22 shorter events, 0.3 us)
Async XLA Ops:
  1.9 14.4 %collective-permute-start = (bf16[128,1024]{1,0:T(8,128)(2,1)S(1)}, bf16[128,1024]{1,0:T(8,128)(2,1)S(1)}, u32[]{:S(2)}, u32[]{:S(2)}) collective-permute-start(bf16[128,1024]{1,0:T(8,128)(2,1)S(1)} %constant_dynamic-slice_fusion.2), channel_id=1, source_target_pairs={{0,8},{8,0},{16,24},{24,16},{1,9},{9,1},{17,25},{25,17},{2,10},{10... | collective-permute-start | bytes 786440 | tf_op jit(solution)/shard_map/ppermute | solution.py:37
  5.0 10.8 %collective-permute-start.1 = (bf16[128,256]{1,0:T(8,128)(2,1)S(1)}, bf16[128,256]{1,0:T(8,128)(2,1)S(1)}, u32[]{:S(2)}, u32[]{:S(2)}) collective-permute-start(bf16[128,256]{1,0:T(8,128)(2,1)S(1)} %get-tuple-element.38), channel_id=1, source_target_pairs={{0,16},{8,24},{16,0},{24,8},{1,17},{9,25},{17,1},{25,9},{2,18},{10... | collective-permute-start | bytes 196616 | tf_op jit(solution)/shard_map/ppermute | solution.py:37
  7.5 8.7 %collective-permute-start.2 = (bf16[128,256]{1,0:T(8,128)(2,1)S(1)}, bf16[128,256]{1,0:T(8,128)(2,1)S(1)}, u32[]{:S(2)}, u32[]{:S(2)}) collective-permute-start(bf16[128,256]{1,0:T(8,128)(2,1)S(1)} %get-tuple-element.39), channel_id=1, source_target_pairs={{0,24},{8,16},{16,8},{24,0},{1,25},{9,17},{17,9},{25,1},{2,26},{10... | collective-permute-start | bytes 196616 | tf_op jit(solution)/shard_map/ppermute | solution.py:37
  16.3 15.7 %collective-permute-start.4 = (bf16[2,64,2048]{2,1,0:T(8,128)(2,1)S(1)}, bf16[2,64,2048]{2,1,0:T(8,128)(2,1)S(1)}, u32[]{:S(2)}, u32[]{:S(2)}) collective-permute-start(bf16[2,64,2048]{2,1,0:T(8,128)(2,1)S(1)} %get-tuple-element.47), channel_id=1, source_target_pairs={{0,8},{8,0},{16,24},{24,16},{1,9},{9,1},{17,25},{25,17},{2,10},{10... | collective-permute-start | bytes 1572872 | tf_op jit(solution)/shard_map/ppermute | solution.py:37
  16.7 11.7 %collective-permute-start.3 = (bf16[1,1,128,1024]{3,2,1,0:T(8,128)(2,1)S(1)}, bf16[1,1,128,1024]{3,2,1,0:T(8,128)(2,1)S(1)}, u32[]{:S(2)}, u32[]{:S(2)}) collective-permute-start(bf16[1,1,128,1024]{3,2,1,0:T(8,128)(2,1)S(1)} %bitcast.53), channel_id=1, source_target_pairs={{0,1},{1,0},{2,3},{3,2},{4,5},{5,4},{6,7},{7,6},{8,9},{9,8},{10,11... | collective-permute-start | bytes 786440 | tf_op jit(solution)/shard_map/ppermute | solution.py:37
  16.8 6.0 %collective-permute-start.7 = (bf16[2,128,256]{2,1,0:T(8,128)(2,1)S(1)}, bf16[2,128,256]{2,1,0:T(8,128)(2,1)S(1)}, u32[]{:S(2)}, u32[]{:S(2)}) collective-permute-start(bf16[2,128,256]{2,1,0:T(8,128)(2,1)S(1)} %get-tuple-element.78), channel_id=1, source_target_pairs={{0,4},{1,5},{2,6},{3,7},{4,0},{5,1},{6,2},{7,3},{8,12},{9,13},{10,... | collective-permute-start | bytes 393224 | tf_op jit(solution)/shard_map/ppermute | solution.py:37
  18.4 6.3 %collective-permute-start.6 = (bf16[2,128,256]{2,1,0:T(8,128)(2,1)S(1)}, bf16[2,128,256]{2,1,0:T(8,128)(2,1)S(1)}, u32[]{:S(2)}, u32[]{:S(2)}) collective-permute-start(bf16[2,128,256]{2,1,0:T(8,128)(2,1)S(1)} %get-tuple-element.78), channel_id=1, source_target_pairs={{0,2},{1,3},{2,0},{3,1},{4,6},{5,7},{6,4},{7,5},{8,10},{9,11},{10,... | collective-permute-start | bytes 393224 | tf_op jit(solution)/shard_map/ppermute | solution.py:37
  19.8 6.9 %collective-permute-start.8 = (bf16[2,128,256]{2,1,0:T(8,128)(2,1)S(1)}, bf16[2,128,256]{2,1,0:T(8,128)(2,1)S(1)}, u32[]{:S(2)}, u32[]{:S(2)}) collective-permute-start(bf16[2,128,256]{2,1,0:T(8,128)(2,1)S(1)} %get-tuple-element.78), channel_id=1, source_target_pairs={{0,6},{1,7},{2,4},{3,5},{4,2},{5,3},{6,0},{7,1},{8,14},{9,15},{10,... | collective-permute-start | bytes 393224 | tf_op jit(solution)/shard_map/ppermute | solution.py:37
  26.8 21.9 %collective-permute-start.13 = (bf16[2,64,2048]{2,1,0:T(8,128)(2,1)S(1)}, bf16[2,64,2048]{2,1,0:T(8,128)(2,1)S(1)}, u32[]{:S(2)}, u32[]{:S(2)}) collective-permute-start(bf16[2,64,2048]{2,1,0:T(8,128)(2,1)S(1)} %get-tuple-element.57), channel_id=1, source_target_pairs={{0,8},{8,0},{16,24},{24,16},{1,9},{9,1},{17,25},{25,17},{2,10},{10... | collective-permute-start | bytes 1572872 | tf_op jit(solution)/shard_map/ppermute | solution.py:37
  28.4 5.8 %collective-permute-start.9 = (bf16[4,2,128,256]{3,2,1,0:T(8,128)(2,1)S(1)}, bf16[4,2,128,256]{3,2,1,0:T(8,128)(2,1)S(1)}, u32[]{:S(2)}, u32[]{:S(2)}) collective-permute-start(bf16[4,2,128,256]{3,2,1,0:T(8,128)(2,1)S(1)} %pad_maximum_fusion.even_ref), channel_id=1, source_target_pairs={{0,1},{1,0},{2,3},{3,2},{4,5},{5,4},{6,7},{7,6},{8,9},{9,8},{10,11... | collective-permute-start | bytes 1572872 | tf_op jit(solution)/shard_map/ppermute | solution.py:37
  28.4 5.8 %copy-start = (s32[8]{0:T(128)S(1)}, s32[8]{0:T(128)}, u32[]{:S(2)}) copy-start(s32[8]{0:T(128)} %constant.66.clone) | copy-start | bytes 100
  32.1 27.1 %collective-permute-start.5 = (bf16[2,64,2048]{2,1,0:T(8,128)(2,1)S(1)}, bf16[2,64,2048]{2,1,0:T(8,128)(2,1)S(1)}, u32[]{:S(2)}, u32[]{:S(2)}) collective-permute-start(bf16[2,64,2048]{2,1,0:T(8,128)(2,1)S(1)} %add_convert_fusion.3), channel_id=1, source_target_pairs={{0,16},{8,24},{16,0},{24,8},{1,17},{9,25},{17,1},{25,9},{2,18},{10... | collective-permute-start | bytes 1572872 | tf_op jit(solution)/shard_map/ppermute | solution.py:37
  40.0 31.2 %collective-permute-start.10 = (bf16[2,64,2048]{2,1,0:T(8,128)(2,1)S(1)}, bf16[2,64,2048]{2,1,0:T(8,128)(2,1)S(1)}, u32[]{:S(2)}, u32[]{:S(2)}) collective-permute-start(bf16[2,64,2048]{2,1,0:T(8,128)(2,1)S(1)} %get-tuple-element.53), channel_id=1, source_target_pairs={{0,8},{8,0},{16,24},{24,16},{1,9},{9,1},{17,25},{25,17},{2,10},{10... | collective-permute-start | bytes 1572872 | tf_op jit(solution)/shard_map/ppermute | solution.py:37
  48.9 32.9 %collective-permute-start.14 = (bf16[2,64,2048]{2,1,0:T(8,128)(2,1)S(1)}, bf16[2,64,2048]{2,1,0:T(8,128)(2,1)S(1)}, u32[]{:S(2)}, u32[]{:S(2)}) collective-permute-start(bf16[2,64,2048]{2,1,0:T(8,128)(2,1)S(1)} %add_convert_fusion.2), channel_id=1, source_target_pairs={{0,16},{8,24},{16,0},{24,8},{1,17},{9,25},{17,1},{25,9},{2,18},{10... | collective-permute-start | bytes 1572872 | tf_op jit(solution)/shard_map/ppermute | solution.py:37
  48.9 43.3 %collective-permute-start.15 = (bf16[2,64,2048]{2,1,0:T(8,128)(2,1)S(1)}, bf16[2,64,2048]{2,1,0:T(8,128)(2,1)S(1)}, u32[]{:S(2)}, u32[]{:S(2)}) collective-permute-start(bf16[2,64,2048]{2,1,0:T(8,128)(2,1)S(1)} %get-tuple-element.59), channel_id=1, source_target_pairs={{0,8},{8,0},{16,24},{24,16},{1,9},{9,1},{17,25},{25,17},{2,10},{10... | collective-permute-start | bytes 1572872 | tf_op jit(solution)/shard_map/ppermute | solution.py:37
  71.5 26.0 %collective-permute-start.12 = (bf16[64,2048]{1,0:T(8,128)(2,1)S(1)}, bf16[64,2048]{1,0:T(8,128)(2,1)S(1)}, u32[]{:S(2)}, u32[]{:S(2)}) collective-permute-start(bf16[64,2048]{1,0:T(8,128)(2,1)S(1)} %fusion.3.refs_3_), channel_id=1, source_target_pairs={{0,8},{8,0},{16,24},{24,16},{1,9},{9,1},{17,25},{25,17},{2,10},{10... | collective-permute-start | bytes 786440 | tf_op jit(solution)/shard_map/ppermute | solution.py:37
  71.6 26.0 %collective-permute-start.11 = (bf16[64,2048]{1,0:T(8,128)(2,1)S(1)}, bf16[64,2048]{1,0:T(8,128)(2,1)S(1)}, u32[]{:S(2)}, u32[]{:S(2)}) collective-permute-start(bf16[64,2048]{1,0:T(8,128)(2,1)S(1)} %fusion.3.refs_3_), channel_id=1, source_target_pairs={{0,16},{8,24},{16,0},{24,8},{1,17},{9,25},{17,1},{25,9},{2,18},{10... | collective-permute-start | bytes 786440 | tf_op jit(solution)/shard_map/ppermute | solution.py:37
  92.6 17.2 %collective-permute-start.21 = (bf16[64,2048]{1,0:T(8,128)(2,1)S(1)}, bf16[64,2048]{1,0:T(8,128)(2,1)S(1)}, u32[]{:S(2)}, u32[]{:S(2)}) collective-permute-start(bf16[64,2048]{1,0:T(8,128)(2,1)S(1)} %fusion.1.refs_3_), channel_id=1, source_target_pairs={{0,16},{8,24},{16,0},{24,8},{1,17},{9,25},{17,1},{25,9},{2,18},{10... | collective-permute-start | bytes 786440 | tf_op jit(solution)/shard_map/ppermute | solution.py:37
  97.5 12.9 %collective-permute-start.16 = (bf16[64,2048]{1,0:T(8,128)(2,1)S(1)}, bf16[64,2048]{1,0:T(8,128)(2,1)S(1)}, u32[]{:S(2)}, u32[]{:S(2)}) collective-permute-start(bf16[64,2048]{1,0:T(8,128)(2,1)S(1)} %collective-permute-done.11.refs_1_), channel_id=1, source_target_pairs={{0,8},{8,0},{16,24},{24,16},{1,9},{9,1},{17,25},{25,17},{2,10},{10... | collective-permute-start | bytes 786440 | tf_op jit(solution)/shard_map/ppermute | solution.py:37
  109.7 9.6 %collective-permute-start.22 = (bf16[64,2048]{1,0:T(8,128)(2,1)S(1)}, bf16[64,2048]{1,0:T(8,128)(2,1)S(1)}, u32[]{:S(2)}, u32[]{:S(2)}) collective-permute-start(bf16[64,2048]{1,0:T(8,128)(2,1)S(1)} %collective-permute-done.21.refs_1_), channel_id=1, source_target_pairs={{0,8},{8,0},{16,24},{24,16},{1,9},{9,1},{17,25},{25,17},{2,10},{10... | collective-permute-start | bytes 786440 | tf_op jit(solution)/shard_map/ppermute | solution.py:37
  110.4 12.0 %collective-permute-start.23 = (bf16[64,2048]{1,0:T(8,128)(2,1)S(1)}, bf16[64,2048]{1,0:T(8,128)(2,1)S(1)}, u32[]{:S(2)}, u32[]{:S(2)}) collective-permute-start(bf16[64,2048]{1,0:T(8,128)(2,1)S(1)} %fusion.1.refs_3_), channel_id=1, source_target_pairs={{0,8},{8,0},{16,24},{24,16},{1,9},{9,1},{17,25},{25,17},{2,10},{10... | collective-permute-start | bytes 786440 | tf_op jit(solution)/shard_map/ppermute | solution.py:37
  119.3 6.5 %collective-permute-start.17 = (bf16[4,32,2048]{2,1,0:T(8,128)(2,1)S(1)}, bf16[4,32,2048]{2,1,0:T(8,128)(2,1)S(1)}, u32[]{:S(2)}, u32[]{:S(2)}) collective-permute-start(bf16[4,32,2048]{2,1,0:T(8,128)(2,1)S(1)} %get-tuple-element.65), channel_id=1, source_target_pairs={{0,1},{1,0},{2,3},{3,2},{4,5},{5,4},{6,7},{7,6},{8,9},{9,8},{10,11... | collective-permute-start | bytes 1572872 | tf_op jit(solution)/shard_map/ppermute | solution.py:37
  125.7 3.8 %collective-permute-start.24 = (bf16[4,32,2048]{2,1,0:T(8,128)(2,1)S(1)}, bf16[4,32,2048]{2,1,0:T(8,128)(2,1)S(1)}, u32[]{:S(2)}, u32[]{:S(2)}) collective-permute-start(bf16[4,32,2048]{2,1,0:T(8,128)(2,1)S(1)} %get-tuple-element.68), channel_id=1, source_target_pairs={{0,1},{1,0},{2,3},{3,2},{4,5},{5,4},{6,7},{7,6},{8,9},{9,8},{10,11... | collective-permute-start | bytes 1572872 | tf_op jit(solution)/shard_map/ppermute | solution.py:37
  125.9 7.3 %collective-permute-start.18 = (bf16[32,2048]{1,0:T(8,128)(2,1)S(1)}, bf16[32,2048]{1,0:T(8,128)(2,1)S(1)}, u32[]{:S(2)}, u32[]{:S(2)}) collective-permute-start(bf16[32,2048]{1,0:T(8,128)(2,1)S(1)} %get-tuple-element.71), channel_id=1, source_target_pairs={{0,6},{1,7},{2,4},{3,5},{4,2},{5,3},{6,0},{7,1},{8,14},{9,15},{10,... | collective-permute-start | bytes 393224 | tf_op jit(solution)/shard_map/ppermute | solution.py:37
  128.2 7.6 %collective-permute-start.20 = (bf16[32,2048]{1,0:T(8,128)(2,1)S(1)}, bf16[32,2048]{1,0:T(8,128)(2,1)S(1)}, u32[]{:S(2)}, u32[]{:S(2)}) collective-permute-start(bf16[32,2048]{1,0:T(8,128)(2,1)S(1)} %get-tuple-element.72), channel_id=1, source_target_pairs={{0,2},{1,3},{2,0},{3,1},{4,6},{5,7},{6,4},{7,5},{8,10},{9,11},{10,... | collective-permute-start | bytes 393224 | tf_op jit(solution)/shard_map/ppermute | solution.py:37
  128.8 7.3 %collective-permute-start.19 = (bf16[32,2048]{1,0:T(8,128)(2,1)S(1)}, bf16[32,2048]{1,0:T(8,128)(2,1)S(1)}, u32[]{:S(2)}, u32[]{:S(2)}) collective-permute-start(bf16[32,2048]{1,0:T(8,128)(2,1)S(1)} %get-tuple-element.73), channel_id=1, source_target_pairs={{0,4},{1,5},{2,6},{3,7},{4,0},{5,1},{6,2},{7,3},{8,12},{9,13},{10,... | collective-permute-start | bytes 393224 | tf_op jit(solution)/shard_map/ppermute | solution.py:37
  129.7 9.2 %collective-permute-start.25 = (bf16[32,2048]{1,0:T(8,128)(2,1)S(1)}, bf16[32,2048]{1,0:T(8,128)(2,1)S(1)}, u32[]{:S(2)}, u32[]{:S(2)}) collective-permute-start(bf16[32,2048]{1,0:T(8,128)(2,1)S(1)} %get-tuple-element.74), channel_id=1, source_target_pairs={{0,6},{1,7},{2,4},{3,5},{4,2},{5,3},{6,0},{7,1},{8,14},{9,15},{10,... | collective-permute-start | bytes 393224 | tf_op jit(solution)/shard_map/ppermute | solution.py:37
  132.0 9.2 %collective-permute-start.27 = (bf16[32,2048]{1,0:T(8,128)(2,1)S(1)}, bf16[32,2048]{1,0:T(8,128)(2,1)S(1)}, u32[]{:S(2)}, u32[]{:S(2)}) collective-permute-start(bf16[32,2048]{1,0:T(8,128)(2,1)S(1)} %get-tuple-element.75), channel_id=1, source_target_pairs={{0,2},{1,3},{2,0},{3,1},{4,6},{5,7},{6,4},{7,5},{8,10},{9,11},{10,... | collective-permute-start | bytes 393224 | tf_op jit(solution)/shard_map/ppermute | solution.py:37
  133.2 8.0 %collective-permute-start.26 = (bf16[32,2048]{1,0:T(8,128)(2,1)S(1)}, bf16[32,2048]{1,0:T(8,128)(2,1)S(1)}, u32[]{:S(2)}, u32[]{:S(2)}) collective-permute-start(bf16[32,2048]{1,0:T(8,128)(2,1)S(1)} %get-tuple-element.76), channel_id=1, source_target_pairs={{0,4},{1,5},{2,6},{3,7},{4,0},{5,1},{6,2},{7,3},{8,12},{9,13},{10,... | collective-permute-start | bytes 393224 | tf_op jit(solution)/shard_map/ppermute | solution.py:37
